TPU v7x, 32 devices: a whole 2x2x4 slice. The times are simulated.
32 devices in a mesh: section: 4 (over y, core), tp: 8 (over z, x).
Axes of the slice: x: 2, y: 2, z: 4, core: 2. Of those that a mesh axis runs over, the one named last changes fastest.
Arguments:
- inputs: bfloat16 [4, 32, 8192], P(None, None, 'tp'), may hold values from -6 to 6
- cotangent: bfloat16 [4, 32, 8192], P(None, None, 'tp'), may hold values from -6 to 6
- weights: bfloat16 [4, 8192, 8192], P('section', 'tp'), may hold values from -0.0625 to 0.0625
- gains: float32 [4, 8192], P('section', 'tp'), may hold values from 0.1 to 1.9
Outputs:
- activations: bfloat16 [4, 4, 32, 8192], P('section', None, None, 'tp')
- gradients: bfloat16 [4, 4, 32, 8192], P('section', None, None, 'tp')
All inputs are finite; a program needn't handle non-finite values.
Results may differ from a plain program's by a relative error of at most 0.019.
Values may be sent and summed in bfloat16 or wider, within the bound.
No kernel may reach another device: no remote copies, remote signals or barrier semaphores. Data moves between devices by JAX's collectives and lax.ppermute only.
A program may use at most 64 MiB of HBM per device.

v0:
```python
import jax
import jax.numpy as jnp
from jax import lax
from jax.sharding import PartitionSpec as P

EPSILON = 1e-05


def shifted(array, axis, by):
    devices = lax.axis_size(axis)
    pairs = [(i, i + by) for i in range(devices) if 0 <= i + by < devices]
    return lax.ppermute(array, axis, pairs)


def store(buffer, value, slot_no, active):
    previous = lax.dynamic_index_in_dim(buffer, slot_no, 0, keepdims=False)
    return lax.dynamic_update_index_in_dim(buffer, jnp.where(active, value, previous), slot_no, 0)


def padded_row(values, width):
    return jnp.pad(values, (0, width - values.shape[0]))


def on_device(inputs, cotangent, weights, gains):
    section_no = lax.axis_index("section")
    section_count = lax.axis_size("section")
    group_count = lax.axis_size("tp")
    micro_count, row_count, local_width = inputs.shape
    full_width = weights.shape[2]
    w_rows = weights[0]
    gain_row = gains[0]
    tick_count = micro_count + section_count - 1

    def forward_branch(wide_in, scaled, active):
        local_squares = jnp.sum(wide_in * wide_in, axis=1).astype(jnp.bfloat16).astype(jnp.float32)
        square_cols = jnp.broadcast_to(local_squares[:, None], (row_count, group_count))
        partial_value = lax.cond(
            active,
            lambda: jnp.dot(scaled, w_rows, preferred_element_type=jnp.float32),
            lambda: jnp.zeros((row_count, full_width), jnp.float32),
        )
        branch, square_mine = (
            lax.psum_scatter(
                partial_value.astype(jnp.bfloat16), "tp", scatter_dimension=1, tiled=True
            ).astype(jnp.float32),
            lax.psum_scatter(
                square_cols.astype(jnp.bfloat16), "tp", scatter_dimension=1, tiled=True
            ).astype(jnp.float32),
        )
        return (branch, square_mine[:, 0])

    def backward_terms(upstream, mix_slot, active):
        partial_dot = jnp.sum(upstream.astype(jnp.float32) * mix_slot, axis=1).astype(jnp.bfloat16)
        extended = jnp.concatenate(
            [upstream, padded_row(partial_dot, local_width)[None, :]], axis=0
        )
        shard_in = lax.all_gather(extended, "tp", axis=1, tiled=True)
        running = jnp.zeros((row_count, local_width), jnp.float32)
        shard_count = shard_in.shape[1] // local_width
        tail_row = shard_in[row_count].astype(jnp.float32).reshape(shard_count, local_width)
        dot_total = jnp.sum(tail_row[:, :row_count], axis=0)
        running = lax.cond(
            active,
            lambda: lax.dot_general(
                shard_in[:row_count],
                w_rows,
                (((1,), (1,)), ((), ())),
                preferred_element_type=jnp.float32,
            ),
            lambda: running,
        )
        return (running, dot_total)

    def forward_tick(tick_no, state_in):
        incoming, outputs, saved_in, saved_mix, saved_rms = state_in
        micro_no = tick_no - section_no
        active = (micro_no >= 0) & (micro_no < micro_count)
        slot_no = jnp.clip(micro_no, 0, micro_count - 1)
        fresh_in = lax.dynamic_index_in_dim(inputs, slot_no, 0, keepdims=False)
        block_in = jnp.where(section_no == 0, fresh_in, incoming)
        wide_in = block_in.astype(jnp.float32)
        scaled = (wide_in * gain_row).astype(jnp.bfloat16)
        branch, squares = forward_branch(wide_in, scaled, active)
        inv_rms = lax.rsqrt(squares / full_width + EPSILON)
        output = (wide_in + inv_rms[:, None] * branch).astype(jnp.bfloat16)
        outputs = store(outputs, output, slot_no, active)
        saved_in = store(saved_in, block_in, slot_no, active)
        saved_mix = store(saved_mix, branch, slot_no, active)
        saved_rms = store(saved_rms, inv_rms, slot_no, active)
        incoming = shifted(output, "section", 1)
        return (incoming, outputs, saved_in, saved_mix, saved_rms)

    start_state = (
        jnp.zeros((row_count, local_width), jnp.bfloat16),
        jnp.zeros_like(inputs),
        jnp.zeros_like(inputs),
        jnp.zeros((micro_count, row_count, local_width), jnp.float32),
        jnp.zeros((micro_count, row_count), jnp.float32),
    )
    _, outputs, saved_in, saved_mix, saved_rms = lax.fori_loop(
        0, tick_count, forward_tick, start_state
    )

    def backward_tick(tick_no, state_in):
        incoming, grads = state_in
        micro_no = tick_no - (section_count - 1 - section_no)
        active = (micro_no >= 0) & (micro_no < micro_count)
        slot_no = jnp.clip(micro_no, 0, micro_count - 1)
        fresh_up = lax.dynamic_index_in_dim(cotangent, slot_no, 0, keepdims=False)
        upstream = jnp.where(section_no == section_count - 1, fresh_up, incoming)
        wide_up = upstream.astype(jnp.float32)
        mix_slot = lax.dynamic_index_in_dim(saved_mix, slot_no, 0, keepdims=False)
        back_rows, row_dot = backward_terms(upstream, mix_slot, active)
        inv_rms = lax.dynamic_index_in_dim(saved_rms, slot_no, 0, keepdims=False)
        block_in = lax.dynamic_index_in_dim(saved_in, slot_no, 0, keepdims=False).astype(
            jnp.float32
        )
        grad_in = (
            wide_up
            + inv_rms[:, None] * gain_row * back_rows
            - (inv_rms**3 / full_width * row_dot)[:, None] * block_in
        ).astype(jnp.bfloat16)
        grads = store(grads, grad_in, slot_no, active)
        incoming = shifted(grad_in, "section", -1)
        return (incoming, grads)

    _, grads = lax.fori_loop(
        0,
        tick_count,
        backward_tick,
        (jnp.zeros((row_count, local_width), jnp.bfloat16), jnp.zeros_like(inputs)),
    )
    return (outputs[None], grads[None])


def solution(mesh):
    placed = (
        P(None, None, "tp"),
        P(None, None, "tp"),
        P("section", "tp", None),
        P("section", "tp"),
    )
    return jax.shard_map(
        on_device,
        mesh=mesh,
        in_specs=placed,
        out_specs=(P("section", None, None, "tp"), P("section", None, None, "tp")),
        check_vma=False,
    )
```

profile of v0, /device:TPU:0, one launch (start us, length us, event | category | flops | bytes accessed | tf_op | source)
XLA Modules:
  0.0 887.7 jit_solution(4764514559532704513)
XLA Ops:
  7.3 550.1 %while.39 = (s32[]{:T(128)}, bf16[32,1024]{1,0:T(8,128)(2,1)S(1)}, bf16[4,32,1024]{2,1,0:T(8,128)(2,1)S(1)}, bf16[4,32,1024]{2,1,0:T(8,128)(2,1)S(1)}, f32[4,32,...) while((s32[]{:T(128)}, bf16[32,1024]{1,0:T(8,128)(2,1)S(1)}, ...), condition=%wide.region_6.7_spmd, body=%wide.region_0.6_spmd.sunk | while | flops 537362944 | bytes 23142216 | solution.py:100
  19.3 23.2 %all-reduce.3 = bf16[32,8]{0,1:T(8,128)(2,1)S(1)} all-reduce(bf16[32,8]{0,1:T(8,128)(2,1)S(1)} %broadcast_in_dim.94), channel_id=2, replica_groups=mesh['section'=4,'tp'=8] {'tp'}, use_global_device_ids=true, to_apply=%region_2.2.clone | all-reduce | flops 256 | bytes 1024 | tf_op jit(solution)/shard_map/while
  43.9 39.1 %reduce-scatter.2.cloned.1.call-done = bf16[32,1024]{1,0:T(8,128)(2,1)} async-done(((bf16[32,8192]{1,0:T(8,128)(2,1)}), bf16[32,1024]{1,0:T(8,128)(2,1)}) %reduce-scatter.2.cloned.1.call-update) | async-done | bytes 65552 | tf_op jit(solution)/shard_map/while/body/eval_jaxpr/reduce_scatter | solution.py:43
  98.2 19.4 %all-reduce.3 = bf16[32,8]{0,1:T(8,128)(2,1)S(1)} all-reduce(bf16[32,8]{0,1:T(8,128)(2,1)S(1)} %broadcast_in_dim.94), channel_id=2, replica_groups=mesh['section'=4,'tp'=8] {'tp'}, use_global_device_ids=true, to_apply=%region_2.2.clone | all-reduce | flops 256 | bytes 1024 | tf_op jit(solution)/shard_map/while
  119.0 41.2 %reduce-scatter.2.cloned.1.call-done = bf16[32,1024]{1,0:T(8,128)(2,1)} async-done(((bf16[32,8192]{1,0:T(8,128)(2,1)}), bf16[32,1024]{1,0:T(8,128)(2,1)}) %reduce-scatter.2.cloned.1.call-update) | async-done | bytes 65552 | tf_op jit(solution)/shard_map/while/body/eval_jaxpr/reduce_scatter | solution.py:43
  175.4 19.7 %all-reduce.3 = bf16[32,8]{0,1:T(8,128)(2,1)S(1)} all-reduce(bf16[32,8]{0,1:T(8,128)(2,1)S(1)} %broadcast_in_dim.94), channel_id=2, replica_groups=mesh['section'=4,'tp'=8] {'tp'}, use_global_device_ids=true, to_apply=%region_2.2.clone | all-reduce | flops 256 | bytes 1024 | tf_op jit(solution)/shard_map/while
  196.4 43.2 %reduce-scatter.2.cloned.1.call-done = bf16[32,1024]{1,0:T(8,128)(2,1)} async-done(((bf16[32,8192]{1,0:T(8,128)(2,1)}), bf16[32,1024]{1,0:T(8,128)(2,1)}) %reduce-scatter.2.cloned.1.call-update) | async-done | bytes 65552 | tf_op jit(solution)/shard_map/while/body/eval_jaxpr/reduce_scatter | solution.py:43
  254.8 19.6 %all-reduce.3 = bf16[32,8]{0,1:T(8,128)(2,1)S(1)} all-reduce(bf16[32,8]{0,1:T(8,128)(2,1)S(1)} %broadcast_in_dim.94), channel_id=2, replica_groups=mesh['section'=4,'tp'=8] {'tp'}, use_global_device_ids=true, to_apply=%region_2.2.clone | all-reduce | flops 256 | bytes 1024 | tf_op jit(solution)/shard_map/while
  275.8 43.2 %reduce-scatter.2.cloned.1.call-done = bf16[32,1024]{1,0:T(8,128)(2,1)} async-done(((bf16[32,8192]{1,0:T(8,128)(2,1)}), bf16[32,1024]{1,0:T(8,128)(2,1)}) %reduce-scatter.2.cloned.1.call-update) | async-done | bytes 65552 | tf_op jit(solution)/shard_map/while/body/eval_jaxpr/reduce_scatter | solution.py:43
  325.4 19.4 %all-reduce.3 = bf16[32,8]{0,1:T(8,128)(2,1)S(1)} all-reduce(bf16[32,8]{0,1:T(8,128)(2,1)S(1)} %broadcast_in_dim.94), channel_id=2, replica_groups=mesh['section'=4,'tp'=8] {'tp'}, use_global_device_ids=true, to_apply=%region_2.2.clone | all-reduce | flops 256 | bytes 1024 | tf_op jit(solution)/shard_map/while
  346.3 52.0 %reduce-scatter.2.cloned.1.call-done = bf16[32,1024]{1,0:T(8,128)(2,1)} async-done(((bf16[32,8192]{1,0:T(8,128)(2,1)}), bf16[32,1024]{1,0:T(8,128)(2,1)}) %reduce-scatter.2.cloned.1.call-update) | async-done | bytes 65552 | tf_op jit(solution)/shard_map/while/body/eval_jaxpr/reduce_scatter | solution.py:43
  404.7 19.5 %all-reduce.3 = bf16[32,8]{0,1:T(8,128)(2,1)S(1)} all-reduce(bf16[32,8]{0,1:T(8,128)(2,1)S(1)} %broadcast_in_dim.94), channel_id=2, replica_groups=mesh['section'=4,'tp'=8] {'tp'}, use_global_device_ids=true, to_apply=%region_2.2.clone | all-reduce | flops 256 | bytes 1024 | tf_op jit(solution)/shard_map/while
  425.6 52.0 %reduce-scatter.2.cloned.1.call-done = bf16[32,1024]{1,0:T(8,128)(2,1)} async-done(((bf16[32,8192]{1,0:T(8,128)(2,1)}), bf16[32,1024]{1,0:T(8,128)(2,1)}) %reduce-scatter.2.cloned.1.call-update) | async-done | bytes 65552 | tf_op jit(solution)/shard_map/while/body/eval_jaxpr/reduce_scatter | solution.py:43
  484.0 19.5 %all-reduce.3 = bf16[32,8]{0,1:T(8,128)(2,1)S(1)} all-reduce(bf16[32,8]{0,1:T(8,128)(2,1)S(1)} %broadcast_in_dim.94), channel_id=2, replica_groups=mesh['section'=4,'tp'=8] {'tp'}, use_global_device_ids=true, to_apply=%region_2.2.clone | all-reduce | flops 256 | bytes 1024 | tf_op jit(solution)/shard_map/while
  504.9 49.3 %reduce-scatter.2.cloned.1.call-done = bf16[32,1024]{1,0:T(8,128)(2,1)} async-done(((bf16[32,8192]{1,0:T(8,128)(2,1)}), bf16[32,1024]{1,0:T(8,128)(2,1)}) %reduce-scatter.2.cloned.1.call-update) | async-done | bytes 65552 | tf_op jit(solution)/shard_map/while/body/eval_jaxpr/reduce_scatter | solution.py:43
  558.1 322.1 %while.40 = (s32[]{:T(128)}, bf16[32,1024]{1,0:T(8,128)(2,1)S(1)}, bf16[4,32,1024]{2,1,0:T(8,128)(2,1)S(1)}, pred[]{:T(512)}, s32[]{:T(128)}, /*index=5*/bf16[4,...) while((s32[]{:T(128)}, bf16[32,1024]{1,0:T(8,128)(2,1)S(1)}, ...), condition=%wide.region_12.13_spmd, body=%wide.region_7.12_spmd.sunk | while | flops 537432640 | bytes 19450432 | solution.py:127
  559.1 31.7 %all_gather.11 = bf16[33,8192]{1,0:T(8,128)(2,1)S(1)} all-gather(bf16[33,1024]{1,0:T(8,128)(2,1)S(1)} %pad_maximum_fusion.2), channel_id=1, replica_groups=mesh['section'=4,'tp'=8] {'tp'}, dimensions={1}, use_global_device_ids=true | all-gather | bytes 608256 | tf_op jit(solution)/shard_map/while/body/eval_jaxpr/all_gather | solution.py:57
  595.4 31.9 %all_gather.11 = bf16[33,8192]{1,0:T(8,128)(2,1)S(1)} all-gather(bf16[33,1024]{1,0:T(8,128)(2,1)S(1)} %pad_maximum_fusion.2), channel_id=1, replica_groups=mesh['section'=4,'tp'=8] {'tp'}, dimensions={1}, use_global_device_ids=true | all-gather | bytes 608256 | tf_op jit(solution)/shard_map/while/body/eval_jaxpr/all_gather | solution.py:57
  631.8 31.8 %all_gather.11 = bf16[33,8192]{1,0:T(8,128)(2,1)S(1)} all-gather(bf16[33,1024]{1,0:T(8,128)(2,1)S(1)} %pad_maximum_fusion.2), channel_id=1, replica_groups=mesh['section'=4,'tp'=8] {'tp'}, dimensions={1}, use_global_device_ids=true | all-gather | bytes 608256 | tf_op jit(solution)/shard_map/while/body/eval_jaxpr/all_gather | solution.py:57
  665.2 24.3 %collective-permute-done.1 = bf16[32,1024]{1,0:T(8,128)(2,1)S(1)} collective-permute-done((bf16[32,1024]{1,0:T(8,128)(2,1)S(1)}, bf16[32,1024]{1,0:T(8,128)(2,1)S(1)}, u32[]{:S(2)}, u32[]{:S(2)}) %collective-permute-start.1) | collective-permute-done | bytes 65568 | tf_op jit(solution)/shard_map/while/body/eval_jaxpr/ppermute | solution.py:12
  690.5 31.7 %all_gather.11 = bf16[33,8192]{1,0:T(8,128)(2,1)S(1)} all-gather(bf16[33,1024]{1,0:T(8,128)(2,1)S(1)} %pad_maximum_fusion.2), channel_id=1, replica_groups=mesh['section'=4,'tp'=8] {'tp'}, dimensions={1}, use_global_device_ids=true | all-gather | bytes 608256 | tf_op jit(solution)/shard_map/while/body/eval_jaxpr/all_gather | solution.py:57
  738.6 31.9 %all_gather.11 = bf16[33,8192]{1,0:T(8,128)(2,1)S(1)} all-gather(bf16[33,1024]{1,0:T(8,128)(2,1)S(1)} %pad_maximum_fusion.2), channel_id=1, replica_groups=mesh['section'=4,'tp'=8] {'tp'}, dimensions={1}, use_global_device_ids=true | all-gather | bytes 608256 | tf_op jit(solution)/shard_map/while/body/eval_jaxpr/all_gather | solution.py:57
  785.8 31.7 %all_gather.11 = bf16[33,8192]{1,0:T(8,128)(2,1)S(1)} all-gather(bf16[33,1024]{1,0:T(8,128)(2,1)S(1)} %pad_maximum_fusion.2), channel_id=1, replica_groups=mesh['section'=4,'tp'=8] {'tp'}, dimensions={1}, use_global_device_ids=true | all-gather | bytes 608256 | tf_op jit(solution)/shard_map/while/body/eval_jaxpr/all_gather | solution.py:57
  834.1 31.8 %all_gather.11 = bf16[33,8192]{1,0:T(8,128)(2,1)S(1)} all-gather(bf16[33,1024]{1,0:T(8,128)(2,1)S(1)} %pad_maximum_fusion.2), channel_id=1, replica_groups=mesh['section'=4,'tp'=8] {'tp'}, dimensions={1}, use_global_device_ids=true | all-gather | bytes 608256 | tf_op jit(solution)/shard_map/while/body/eval_jaxpr/all_gather | solution.py:57
  (276 shorter events, 243.5 us)
Async XLA Ops:
  7.3 75.7 %reduce-scatter.2.cloned.1.call-start = ((), (), s32[]{:S(2)}) async-start(), calls=%async_computation.1 | async-start | bytes 589824 | tf_op jit(solution)/shard_map/while/body/eval_jaxpr/reduce_scatter | solution.py:43
  83.9 2.2 collective-permute-start
  86.1 74.1 %reduce-scatter.2.cloned.1.call-start = ((), (), s32[]{:S(2)}) async-start(), calls=%async_computation.1 | async-start | bytes 589824 | tf_op jit(solution)/shard_map/while/body/eval_jaxpr/reduce_scatter | solution.py:43
  161.2 2.2 collective-permute-start
  163.4 76.3 %reduce-scatter.2.cloned.1.call-start = ((), (), s32[]{:S(2)}) async-start(), calls=%async_computation.1 | async-start | bytes 589824 | tf_op jit(solution)/shard_map/while/body/eval_jaxpr/reduce_scatter | solution.py:43
  240.6 2.2 collective-permute-start
  242.8 76.2 %reduce-scatter.2.cloned.1.call-start = ((), (), s32[]{:S(2)}) async-start(), calls=%async_computation.1 | async-start | bytes 589824 | tf_op jit(solution)/shard_map/while/body/eval_jaxpr/reduce_scatter | solution.py:43
  319.9 2.2 collective-permute-start
  322.1 76.1 %reduce-scatter.2.cloned.1.call-start = ((), (), s32[]{:S(2)}) async-start(), calls=%async_computation.1 | async-start | bytes 589824 | tf_op jit(solution)/shard_map/while/body/eval_jaxpr/reduce_scatter | solution.py:43
  399.2 2.2 collective-permute-start
  401.4 76.2 %reduce-scatter.2.cloned.1.call-start = ((), (), s32[]{:S(2)}) async-start(), calls=%async_computation.1 | async-start | bytes 589824 | tf_op jit(solution)/shard_map/while/body/eval_jaxpr/reduce_scatter | solution.py:43
  478.5 2.2 collective-permute-start
  480.7 73.6 %reduce-scatter.2.cloned.1.call-start = ((), (), s32[]{:S(2)}) async-start(), calls=%async_computation.1 | async-start | bytes 589824 | tf_op jit(solution)/shard_map/while/body/eval_jaxpr/reduce_scatter | solution.py:43
  555.2 2.2 collective-permute-start
  591.2 3.1 collective-permute-start.1
  627.6 3.1 collective-permute-start.1
  663.9 25.6 %collective-permute-start.1 = (bf16[32,1024]{1,0:T(8,128)(2,1)S(1)}, bf16[32,1024]{1,0:T(8,128)(2,1)S(1)}, u32[]{:S(2)}, u32[]{:S(2)}) collective-permute-start(bf16[32,1024]{1,0:T(8,128)(2,1)S(1)} %get-tuple-element.715), channel_id=1, source_target_pairs={{8,0},{16,8},{24,16},{9,1},{17,9},{25,17},{10,2},{18,10},{26,18},{... | collective-permute-start | bytes 196616 | tf_op jit(solution)/shard_map/while/body/eval_jaxpr/ppermute | solution.py:12
  689.5 43.8 %copy-start.3 = (f32[1,1024]{1,0:T(1,128)S(1)}, f32[1,1024]{1,0:T(1,128)}, u32[]{:S(2)}) copy-start(f32[1,1024]{1,0:T(1,128)} %get-tuple-element.807) | copy-start | bytes 12292 | tf_op jit(solution)/shard_map/while
  733.4 4.2 collective-permute-start.1
  737.6 43.9 %copy-start.3 = (f32[1,1024]{1,0:T(1,128)S(1)}, f32[1,1024]{1,0:T(1,128)}, u32[]{:S(2)}) copy-start(f32[1,1024]{1,0:T(1,128)} %get-tuple-element.807) | copy-start | bytes 12292 | tf_op jit(solution)/shard_map/while
  781.6 3.1 collective-permute-start.1
  828.6 4.5 collective-permute-start.1
  833.1 43.8 %copy-start.3 = (f32[1,1024]{1,0:T(1,128)S(1)}, f32[1,1024]{1,0:T(1,128)}, u32[]{:S(2)}) copy-start(f32[1,1024]{1,0:T(1,128)} %get-tuple-element.807) | copy-start | bytes 12292 | tf_op jit(solution)/shard_map/while
  877.0 3.1 collective-permute-start.1
  (20 other events, 203.6 us)
Sparse Core Ops, SparseCore 0:
  18.8 64.1 reduce-scatter.1
  97.6 62.5 reduce-scatter.1
  174.9 64.7 reduce-scatter.1
  254.3 64.6 reduce-scatter.1
  326.0 72.2 reduce-scatter.1
  405.3 72.2 reduce-scatter.1
  484.9 69.3 reduce-scatter.1
where the time goes:
time: 890 us; the launch traced here: 888 us
  blocking collectives  363 us (41%)
  waiting for transfers between devices  358 us (40%)
  matrix products  78.2 us (9%)
  other arithmetic  41.5 us (5%)
  starting transfers between devices  18.4 us (2%)
  between operations  14.1 us (2%)
  local copies, waits for them, and re-layouts  13.1 us (1%)
    reduce_scatter x7, waiting for transfers between devices, forward_branch(): lax.psum_scatter(partial_value.astype(jnp.bfloat16), 'tp', scatter_dimens...  320 us
    all_gather x7, blocking collectives, backward_terms(): shard_in = lax.all_gather(extended, 'tp', axis=1, tiled=True)  222 us
    while x7, blocking collectives  140 us
    dot_general x4, matrix products, backward_terms(): lax.dot_general(shard_in[:row_count], w_rows, (((1,), (1,)), ((), ())), p...  43.2 us
    ppermute x14, waiting for transfers between devices, shifted(): return lax.ppermute(array, axis, pairs)  37.8 us
    dot_general x4, matrix products, forward_branch(): jnp.dot(scaled, w_rows, preferred_element_type=jnp.float32)  35 us
    dynamic_update_slice x28, other arithmetic, store(): lax.dynamic_update_index_in_dim(buffer, jnp.where(active, value, previous...  19.6 us
    ppermute x14, starting transfers between devices, shifted(): return lax.ppermute(array, axis, pairs)  18.1 us
  transfers between devices with their start and end apart: 21, of which 14 were waited for; matrix products, arithmetic and copies ran while one was open for 2% of the time, Pallas kernels for 0%

commit v1 on v0

v1 whole, which is shorter than its diff:
```python
import jax
import jax.numpy as jnp
from jax import lax
from jax.experimental import pallas as pl
from jax.experimental.pallas import tpu as pltpu
from jax.sharding import PartitionSpec as P

EPSILON = 1e-05
MIB = 1 << 20


def forward_kernel(block_count, place_ref, a_ref, gain_ref, w_ref, *rest):
    out_refs, scaled_ref = rest[:-1], rest[-1]
    step = pl.program_id(0)

    @pl.when(step == 0)
    def _():
        wide = a_ref[...].astype(jnp.float32)
        scaled_ref[...] = (wide * gain_ref[...]).astype(jnp.bfloat16)

    partial = jnp.dot(scaled_ref[...], w_ref[...], preferred_element_type=jnp.float32)
    for block in range(block_count):

        @pl.when(step == block)
        def _(block=block):
            out_refs[block][...] = partial.astype(jnp.bfloat16)


def forward_blocks(a, gain_row, w_rows, blocks):
    rows, width = a.shape
    count = len(blocks)
    whole = pl.BlockSpec((rows, width), lambda k, place_ref: (0, 0))
    return pl.pallas_call(
        lambda *refs: forward_kernel(count, *refs),
        out_shape=[jax.ShapeDtypeStruct((rows, width), jnp.bfloat16)] * count,
        grid_spec=pltpu.PrefetchScalarGridSpec(
            num_scalar_prefetch=1,
            grid=(count,),
            in_specs=[
                whole,
                pl.BlockSpec((1, width), lambda k, place_ref: (0, 0)),
                pl.BlockSpec((width, width), lambda k, place_ref: (0, place_ref[k])),
            ],
            out_specs=[whole] * count,
            scratch_shapes=[pltpu.VMEM((rows, width), jnp.bfloat16)],
        ),
        compiler_params=pltpu.CompilerParams(vmem_limit_bytes=24 * MIB),
        cost_estimate=pl.CostEstimate(
            flops=2 * rows * width * width * count,
            bytes_accessed=2 * width * width * count,
            transcendentals=0,
        ),
    )(jnp.stack(blocks), a, gain_row, w_rows)


def backward_kernel(block_count, place_ref, w_ref, *rest):
    g_refs, out_ref, held_ref = rest[:block_count], rest[block_count], rest[block_count + 1]
    step = pl.program_id(0)
    for block in range(block_count):

        @pl.when(step == block)
        def _(block=block):
            held_ref[...] = g_refs[block][...]

    product = lax.dot_general(
        held_ref[...], w_ref[...], (((1,), (1,)), ((), ())), preferred_element_type=jnp.float32
    )

    @pl.when(step == 0)
    def _():
        out_ref[...] = product

    @pl.when(step > 0)
    def _():
        out_ref[...] += product


def backward_blocks(shards, w_rows, blocks):
    rows, width = shards[0].shape
    count = len(blocks)
    whole = pl.BlockSpec((rows, width), lambda k, place_ref: (0, 0))
    return pl.pallas_call(
        lambda *refs: backward_kernel(count, *refs),
        out_shape=jax.ShapeDtypeStruct((rows, width), jnp.float32),
        grid_spec=pltpu.PrefetchScalarGridSpec(
            num_scalar_prefetch=1,
            grid=(count,),
            in_specs=[pl.BlockSpec((width, width), lambda k, place_ref: (0, place_ref[k]))]
            + [whole] * count,
            out_specs=whole,
            scratch_shapes=[pltpu.VMEM((rows, width), jnp.bfloat16)],
        ),
        compiler_params=pltpu.CompilerParams(vmem_limit_bytes=24 * MIB),
        cost_estimate=pl.CostEstimate(
            flops=2 * rows * width * width * count,
            bytes_accessed=2 * width * width * count,
            transcendentals=0,
        ),
    )(jnp.stack(blocks), w_rows, *shards)


def on_device(inputs, cotangent, weights, gains):
    section_no = lax.axis_index("section")
    section_count = lax.axis_size("section")
    tp_no = lax.axis_index("tp")
    tp_count = lax.axis_size("tp")
    inner = tp_count // 4 if tp_count % 4 == 0 else tp_count
    outer = tp_count // inner
    micro_count, row_count, width = inputs.shape
    rows = micro_count * row_count
    full_width = weights.shape[2]
    w_rows = weights[0]
    gain_row = gains
    last = section_count - 1

    def send(value, sections, step=0, hop=0):
        pairs = [
            (s * tp_count + t, (s + hop) * tp_count + (t ^ step))
            for s in sections
            for t in range(tp_count)
        ]
        return lax.ppermute(value, ("section", "tp"), pairs)

    def chosen(section, new, old):
        return jnp.where(section_no == section, new, old)

    def row_totals(partial, sections):
        total = partial
        step = 1
        while step < tp_count:
            total = total + send(total, sections, step)
            step *= 2
        return total

    def row_sum(value):
        return jnp.sum(value, axis=1).astype(jnp.bfloat16).astype(jnp.float32)

    def place(dz, dx):
        return tp_no ^ (dz * inner + dx)

    def gathered(shard, sections):
        found = []
        for dz in [0] + list(range(1, outer)):
            column = shard if dz == 0 else send(shard, sections, dz * inner)
            found.append((column, place(dz, 0)))
            for dx in range(1, inner):
                found.append((send(column, sections, dx), place(dz, dx)))
        return found

    def scattered_sum(a, sections):
        order = list(range(outer - 1, -1, -1))
        mine = {}
        theirs = {}
        for dx in range(inner - 1, -1, -1):
            parts = forward_blocks(a, gain_row, w_rows, [place(dz, dx) for dz in order])
            for dz, part in zip(order, parts):
                if dx == 0:
                    mine[dz] = part
                else:
                    theirs[dz, dx] = send(part, sections, dx)
        total = None
        for dz in order:
            column = mine[dz].astype(jnp.float32)
            for dx in range(1, inner):
                column = column + theirs[dz, dx].astype(jnp.float32)
            if dz:
                column = send(column.astype(jnp.bfloat16), sections, dz * inner).astype(jnp.float32)
            total = column if total is None else total + column
        return total

    def forward(a, sections):
        wide = a.astype(jnp.float32)
        squares = row_totals(row_sum(wide * wide), sections)
        inv_rms = lax.rsqrt(squares / full_width + EPSILON)
        branch = scattered_sum(a, sections)
        return branch, inv_rms, (wide + inv_rms[:, None] * branch).astype(jnp.bfloat16)

    def back_rows(g, sections):
        found = gathered(g, sections)
        return backward_blocks([f[0] for f in found], w_rows, [f[1] for f in found])

    cot = cotangent.reshape(rows, width)
    last_back = gain_row * back_rows(cot, [last])

    block_in = inputs.reshape(rows, width)
    outputs = jnp.zeros_like(block_in)
    inv_rms = jnp.zeros((rows,), jnp.float32)
    branch = jnp.zeros((rows, width), jnp.float32)
    for section in range(last):
        new_branch, new_rms, output = forward(block_in, [section])
        incoming = send(output, [section], hop=1)
        outputs = chosen(section, output, outputs)
        inv_rms = chosen(section, new_rms, inv_rms)
        branch = chosen(section, new_branch, branch)
        block_in = chosen(section + 1, incoming, block_in)

    wide = block_in.astype(jnp.float32)
    sums = row_totals(jnp.stack([row_sum(wide * wide), row_sum(wide * last_back)]), [last])
    last_rms = lax.rsqrt(sums[0] / full_width + EPSILON)
    grad = (
        cot.astype(jnp.float32)
        + last_rms[:, None] * last_back
        - (last_rms**3 / full_width * sums[1])[:, None] * wide
    ).astype(jnp.bfloat16)
    grads = grad
    last_branch = scattered_sum(block_in, [last])
    outputs = chosen(
        last, (wide + last_rms[:, None] * last_branch).astype(jnp.bfloat16), outputs
    )
    for section in range(last - 1, -1, -1):
        upstream = send(grad, [section + 1], hop=-1)
        wide_up = upstream.astype(jnp.float32)
        row_dot = row_totals(row_sum(wide_up * branch), [section])
        back = back_rows(upstream, [section])
        grad = (
            wide_up
            + inv_rms[:, None] * gain_row * back
            - (inv_rms**3 / full_width * row_dot)[:, None] * wide
        ).astype(jnp.bfloat16)
        grads = chosen(section, grad, grads)
    shape = (1, micro_count, row_count, width)
    return outputs.reshape(shape), grads.reshape(shape)


def solution(mesh):
    placed = (
        P(None, None, "tp"),
        P(None, None, "tp"),
        P("section", "tp", None),
        P("section", "tp"),
    )
    return jax.shard_map(
        on_device,
        mesh=mesh,
        in_specs=placed,
        out_specs=(P("section", None, None, "tp"), P("section", None, None, "tp")),
        check_vma=False,
    )
```

time: 890 us -> 386 us (0.43)
  blocking collectives: 363 us -> 0 us
  waiting for transfers between devices: 358 us -> 56 us
  starting transfers between devices: 18.4 us -> 218 us
  matrix products: 78.2 us -> 0 us
  Pallas kernels: 0 us -> 61.9 us
  other arithmetic: 41.5 us -> 9.38 us
  local copies, waits for them, and re-layouts: 13.1 us -> 36.5 us
  between operations: 14.1 us -> 2.5 us
    reduce_scatter x7 -> x0, waiting for transfers between devices: 320 us -> none  [forward_branch(): lax.psum_scatter(partial_value.astype(jnp.bfloat16), 'tp', scatter_dimens...]
    all_gather x7 -> x0, blocking collectives: 222 us -> none  [backward_terms(): shard_in = lax.all_gather(extended, 'tp', axis=1, tiled=True)]
    ppermute x14 -> x83, starting transfers between devices: 18.1 us -> 218 us  [send(): return lax.ppermute(value, ('section', 'tp'), pairs)]
    while x7 -> x0, blocking collectives: 140 us -> none
    dot_general x8 -> x0, matrix products: 78.2 us -> none  [the longest x4 43.2 us: backward_terms(): lax.dot_general(shard_in[:row_count], w_rows, (((1,), (1,)), ((), ())), p...]
    pallas_call x0 -> x12, Pallas kernels: none -> 61.9 us  [the longest x4 36.6 us: backward_blocks(): pl.pallas_call(lambda *refs: backward_kernel(count, *refs), out_shape=jax...]
    unnamed x4 -> x52, local copies, waits for them, and re-layouts: 1.35 us -> 36.3 us
    dynamic_update_slice x28 -> x0, other arithmetic: 19.6 us -> none  [store(): lax.dynamic_update_index_in_dim(buffer, jnp.where(active, value, previous...]
  transfers between devices with their start and end apart: 21 -> 83, of which waited for: 14 -> 8; matrix products, arithmetic and copies ran while one was open for 2% -> 2% of each run, Pallas kernels for 0% -> 10%
where the time goes in v1:
time: 386 us; the launch traced here: 385 us
  starting transfers between devices  218 us (56%)
  Pallas kernels  61.9 us (16%)
  waiting for transfers between devices  56 us (15%)
  local copies, waits for them, and re-layouts  36.5 us (9%)
  other arithmetic  9.38 us (2%)
    ppermute x83, starting transfers between devices, send(): return lax.ppermute(value, ('section', 'tp'), pairs)  218 us
    ppermute x83, waiting for transfers between devices, send(): return lax.ppermute(value, ('section', 'tp'), pairs)  56 us
    pallas_call x4, Pallas kernels, backward_blocks(): pl.pallas_call(lambda *refs: backward_kernel(count, *refs), out_shape=jax...  36.6 us
    unnamed x52, local copies, waits for them, and re-layouts  36.3 us
    pallas_call x8, Pallas kernels, forward_blocks(): pl.pallas_call(lambda *refs: forward_kernel(count, *refs), out_shape=[jax...  25.3 us
  transfers between devices with their start and end apart: 83, of which 8 were waited for; matrix products, arithmetic and copies ran while one was open for 2% of the time, Pallas kernels for 10%

profile of v1, /device:TPU:0, one launch (start us, length us, event | category | flops | bytes accessed | tf_op | source)
XLA Modules:
  0.0 384.6 jit_solution(1392717860083431911)
XLA Ops:
  0.7 5.8 %copy-done = bf16[1,1024,8192]{2,1,0:T(8,128)(2,1)S(1)} copy-done((bf16[1,1024,8192]{2,1,0:T(8,128)(2,1)S(1)}, bf16[1,1024,8192]{2,1,0:T(8,128)(2,1)}, u32[]{:S(2)}) %copy-start) | copy-done | bytes 16777240
  11.3 4.8 %collective-permute-start.3 = (bf16[128,1024]{1,0:T(8,128)(2,1)S(1)}, bf16[128,1024]{1,0:T(8,128)(2,1)S(1)}, u32[]{:S(2)}, u32[]{:S(2)}) collective-permute-start(bf16[128,1024]{1,0:T(8,128)(2,1)S(1)} %get-tuple-element.35), channel_id=1, source_target_pairs={{0,1},{1,0},{2,3},{3,2},{4,5},{5,4},{6,7},{7,6}} | collective-permute-start | bytes 786440 | tf_op jit(solution)/shard_map/ppermute | solution.py:122
  18.1 3.9 %collective-permute-start.7 = (bf16[128,1024]{1,0:T(8,128)(2,1)S(1)}, bf16[128,1024]{1,0:T(8,128)(2,1)S(1)}, u32[]{:S(2)}, u32[]{:S(2)}) collective-permute-start(bf16[128,1024]{1,0:T(8,128)(2,1)S(1)} %get-tuple-element.39), channel_id=1, source_target_pairs={{0,1},{1,0},{2,3},{3,2},{4,5},{5,4},{6,7},{7,6}} | collective-permute-start | bytes 786440 | tf_op jit(solution)/shard_map/ppermute | solution.py:122
  24.0 5.8 %copy-done.1 = bf16[1,1024,8192]{2,1,0:T(8,128)(2,1)S(1)} copy-done((bf16[1,1024,8192]{2,1,0:T(8,128)(2,1)S(1)}, bf16[1,1024,8192]{2,1,0:T(8,128)(2,1)}, u32[]{:S(2)}) %copy-start.1) | copy-done | bytes 16777240
  33.1 6.0 %collective-permute-start.4 = (bf16[128,1024]{1,0:T(8,128)(2,1)S(1)}, bf16[128,1024]{1,0:T(8,128)(2,1)S(1)}, u32[]{:S(2)}, u32[]{:S(2)}) collective-permute-start(bf16[128,1024]{1,0:T(8,128)(2,1)S(1)} %add_convert_fusion.12), channel_id=1, source_target_pairs={{0,6},{1,7},{2,4},{3,5},{4,2},{5,3},{6,0},{7,1}} | collective-permute-start | bytes 786440 | tf_op jit(solution)/shard_map/ppermute | solution.py:122
  43.9 3.6 collective-permute-start
  49.3 3.4 collective-permute-start.1
  54.8 4.3 %collective-permute-start.2 = (f32[128]{0:T(128)S(1)}, f32[128]{0:T(128)S(1)}, u32[]{:S(2)}, u32[]{:S(2)}) collective-permute-start(f32[128]{0:T(128)S(1)} %add.192), channel_id=1, source_target_pairs={{0,4},{1,5},{2,6},{3,7},{4,0},{5,1},{6,2},{7,3}} | collective-permute-start | bytes 1544 | tf_op jit(solution)/shard_map/ppermute | solution.py:122
  64.1 5.8 %copy-done.2 = bf16[1,1024,8192]{2,1,0:T(8,128)(2,1)S(1)} copy-done((bf16[1,1024,8192]{2,1,0:T(8,128)(2,1)S(1)}, bf16[1,1024,8192]{2,1,0:T(8,128)(2,1)}, u32[]{:S(2)}) %copy-start.2) | copy-done | bytes 16777240
  86.7 5.8 %copy-done.3 = bf16[1,1024,8192]{2,1,0:T(8,128)(2,1)S(1)} copy-done((bf16[1,1024,8192]{2,1,0:T(8,128)(2,1)S(1)}, bf16[1,1024,8192]{2,1,0:T(8,128)(2,1)}, u32[]{:S(2)}) %copy-start.3) | copy-done | bytes 16777240
  103.9 54.8 %collective-permute-start.28 = (bf16[128,1024]{1,0:T(8,128)(2,1)S(1)}, bf16[128,1024]{1,0:T(8,128)(2,1)S(1)}, u32[]{:S(2)}, u32[]{:S(2)}) collective-permute-start(bf16[128,1024]{1,0:T(8,128)(2,1)S(1)} %add_convert_fusion.4), channel_id=1, source_target_pairs={{16,20},{17,21},{18,22},{19,23},{20,16},{21,17},{22,18},{23,19}} | collective-permute-start | bytes 786440 | tf_op jit(solution)/shard_map/ppermute | solution.py:122
  164.0 16.7 %collective-permute-start.32 = (bf16[128,1024]{1,0:T(8,128)(2,1)}, bf16[128,1024]{1,0:T(8,128)(2,1)}, u32[]{:S(2)}, u32[]{:S(2)}) collective-permute-start(bf16[128,1024]{1,0:T(8,128)(2,1)} %fusion.3), channel_id=1, source_target_pairs={{16,24},{17,25},{18,26},{19,27},{20,28},{21,29},{22,30},{23,31}} | collective-permute-start | bytes 786440 | tf_op jit(solution)/shard_map/ppermute | solution.py:122
  180.8 5.8 %copy-done.4 = bf16[1,1024,8192]{2,1,0:T(8,128)(2,1)S(1)} copy-done((bf16[1,1024,8192]{2,1,0:T(8,128)(2,1)S(1)}, bf16[1,1024,8192]{2,1,0:T(8,128)(2,1)}, u32[]{:S(2)}) %copy-start.4) | copy-done | bytes 16777240
  186.5 9.2 %shard_map.65 = f32[128,1024]{1,0:T(8,128)S(1)} custom-call(s32[8]{0:T(128)S(1)} %stack.37.refs_0_, bf16[1024,8192]{1,0:T(8,128)(2,1)S(1)} %bitcast.36, bf16[128,1024]{1,0:T(8,128)(2,1)S(1)} %bitcast.48, bf16[128,1024]{1,0:T(8,128)(2,1)S(1)} %collective-permute-done.33.refs_3_, bf16[128,1024]{1,0:T(8,128)(2,1)S(1)} %collective-permute-done.34.refs_4_, ...), custom_call_target="tpu_custom_call" | custom-call | flops 2147483648 | bytes 16777216 | tf_op jit(solution)/shard_map/pallas_call | solution.py:82
  198.3 18.2 %collective-permute-start.50 = (bf16[128,1024]{1,0:T(8,128)(2,1)S(1)}, bf16[128,1024]{1,0:T(8,128)(2,1)S(1)}, u32[]{:S(2)}, u32[]{:S(2)}) collective-permute-start(bf16[128,1024]{1,0:T(8,128)(2,1)S(1)} %fusion.17), channel_id=1, source_target_pairs={{24,16},{25,17},{26,18},{27,19},{28,20},{29,21},{30,22},{31,23}} | collective-permute-start | bytes 786440 | tf_op jit(solution)/shard_map/ppermute | solution.py:122
  221.5 16.2 %collective-permute-start.58 = (f32[128]{0:T(128)S(1)}, f32[128]{0:T(128)S(1)}, u32[]{:S(2)}, u32[]{:S(2)}) collective-permute-start(f32[128]{0:T(128)S(1)} %convert_element_type.637), channel_id=1, source_target_pairs={{16,17},{17,16},{18,19},{19,18},{20,21},{21,20},{22,23},{23,22}} | collective-permute-start | bytes 1544 | tf_op jit(solution)/shard_map/ppermute | solution.py:122
  238.4 8.8 %collective-permute-start.57 = (bf16[128,1024]{1,0:T(8,128)(2,1)S(1)}, bf16[128,1024]{1,0:T(8,128)(2,1)S(1)}, u32[]{:S(2)}, u32[]{:S(2)}) collective-permute-start(bf16[128,1024]{1,0:T(8,128)(2,1)S(1)} %collective-permute-done.56.refs_8_), channel_id=1, source_target_pairs={{16,17},{17,16},{18,19},{19,18},{20,21},{21,20},{22,23},{23,22}} | collective-permute-start | bytes 786440 | tf_op jit(solution)/shard_map/ppermute | solution.py:122
  250.1 5.8 %copy-done.5 = bf16[1,1024,8192]{2,1,0:T(8,128)(2,1)S(1)} copy-done((bf16[1,1024,8192]{2,1,0:T(8,128)(2,1)S(1)}, bf16[1,1024,8192]{2,1,0:T(8,128)(2,1)}, u32[]{:S(2)}) %copy-start.5) | copy-done | bytes 16777240
  255.9 9.2 %shard_map.68 = f32[128,1024]{1,0:T(8,128)S(1)} custom-call(s32[8]{0:T(128)S(1)} %stack.37.refs_0_, bf16[1024,8192]{1,0:T(8,128)(2,1)S(1)} %bitcast.37, bf16[128,1024]{1,0:T(8,128)(2,1)S(1)} %collective-permute-done.50.refs_2_, bf16[128,1024]{1,0:T(8,128)(2,1)S(1)} %collective-permute-done.51.refs_3_, bf16[128,1024]{1,0:T(8,128)(2,1)S(1)} %collective-permute-done.52.refs_4_, ...), custom_call_target="tpu_custom_call" | custom-call | flops 2147483648 | bytes 16777216 | tf_op jit(solution)/shard_map/pallas_call | solution.py:82
  276.9 9.2 %shard_map.69 = f32[128,1024]{1,0:T(8,128)S(1)} custom-call(s32[8]{0:T(128)S(1)} %stack.37.refs_0_, bf16[1024,8192]{1,0:T(8,128)(2,1)S(1)} %bitcast.39, bf16[128,1024]{1,0:T(8,128)(2,1)S(1)} %collective-permute-done.61.refs_2_, bf16[128,1024]{1,0:T(8,128)(2,1)S(1)} %collective-permute-done.62.refs_3_, bf16[128,1024]{1,0:T(8,128)(2,1)S(1)} %collective-permute-done.63.refs_4_, ...), custom_call_target="tpu_custom_call" | custom-call | flops 2147483648 | bytes 16777216 | tf_op jit(solution)/shard_map/pallas_call | solution.py:82
  293.6 42.9 %collective-permute-done.72.refs_2_ = bf16[128,1024]{1,0:T(8,128)(2,1)S(1)} collective-permute-done((bf16[128,1024]{1,0:T(8,128)(2,1)S(1)}, bf16[128,1024]{1,0:T(8,128)(2,1)S(1)}, u32[]{:S(2)}, u32[]{:S(2)}) %collective-permute-start.72) | collective-permute-done | bytes 262176 | tf_op jit(solution)/shard_map/ppermute | solution.py:122
  345.1 3.4 collective-permute-start.78
  348.5 3.6 collective-permute-start.76
  374.5 9.2 %shard_map.70 = f32[128,1024]{1,0:T(8,128)S(1)} custom-call(s32[8]{0:T(128)S(1)} %stack.37.refs_0_, bf16[1024,8192]{1,0:T(8,128)(2,1)S(1)} %bitcast.41, bf16[128,1024]{1,0:T(8,128)(2,1)S(1)} %collective-permute-done.72.refs_2_, bf16[128,1024]{1,0:T(8,128)(2,1)S(1)} %collective-permute-done.73.refs_3_, bf16[128,1024]{1,0:T(8,128)(2,1)S(1)} %collective-permute-done.74.refs_4_, ...), custom_call_target="tpu_custom_call" | custom-call | flops 2147483648 | bytes 16777216 | tf_op jit(solution)/shard_map/pallas_call | solution.py:82
  (266 shorter events, 120.3 us)
Async XLA Ops:
  11.3 21.7 %collective-permute-start.3 = (bf16[128,1024]{1,0:T(8,128)(2,1)S(1)}, bf16[128,1024]{1,0:T(8,128)(2,1)S(1)}, u32[]{:S(2)}, u32[]{:S(2)}) collective-permute-start(bf16[128,1024]{1,0:T(8,128)(2,1)S(1)} %get-tuple-element.35), channel_id=1, source_target_pairs={{0,1},{1,0},{2,3},{3,2},{4,5},{5,4},{6,7},{7,6}} | collective-permute-start | bytes 786440 | tf_op jit(solution)/shard_map/ppermute | solution.py:122
  16.2 22.9 %collective-permute-start.5 = (bf16[128,1024]{1,0:T(8,128)(2,1)S(1)}, bf16[128,1024]{1,0:T(8,128)(2,1)S(1)}, u32[]{:S(2)}, u32[]{:S(2)}) collective-permute-start(bf16[128,1024]{1,0:T(8,128)(2,1)S(1)} %get-tuple-element.37), channel_id=1, source_target_pairs={{0,1},{1,0},{2,3},{3,2},{4,5},{5,4},{6,7},{7,6}} | collective-permute-start | bytes 786440 | tf_op jit(solution)/shard_map/ppermute | solution.py:122
  18.1 23.0 %collective-permute-start.7 = (bf16[128,1024]{1,0:T(8,128)(2,1)S(1)}, bf16[128,1024]{1,0:T(8,128)(2,1)S(1)}, u32[]{:S(2)}, u32[]{:S(2)}) collective-permute-start(bf16[128,1024]{1,0:T(8,128)(2,1)S(1)} %get-tuple-element.39), channel_id=1, source_target_pairs={{0,1},{1,0},{2,3},{3,2},{4,5},{5,4},{6,7},{7,6}} | collective-permute-start | bytes 786440 | tf_op jit(solution)/shard_map/ppermute | solution.py:122
  22.0 39.1 %collective-permute-start.9 = (bf16[128,1024]{1,0:T(8,128)(2,1)S(1)}, bf16[128,1024]{1,0:T(8,128)(2,1)S(1)}, u32[]{:S(2)}, u32[]{:S(2)}) collective-permute-start(bf16[128,1024]{1,0:T(8,128)(2,1)S(1)} %get-tuple-element.41), channel_id=1, source_target_pairs={{0,1},{1,0},{2,3},{3,2},{4,5},{5,4},{6,7},{7,6}} | collective-permute-start | bytes 786440 | tf_op jit(solution)/shard_map/ppermute | solution.py:122
  33.1 28.0 %collective-permute-start.4 = (bf16[128,1024]{1,0:T(8,128)(2,1)S(1)}, bf16[128,1024]{1,0:T(8,128)(2,1)S(1)}, u32[]{:S(2)}, u32[]{:S(2)}) collective-permute-start(bf16[128,1024]{1,0:T(8,128)(2,1)S(1)} %add_convert_fusion.12), channel_id=1, source_target_pairs={{0,6},{1,7},{2,4},{3,5},{4,2},{5,3},{6,0},{7,1}} | collective-permute-start | bytes 786440 | tf_op jit(solution)/shard_map/ppermute | solution.py:122
  39.2 21.9 %collective-permute-start.6 = (bf16[128,1024]{1,0:T(8,128)(2,1)S(1)}, bf16[128,1024]{1,0:T(8,128)(2,1)S(1)}, u32[]{:S(2)}, u32[]{:S(2)}) collective-permute-start(bf16[128,1024]{1,0:T(8,128)(2,1)S(1)} %add_convert_fusion.11), channel_id=1, source_target_pairs={{0,4},{1,5},{2,6},{3,7},{4,0},{5,1},{6,2},{7,3}} | collective-permute-start | bytes 786440 | tf_op jit(solution)/shard_map/ppermute | solution.py:122
  41.2 19.9 %collective-permute-start.8 = (bf16[128,1024]{1,0:T(8,128)(2,1)S(1)}, bf16[128,1024]{1,0:T(8,128)(2,1)S(1)}, u32[]{:S(2)}, u32[]{:S(2)}) collective-permute-start(bf16[128,1024]{1,0:T(8,128)(2,1)S(1)} %add_convert_fusion.10), channel_id=1, source_target_pairs={{0,2},{1,3},{2,0},{3,1},{4,6},{5,7},{6,4},{7,5}} | collective-permute-start | bytes 786440 | tf_op jit(solution)/shard_map/ppermute | solution.py:122
  85.2 73.6 %collective-permute-start.36 = (bf16[128,1024]{1,0:T(8,128)(2,1)S(1)}, bf16[128,1024]{1,0:T(8,128)(2,1)S(1)}, u32[]{:S(2)}, u32[]{:S(2)}) collective-permute-start(bf16[128,1024]{1,0:T(8,128)(2,1)S(1)} %bitcast.45), channel_id=1, source_target_pairs={{24,28},{25,29},{26,30},{27,31},{28,24},{29,25},{30,26},{31,27}} | collective-permute-start | bytes 786440 | tf_op jit(solution)/shard_map/ppermute | solution.py:122
  100.9 59.2 %collective-permute-start.34 = (bf16[128,1024]{1,0:T(8,128)(2,1)S(1)}, bf16[128,1024]{1,0:T(8,128)(2,1)S(1)}, u32[]{:S(2)}, u32[]{:S(2)}) collective-permute-start(bf16[128,1024]{1,0:T(8,128)(2,1)S(1)} %bitcast.46), channel_id=1, source_target_pairs={{24,26},{25,27},{26,24},{27,25},{28,30},{29,31},{30,28},{31,29}} | collective-permute-start | bytes 786440 | tf_op jit(solution)/shard_map/ppermute | solution.py:122
  102.4 58.4 %collective-permute-start.31 = (bf16[128,1024]{1,0:T(8,128)(2,1)S(1)}, bf16[128,1024]{1,0:T(8,128)(2,1)S(1)}, u32[]{:S(2)}, u32[]{:S(2)}) collective-permute-start(bf16[128,1024]{1,0:T(8,128)(2,1)S(1)} %get-tuple-element.57), channel_id=1, source_target_pairs={{16,17},{17,16},{18,19},{19,18},{20,21},{21,20},{22,23},{23,22}} | collective-permute-start | bytes 786440 | tf_op jit(solution)/shard_map/ppermute | solution.py:122
  103.2 56.3 %collective-permute-start.24 = (f32[128]{0:T(128)S(1)}, f32[128]{0:T(128)S(1)}, u32[]{:S(2)}, u32[]{:S(2)}) collective-permute-start(f32[128]{0:T(128)S(1)} %add.216), channel_id=1, source_target_pairs={{16,20},{17,21},{18,22},{19,23},{20,16},{21,17},{22,18},{23,19}} | collective-permute-start | bytes 1544 | tf_op jit(solution)/shard_map/ppermute | solution.py:122
  103.9 57.6 %collective-permute-start.28 = (bf16[128,1024]{1,0:T(8,128)(2,1)S(1)}, bf16[128,1024]{1,0:T(8,128)(2,1)S(1)}, u32[]{:S(2)}, u32[]{:S(2)}) collective-permute-start(bf16[128,1024]{1,0:T(8,128)(2,1)S(1)} %add_convert_fusion.4), channel_id=1, source_target_pairs={{16,20},{17,21},{18,22},{19,23},{20,16},{21,17},{22,18},{23,19}} | collective-permute-start | bytes 786440 | tf_op jit(solution)/shard_map/ppermute | solution.py:122
  160.1 20.6 %collective-permute-start.33 = (bf16[128,1024]{1,0:T(8,128)(2,1)S(1)}, bf16[128,1024]{1,0:T(8,128)(2,1)S(1)}, u32[]{:S(2)}, u32[]{:S(2)}) collective-permute-start(bf16[128,1024]{1,0:T(8,128)(2,1)S(1)} %bitcast.47), channel_id=1, source_target_pairs={{24,25},{25,24},{26,27},{27,26},{28,29},{29,28},{30,31},{31,30}} | collective-permute-start | bytes 786440 | tf_op jit(solution)/shard_map/ppermute | solution.py:122
  160.8 19.9 %collective-permute-start.39 = (bf16[128,1024]{1,0:T(8,128)(2,1)S(1)}, bf16[128,1024]{1,0:T(8,128)(2,1)S(1)}, u32[]{:S(2)}, u32[]{:S(2)}) collective-permute-start(bf16[128,1024]{1,0:T(8,128)(2,1)S(1)} %collective-permute-done.38.refs_8_), channel_id=1, source_target_pairs={{24,25},{25,24},{26,27},{27,26},{28,29},{29,28},{30,31},{31,30}} | collective-permute-start | bytes 786440 | tf_op jit(solution)/shard_map/ppermute | solution.py:122
  164.0 31.7 %collective-permute-start.32 = (bf16[128,1024]{1,0:T(8,128)(2,1)}, bf16[128,1024]{1,0:T(8,128)(2,1)}, u32[]{:S(2)}, u32[]{:S(2)}) collective-permute-start(bf16[128,1024]{1,0:T(8,128)(2,1)} %fusion.3), channel_id=1, source_target_pairs={{16,24},{17,25},{18,26},{19,27},{20,28},{21,29},{22,30},{23,31}} | collective-permute-start | bytes 786440 | tf_op jit(solution)/shard_map/ppermute | solution.py:122
  216.5 21.9 %collective-permute-start.56 = (bf16[128,1024]{1,0:T(8,128)(2,1)S(1)}, bf16[128,1024]{1,0:T(8,128)(2,1)S(1)}, u32[]{:S(2)}, u32[]{:S(2)}) collective-permute-start(bf16[128,1024]{1,0:T(8,128)(2,1)S(1)} %collective-permute-done.50.refs_2_), channel_id=1, source_target_pairs={{16,22},{17,23},{18,20},{19,21},{20,18},{21,19},{22,16},{23,17}} | collective-permute-start | bytes 786440 | tf_op jit(solution)/shard_map/ppermute | solution.py:122
  217.2 30.1 %collective-permute-start.54 = (bf16[128,1024]{1,0:T(8,128)(2,1)S(1)}, bf16[128,1024]{1,0:T(8,128)(2,1)S(1)}, u32[]{:S(2)}, u32[]{:S(2)}) collective-permute-start(bf16[128,1024]{1,0:T(8,128)(2,1)S(1)} %collective-permute-done.50.refs_2_), channel_id=1, source_target_pairs={{16,20},{17,21},{18,22},{19,23},{20,16},{21,17},{22,18},{23,19}} | collective-permute-start | bytes 786440 | tf_op jit(solution)/shard_map/ppermute | solution.py:122
  217.9 30.1 %collective-permute-start.52 = (bf16[128,1024]{1,0:T(8,128)(2,1)S(1)}, bf16[128,1024]{1,0:T(8,128)(2,1)S(1)}, u32[]{:S(2)}, u32[]{:S(2)}) collective-permute-start(bf16[128,1024]{1,0:T(8,128)(2,1)S(1)} %collective-permute-done.50.refs_2_), channel_id=1, source_target_pairs={{16,18},{17,19},{18,16},{19,17},{20,22},{21,23},{22,20},{23,21}} | collective-permute-start | bytes 786440 | tf_op jit(solution)/shard_map/ppermute | solution.py:122
  221.5 27.1 %collective-permute-start.58 = (f32[128]{0:T(128)S(1)}, f32[128]{0:T(128)S(1)}, u32[]{:S(2)}, u32[]{:S(2)}) collective-permute-start(f32[128]{0:T(128)S(1)} %convert_element_type.637), channel_id=1, source_target_pairs={{16,17},{17,16},{18,19},{19,18},{20,21},{21,20},{22,23},{23,22}} | collective-permute-start | bytes 1544 | tf_op jit(solution)/shard_map/ppermute | solution.py:122
  286.3 50.2 %collective-permute-start.72 = (bf16[128,1024]{1,0:T(8,128)(2,1)S(1)}, bf16[128,1024]{1,0:T(8,128)(2,1)S(1)}, u32[]{:S(2)}, u32[]{:S(2)}) collective-permute-start(bf16[128,1024]{1,0:T(8,128)(2,1)S(1)} %fusion.8), channel_id=1, source_target_pairs={{8,0},{9,1},{10,2},{11,3},{12,4},{13,5},{14,6},{15,7}} | collective-permute-start | bytes 786440 | tf_op jit(solution)/shard_map/ppermute | solution.py:122
  290.8 48.7 %collective-permute-start.43 = (bf16[128,1024]{1,0:T(8,128)(2,1)S(1)}, bf16[128,1024]{1,0:T(8,128)(2,1)S(1)}, u32[]{:S(2)}, u32[]{:S(2)}) collective-permute-start(bf16[128,1024]{1,0:T(8,128)(2,1)S(1)} %get-tuple-element.59), channel_id=1, source_target_pairs={{24,25},{25,24},{26,27},{27,26},{28,29},{29,28},{30,31},{31,30}} | collective-permute-start | bytes 786440 | tf_op jit(solution)/shard_map/ppermute | solution.py:122
  291.5 52.9 %collective-permute-start.47 = (bf16[128,1024]{1,0:T(8,128)(2,1)S(1)}, bf16[128,1024]{1,0:T(8,128)(2,1)S(1)}, u32[]{:S(2)}, u32[]{:S(2)}) collective-permute-start(bf16[128,1024]{1,0:T(8,128)(2,1)S(1)} %get-tuple-element.63), channel_id=1, source_target_pairs={{24,25},{25,24},{26,27},{27,26},{28,29},{29,28},{30,31},{31,30}} | collective-permute-start | bytes 786440 | tf_op jit(solution)/shard_map/ppermute | solution.py:122
  292.2 52.9 %collective-permute-start.49 = (bf16[128,1024]{1,0:T(8,128)(2,1)S(1)}, bf16[128,1024]{1,0:T(8,128)(2,1)S(1)}, u32[]{:S(2)}, u32[]{:S(2)}) collective-permute-start(bf16[128,1024]{1,0:T(8,128)(2,1)S(1)} %get-tuple-element.65), channel_id=1, source_target_pairs={{24,25},{25,24},{26,27},{27,26},{28,29},{29,28},{30,31},{31,30}} | collective-permute-start | bytes 786440 | tf_op jit(solution)/shard_map/ppermute | solution.py:122
  292.9 55.6 %collective-permute-start.46 = (bf16[128,1024]{1,0:T(8,128)(2,1)S(1)}, bf16[128,1024]{1,0:T(8,128)(2,1)S(1)}, u32[]{:S(2)}, u32[]{:S(2)}) collective-permute-start(bf16[128,1024]{1,0:T(8,128)(2,1)S(1)} %add_convert_fusion.1), channel_id=1, source_target_pairs={{24,28},{25,29},{26,30},{27,31},{28,24},{29,25},{30,26},{31,27}} | collective-permute-start | bytes 786440 | tf_op jit(solution)/shard_map/ppermute | solution.py:122
  (85 other events, 628.4 us)

commit v2 on v1

v2 whole, which is shorter than its diff:
```python
import jax
import jax.numpy as jnp
from jax import lax
from jax.experimental import pallas as pl
from jax.experimental.pallas import tpu as pltpu
from jax.sharding import PartitionSpec as P

EPSILON = 1e-05
MIB = 1 << 20
TAIL = 16
LANES = 128
VMEM_LIMIT = 20 * MIB
SMEM_SPEC = pl.BlockSpec(memory_space=pltpu.SMEM)
VMEM_SPEC = pl.BlockSpec(memory_space=pltpu.VMEM)


def as_line(column):
    return jnp.broadcast_to(column, (column.shape[0], LANES)).T[:1]


def as_column(line):
    return jnp.broadcast_to(line, (LANES, line.shape[1])).T[:, :1]


def store_tail(out_ref, rows, line, row_no):
    row_ids = lax.broadcasted_iota(jnp.int32, (TAIL, rows), 0)
    tile = jnp.where(row_ids == row_no, jnp.broadcast_to(line, (TAIL, rows)), 0.0)
    out_ref[rows:, :] = jnp.zeros((TAIL, out_ref.shape[1]), out_ref.dtype)
    out_ref[rows:, :rows] = tile.astype(out_ref.dtype)


def tail_sum(chunk_refs, rows):
    total = chunk_refs[0][rows:, :rows].astype(jnp.float32)
    for chunk in chunk_refs[1:]:
        total = total + chunk[rows:, :rows].astype(jnp.float32)
    return jnp.sum(total, axis=0, keepdims=True)


def matmul_cost(rows, width, count):
    return pl.CostEstimate(
        flops=2 * rows * width * width * count,
        bytes_accessed=2 * width * width * count,
        transcendentals=0,
    )


def forward_blocks(a, gain_row, w_rows, blocks, tail_row, other=None, use_other=None):
    rows, width = a.shape
    count = len(blocks)
    with_other = other is not None
    meta = jnp.stack(blocks + [tail_row] + ([use_other] if with_other else []))

    def kernel(meta_ref, *refs):
        a_ref, gain_ref, w_ref = refs[:3]
        other_ref = refs[3] if with_other else None
        out_refs = refs[4 if with_other else 3 : -1]
        scaled_ref = refs[-1]
        step = pl.program_id(0)

        @pl.when(step == 0)
        def _():
            wide = a_ref[...].astype(jnp.float32)
            scaled_ref[...] = (wide * gain_ref[...]).astype(jnp.bfloat16)
            line = as_line(jnp.sum(wide * wide, axis=1, keepdims=True))
            for out_ref in out_refs:
                store_tail(out_ref, rows, line, meta_ref[count])

        partial = jnp.dot(scaled_ref[...], w_ref[...], preferred_element_type=jnp.float32)
        for block in range(count):

            @pl.when(step == block)
            def _(block=block):
                out_refs[block][:rows, :] = partial.astype(jnp.bfloat16)

        if with_other:

            @pl.when((step == count - 1) & (meta_ref[count + 1] == 1))
            def _():
                for out_ref in out_refs:
                    out_ref[...] = other_ref[...]

    def whole(shape):
        return pl.BlockSpec(shape, lambda k, meta_ref: (0, 0))

    chunk = (rows + TAIL, width)
    return pl.pallas_call(
        kernel,
        out_shape=[jax.ShapeDtypeStruct(chunk, jnp.bfloat16)] * count,
        grid_spec=pltpu.PrefetchScalarGridSpec(
            num_scalar_prefetch=1,
            grid=(count,),
            in_specs=[
                whole((rows, width)),
                whole((1, width)),
                pl.BlockSpec((width, width), lambda k, meta_ref: (0, meta_ref[k])),
            ]
            + [whole(chunk)] * with_other,
            out_specs=[whole(chunk)] * count,
            scratch_shapes=[pltpu.VMEM((rows, width), jnp.bfloat16)],
        ),
        compiler_params=pltpu.CompilerParams(vmem_limit_bytes=VMEM_LIMIT),
        cost_estimate=matmul_cost(rows, width, count),
    )(meta, a, gain_row, w_rows, *([other] if with_other else []))


def add_chunks(chunks, other=None, use_other=None):
    def kernel(meta_ref, *refs):
        total = refs[0][...].astype(jnp.float32)
        for chunk in refs[1 : len(chunks)]:
            total = total + chunk[...].astype(jnp.float32)
        refs[-1][...] = total.astype(jnp.bfloat16)
        if other is not None:

            @pl.when(meta_ref[0] == 1)
            def _():
                refs[-1][...] = refs[len(chunks)][...]

    operands = chunks + ([other] if other is not None else [])
    meta = jnp.stack([use_other if other is not None else jnp.int32(0)])
    return pl.pallas_call(
        kernel,
        out_shape=jax.ShapeDtypeStruct(chunks[0].shape, jnp.bfloat16),
        in_specs=[SMEM_SPEC] + [VMEM_SPEC] * len(operands),
        out_specs=VMEM_SPEC,
        compiler_params=pltpu.CompilerParams(vmem_limit_bytes=VMEM_LIMIT),
    )(meta, *operands)


def finish_forward(chunks, a, full_width, kept, keep):
    rows, width = a.shape

    def kernel(meta_ref, a_ref, *refs):
        chunk_refs, rest = refs[: len(chunks)], refs[len(chunks) :]
        old_refs, (out_ref, *new_refs) = rest[:3], rest[3:]
        branch = chunk_refs[0][:rows, :].astype(jnp.float32)
        for chunk in chunk_refs[1:]:
            branch = branch + chunk[:rows, :].astype(jnp.float32)
        squares = as_column(tail_sum(chunk_refs, rows))
        inv_rms = lax.rsqrt(squares / full_width + EPSILON)
        out_ref[...] = (a_ref[...].astype(jnp.float32) + inv_rms * branch).astype(jnp.bfloat16)
        held = meta_ref[0] == 1

        @pl.when(held)
        def _():
            new_refs[0][...] = out_ref[...]
            new_refs[1][...] = branch
            new_refs[2][...] = jnp.broadcast_to(inv_rms, (rows, LANES))

        @pl.when(jnp.logical_not(held))
        def _():
            for new, old in zip(new_refs, old_refs):
                new[...] = old[...]

    out = jax.ShapeDtypeStruct((rows, width), jnp.bfloat16)
    return pl.pallas_call(
        kernel,
        out_shape=[out, out, jax.ShapeDtypeStruct((rows, width), jnp.float32), jax.ShapeDtypeStruct((rows, LANES), jnp.float32)],
        in_specs=[SMEM_SPEC] + [VMEM_SPEC] * (1 + len(chunks) + 3),
        out_specs=[VMEM_SPEC] * 4,
        compiler_params=pltpu.CompilerParams(vmem_limit_bytes=VMEM_LIMIT),
    )(jnp.stack([keep]), a, *chunks, *kept)


def gradient_chunks(upstream, branch, tail_row, others, use_other):
    rows, width = upstream.shape
    replaced = [other for other in others if other is not None]

    def kernel(meta_ref, up_ref, branch_ref, *refs):
        other_refs, out_refs = list(refs[: len(replaced)]), refs[len(replaced) :]
        up = up_ref[...]
        line = as_line(
            jnp.sum(up.astype(jnp.float32) * branch_ref[...], axis=1, keepdims=True)
        )
        for out_ref in out_refs:
            out_ref[:rows, :] = up
            store_tail(out_ref, rows, line, meta_ref[0])

        @pl.when(meta_ref[1] == 1)
        def _():
            for other, out_ref in zip(others, out_refs):
                if other is not None:
                    out_ref[...] = other_refs.pop(0)[...]

    return pl.pallas_call(
        kernel,
        out_shape=[jax.ShapeDtypeStruct((rows + TAIL, width), jnp.bfloat16)] * len(others),
        in_specs=[SMEM_SPEC] + [VMEM_SPEC] * (2 + len(replaced)),
        out_specs=[VMEM_SPEC] * len(others),
        compiler_params=pltpu.CompilerParams(vmem_limit_bytes=VMEM_LIMIT),
    )(jnp.stack([tail_row, use_other]), upstream, branch, *replaced)


def backward_blocks(chunks, w_rows, blocks):
    rows = chunks[0].shape[0] - TAIL
    width = w_rows.shape[0]
    count = len(blocks)

    def kernel(meta_ref, w_ref, *refs):
        chunk_refs, (out_ref, sum_ref, held_ref) = refs[:count], refs[count:]
        step = pl.program_id(0)
        for block in range(count):

            @pl.when(step == block)
            def _(block=block):
                held_ref[...] = chunk_refs[block][:rows, :]

        product = lax.dot_general(
            w_ref[...], held_ref[...], (((1,), (1,)), ((), ())), preferred_element_type=jnp.float32
        )

        @pl.when(step == 0)
        def _():
            out_ref[...] = product
            sum_ref[...] = jnp.broadcast_to(tail_sum(chunk_refs, rows), (8, rows))

        @pl.when(step > 0)
        def _():
            out_ref[...] += product

    def whole(shape):
        return pl.BlockSpec(shape, lambda k, meta_ref: (0, 0))

    return pl.pallas_call(
        kernel,
        out_shape=[jax.ShapeDtypeStruct((width, rows), jnp.float32), jax.ShapeDtypeStruct((8, rows), jnp.float32)],
        grid_spec=pltpu.PrefetchScalarGridSpec(
            num_scalar_prefetch=1,
            grid=(count,),
            in_specs=[pl.BlockSpec((width, width), lambda k, meta_ref: (0, meta_ref[k]))]
            + [whole((rows + TAIL, width))] * count,
            out_specs=[whole((width, rows)), whole((8, rows))],
            scratch_shapes=[pltpu.VMEM((rows, width), jnp.bfloat16)],
        ),
        compiler_params=pltpu.CompilerParams(vmem_limit_bytes=VMEM_LIMIT),
        cost_estimate=matmul_cost(rows, width, count),
    )(jnp.stack(blocks), w_rows, *chunks)


def finish_backward(halves, upstream, inv_rms, gain_row, a, full_width, grads, keep):
    rows, width = a.shape

    def kernel(meta_ref, b0_ref, s0_ref, b1_ref, s1_ref, up_ref, rms_ref, gain_ref, a_ref, old_ref, out_ref, new_ref):
        back = (b0_ref[...] + b1_ref[...]).T
        row_dot = as_column((s0_ref[...] + s1_ref[...])[:1])
        rms = rms_ref[:, :1]
        grad = (
            up_ref[...].astype(jnp.float32)
            + rms * gain_ref[...] * back
            - (rms * rms * rms / full_width * row_dot) * a_ref[...].astype(jnp.float32)
        ).astype(jnp.bfloat16)
        out_ref[...] = grad
        held = meta_ref[0] == 1

        @pl.when(held)
        def _():
            new_ref[...] = grad

        @pl.when(jnp.logical_not(held))
        def _():
            new_ref[...] = old_ref[...]

    out = jax.ShapeDtypeStruct((rows, width), jnp.bfloat16)
    return pl.pallas_call(
        kernel,
        out_shape=[out, out],
        in_specs=[SMEM_SPEC] + [VMEM_SPEC] * 9,
        out_specs=[VMEM_SPEC] * 2,
        compiler_params=pltpu.CompilerParams(vmem_limit_bytes=VMEM_LIMIT),
    )(jnp.stack([keep]), *halves[0], *halves[1], upstream, inv_rms, gain_row, a, grads)


def on_device(inputs, cotangent, weights, gains):
    section_no = lax.axis_index("section")
    section_count = lax.axis_size("section")
    tp_no = lax.axis_index("tp")
    tp_count = lax.axis_size("tp")
    micro_count, row_count, width = inputs.shape
    rows = micro_count * row_count
    full_width = weights.shape[2]
    w_rows = weights[0]
    last = section_count - 1
    across = tp_count // 2
    near = list(range(1, across))
    tail_row = tp_no % TAIL

    def send(value, sections, step=0, hop=0):
        pairs = [
            (s * tp_count + t, (s + hop) * tp_count + (t ^ step))
            for s in sections
            for t in range(tp_count)
        ]
        return lax.ppermute(value, ("section", "tp"), pairs)

    def is_section(section):
        return (section_no == section).astype(jnp.int32)

    def row_totals(partial, sections):
        total = partial
        step = 1
        while step < tp_count:
            total = total + send(total, sections, step)
            step *= 2
        return total

    def row_sum(value):
        return jnp.sum(value, axis=1).astype(jnp.bfloat16).astype(jnp.float32)

    cot = cotangent.reshape(rows, width)
    block_in = inputs.reshape(rows, width)
    kept = (
        jnp.zeros_like(block_in),
        jnp.zeros((rows, width), jnp.float32),
        jnp.zeros((rows, LANES), jnp.float32),
    )
    far_blocks = [tp_no ^ across ^ e for e in [0] + near]
    near_blocks = [tp_no ^ e for e in [0] + near]

    cot_chunk = jnp.pad(cot, ((0, TAIL), (0, 0)))
    other = cot_chunk
    cot_found = {0: cot_chunk}
    last_back = None
    for section in range(last):
        shared = section < 2
        sections = [section] + ([last] if shared else [])
        use_other = is_section(last) if shared else None
        far = forward_blocks(
            block_in, gains, w_rows, far_blocks, tail_row, other if shared else None, use_other
        )
        arrived = [send(chunk, sections, e) for e, chunk in zip(near, far[1:])]
        own = forward_blocks(block_in, gains, w_rows, near_blocks, tail_row)
        if shared:
            for e, chunk in zip(near, arrived):
                cot_found[e if section == 0 else across ^ e] = chunk
        first_pass = section == 0
        combined = add_chunks(
            [far[0]] + arrived, other if first_pass else None, use_other if first_pass else None
        )
        crossed = send(combined, [section] + ([last] if first_pass else []), across)
        if first_pass:
            cot_found[across] = other = crossed
        direct = [send(chunk, [section], e) for e, chunk in zip(near, own[1:])]
        output, *kept = finish_forward(
            [own[0]] + direct + [crossed], block_in, full_width, kept, is_section(section)
        )
        incoming = send(output, [section], hop=1)
        block_in = jnp.where(section_no == section + 1, incoming, block_in)
        if section == 1:
            order = sorted(cot_found)

            def cotangent_rows():
                chunks = [cot_found[e] for e in order]
                back, _ = backward_blocks(chunks, w_rows, [tp_no ^ e for e in order])
                return gains * back.T

            last_back = lax.cond(
                section_no == last, cotangent_rows, lambda: jnp.zeros((rows, width), jnp.float32)
            )

    outputs, branch, inv_rms = kept
    wide = block_in.astype(jnp.float32)
    sums = row_totals(jnp.stack([row_sum(wide * wide), row_sum(wide * last_back)]), [last])
    last_rms = lax.rsqrt(sums[0] / full_width + EPSILON)[:, None]
    grad = (
        cot.astype(jnp.float32)
        + last_rms * last_back
        - (last_rms**3 / full_width * sums[1][:, None]) * wide
    ).astype(jnp.bfloat16)
    grads = grad

    chunk_zero = jnp.zeros((rows + TAIL, width), jnp.bfloat16)
    upstream = send(grad, [last], hop=-1)
    last_in, upstream = lax.optimization_barrier((block_in, upstream))
    parts = lax.cond(
        section_no == last,
        lambda: tuple(forward_blocks(last_in, gains, w_rows, far_blocks, tail_row))
        + tuple(forward_blocks(last_in, gains, w_rows, near_blocks, tail_row)),
        lambda: (chunk_zero,) * tp_count,
    )
    far, own = parts[:across], parts[across:]
    for section in range(last - 1, -1, -1):
        turn = last - 1 - section
        if turn == 0:
            others = [None] + list(far[1:])
            cross_sections, near_sections = [section], [section, last]
        elif turn == 1:
            others = [combined] + list(own[1:])
            cross_sections, near_sections = [section, last], [section, last]
        else:
            others = [None] * across
            cross_sections, near_sections = [section], [section]
        chunks = gradient_chunks(upstream, branch, tail_row, others, is_section(last))
        crossed = send(chunks[0], cross_sections, across)
        direct = [send(chunk, near_sections, e) for e, chunk in zip(near, chunks[1:])]
        half = backward_blocks([chunks[0]] + direct, w_rows, near_blocks)
        forwarded = [send(crossed, [section], e) for e in near]
        if turn == 0:
            combined = add_chunks([far[0]] + direct)
        if turn == 1:
            _, outputs, _, _ = finish_forward(
                [own[0]] + direct + [crossed], block_in, full_width, (outputs, branch, inv_rms), is_section(last)
            )
        other_half = backward_blocks([crossed] + forwarded, w_rows, far_blocks)
        grad, grads = finish_backward(
            (half, other_half), upstream, inv_rms, gains, block_in, full_width, grads, is_section(section)
        )
        if section:
            upstream = send(grad, [section], hop=-1)
    shape = (1, micro_count, row_count, width)
    return outputs.reshape(shape), grads.reshape(shape)


def solution(mesh):
    placed = (
        P(None, None, "tp"),
        P(None, None, "tp"),
        P("section", "tp", None),
        P("section", "tp"),
    )
    return jax.shard_map(
        on_device,
        mesh=mesh,
        in_specs=placed,
        out_specs=(P("section", None, None, "tp"), P("section", None, None, "tp")),
        check_vma=False,
    )
```

time: 386 us -> 300 us (0.78)
  starting transfers between devices: 218 us -> 165 us
  local copies, waits for them, and re-layouts: 36.5 us -> 7.84 us
  Pallas kernels: 61.9 us -> 80 us
  waiting for transfers between devices: 56 us -> 42.3 us
  other arithmetic: 9.38 us -> 1.74 us
    ppermute x83 -> x51, starting transfers between devices: 218 us -> 165 us  [send(): return lax.ppermute(value, ('section', 'tp'), pairs)]
    unnamed x52 -> x28, local copies, waits for them, and re-layouts: 36.3 us -> 3.35 us
    pallas_call x12 -> x26, Pallas kernels: 61.9 us -> 80 us  [the longest x6 36.6 us: forward_blocks(): pl.pallas_call(kernel, out_shape=[jax.ShapeDtypeStruct(chunk, jnp.bfloat1...]
    ppermute x83 -> x51, waiting for transfers between devices: 56 us -> 42.3 us  [send(): return lax.ppermute(value, ('section', 'tp'), pairs)]
  transfers between devices with their start and end apart: 83 -> 51, of which waited for: 8 -> 5; matrix products, arithmetic and copies ran while one was open for 2% -> 0% of each run, Pallas kernels for 10% -> 13%
where the time goes in v2:
time: 300 us; the launch traced here: 299 us
  starting transfers between devices  165 us (55%)
  Pallas kernels  80 us (27%)
  waiting for transfers between devices  42.3 us (14%)
  local copies, waits for them, and re-layouts  7.84 us (3%)
    ppermute x51, starting transfers between devices, send(): return lax.ppermute(value, ('section', 'tp'), pairs)  165 us
    ppermute x51, waiting for transfers between devices, send(): return lax.ppermute(value, ('section', 'tp'), pairs)  42.3 us
    pallas_call x6, Pallas kernels, forward_blocks(): pl.pallas_call(kernel, out_shape=[jax.ShapeDtypeStruct(chunk, jnp.bfloat1...  36.6 us
    pallas_call x6, Pallas kernels, backward_blocks(): pl.pallas_call(kernel, out_shape=[jax.ShapeDtypeStruct((width, rows), jnp...  31.1 us
  transfers between devices with their start and end apart: 51, of which 5 were waited for; matrix products, arithmetic and copies ran while one was open for 0% of the time, Pallas kernels for 13%

profile of v2, /device:TPU:0, one launch (start us, length us, event | category | flops | bytes accessed | tf_op | source)
XLA Modules:
  0.0 298.8 jit_solution(9469396180280438361)
XLA Ops:
  2.8 5.7 %shard_map.60 = (bf16[144,1024]{1,0:T(8,128)(2,1)S(1)}, bf16[144,1024]{1,0:T(8,128)(2,1)S(1)}, bf16[144,1024]{1,0:T(8,128)(2,1)S(1)}, bf16[144,1024]{1,0:T(8,128)(2,1)S(1)}) custom-call(s32[6]{0:T(128)S(1)} %stack.127.meta_ref, bf16[128,1024]{1,0:T(8,128)(2,1)S(1)} %bitcast.52, f32[1,1024]{1,0:T(1,128)} %gain_ref.5, bf16[1024,8192]{1,0:T(8,128)(2,1)} %bitcast.55, ...), custom_call_target="tpu_custom_call" | custom-call | flops 1073741824 | bytes 8388608 | tf_op jit(solution)/shard_map/pallas_call | solution.py:86
  8.5 4.8 %collective-permute-start.3 = (bf16[144,1024]{1,0:T(8,128)(2,1)S(1)}, bf16[144,1024]{1,0:T(8,128)(2,1)}, u32[]{:S(2)}, u32[]{:S(2)}) collective-permute-start(bf16[144,1024]{1,0:T(8,128)(2,1)S(1)} %get-tuple-element.164), channel_id=1, source_target_pairs={{0,1},{1,0},{2,3},{3,2},{4,5},{5,4},{6,7},{7,6},{24,25},{25,24},{2... | collective-permute-start | bytes 884744 | tf_op jit(solution)/shard_map/ppermute | solution.py:292
  13.3 3.5 %collective-permute-start.4 = (bf16[144,1024]{1,0:T(8,128)(2,1)S(1)}, bf16[144,1024]{1,0:T(8,128)(2,1)}, u32[]{:S(2)}, u32[]{:S(2)}) collective-permute-start(bf16[144,1024]{1,0:T(8,128)(2,1)S(1)} %get-tuple-element.165), channel_id=1, source_target_pairs={{0,2},{1,3},{2,0},{3,1},{4,6},{5,7},{6,4},{7,5},{24,26},{25,27},{2... | collective-permute-start | bytes 884744 | tf_op jit(solution)/shard_map/ppermute | solution.py:292
  18.9 6.4 %shard_map.59 = (bf16[144,1024]{1,0:T(8,128)(2,1)S(1)}, bf16[144,1024]{1,0:T(8,128)(2,1)}, bf16[144,1024]{1,0:T(8,128)(2,1)S(1)}, bf16[144,1024]{1,0:T(8,128)(2,1)S(1)}) custom-call(s32[5]{0:T(128)S(1)} %stack.122.meta_ref, bf16[128,1024]{1,0:T(8,128)(2,1)S(1)} %bitcast.53, f32[1,1024]{1,0:T(1,128)S(1)} %copy-done.9, bf16[1024,8192]{1,0:T(8,128)(2,1)} %bitcast.56), custom_call_target="tpu_custom_call" | custom-call | flops 1073741824 | bytes 8388608 | tf_op jit(solution)/shard_map/pallas_call | solution.py:86
  25.3 3.8 %collective-permute-start = (bf16[144,1024]{1,0:T(8,128)(2,1)}, bf16[144,1024]{1,0:T(8,128)(2,1)S(1)}, u32[]{:S(2)}, u32[]{:S(2)}) collective-permute-start(bf16[144,1024]{1,0:T(8,128)(2,1)} %get-tuple-element.160), channel_id=1, source_target_pairs={{0,1},{1,0},{2,3},{3,2},{4,5},{5,4},{6,7},{7,6}} | collective-permute-start | bytes 884744 | tf_op jit(solution)/shard_map/ppermute | solution.py:292
  29.1 3.5 %collective-permute-start.1 = (bf16[144,1024]{1,0:T(8,128)(2,1)S(1)}, bf16[144,1024]{1,0:T(8,128)(2,1)S(1)}, u32[]{:S(2)}, u32[]{:S(2)}) collective-permute-start(bf16[144,1024]{1,0:T(8,128)(2,1)S(1)} %get-tuple-element.161), channel_id=1, source_target_pairs={{0,2},{1,3},{2,0},{3,1},{4,6},{5,7},{6,4},{7,5}} | collective-permute-start | bytes 884744 | tf_op jit(solution)/shard_map/ppermute | solution.py:292
  35.8 4.9 %collective-permute-start.6 = (bf16[144,1024]{1,0:T(8,128)(2,1)S(1)}, bf16[144,1024]{1,0:T(8,128)(2,1)S(1)}, u32[]{:S(2)}, u32[]{:S(2)}) collective-permute-start(bf16[144,1024]{1,0:T(8,128)(2,1)S(1)} %shard_map.61), channel_id=1, source_target_pairs={{0,4},{1,5},{2,6},{3,7},{4,0},{5,1},{6,2},{7,3},{24,28},{25,29},{2... | collective-permute-start | bytes 884744 | tf_op jit(solution)/shard_map/ppermute | solution.py:292
  42.1 6.5 %collective-permute-done.6.refs_4_.refs_3_ = bf16[144,1024]{1,0:T(8,128)(2,1)S(1)} collective-permute-done((bf16[144,1024]{1,0:T(8,128)(2,1)S(1)}, bf16[144,1024]{1,0:T(8,128)(2,1)S(1)}, u32[]{:S(2)}, u32[]{:S(2)}) %collective-permute-start.6) | collective-permute-done | bytes 294944 | tf_op jit(solution)/shard_map/ppermute | solution.py:292
  52.3 5.7 %shard_map.64 = (bf16[144,1024]{1,0:T(8,128)(2,1)S(1)}, bf16[144,1024]{1,0:T(8,128)(2,1)S(1)}, bf16[144,1024]{1,0:T(8,128)(2,1)S(1)}, bf16[144,1024]{1,0:T(8,128)(2,1)S(1)}) custom-call(s32[6]{0:T(128)S(1)} %stack.127.meta_ref, bf16[128,1024]{1,0:T(8,128)(2,1)S(1)} %broadcast_select_fusion.refs_0_.a_ref, f32[1,1024]{1,0:T(1,128)S(1)} %copy-done.9, ...), custom_call_target="tpu_custom_call" | custom-call | flops 1073741824 | bytes 8388608 | tf_op jit(solution)/shard_map/pallas_call | solution.py:86
  60.7 6.5 %shard_map.63 = (bf16[144,1024]{1,0:T(8,128)(2,1)S(1)}, bf16[144,1024]{1,0:T(8,128)(2,1)}, bf16[144,1024]{1,0:T(8,128)(2,1)S(1)}, bf16[144,1024]{1,0:T(8,128)(2,1)}) custom-call(s32[5]{0:T(128)S(1)} %stack.122.meta_ref, bf16[128,1024]{1,0:T(8,128)(2,1)S(1)} %broadcast_select_fusion.refs_0_.a_ref, f32[1,1024]{1,0:T(1,128)S(1)} %copy-done.9, ...), custom_call_target="tpu_custom_call" | custom-call | flops 1073741824 | bytes 8388608 | tf_op jit(solution)/shard_map/pallas_call | solution.py:86
  74.7 5.7 %shard_map.68 = (bf16[144,1024]{1,0:T(8,128)(2,1)S(1)}, bf16[144,1024]{1,0:T(8,128)(2,1)S(1)}, bf16[144,1024]{1,0:T(8,128)(2,1)S(1)}, bf16[144,1024]{1,0:T(8,128)(2,1)S(1)}) custom-call(s32[5]{0:T(128)S(1)} %stack.128.meta_ref, bf16[128,1024]{1,0:T(8,128)(2,1)S(1)} %broadcast_select_fusion.1.refs_0_.a_ref, f32[1,1024]{1,0:T(1,128)S(1)} %copy-done.9, ...), custom_call_target="tpu_custom_call" | custom-call | flops 1073741824 | bytes 8388608 | tf_op jit(solution)/shard_map/pallas_call | solution.py:86
  82.5 6.6 %shard_map.67 = (bf16[144,1024]{1,0:T(8,128)(2,1)S(1)}, bf16[144,1024]{1,0:T(8,128)(2,1)}, bf16[144,1024]{1,0:T(8,128)(2,1)}, bf16[144,1024]{1,0:T(8,128)(2,1)}) custom-call(s32[5]{0:T(128)S(1)} %stack.122.meta_ref, bf16[128,1024]{1,0:T(8,128)(2,1)S(1)} %broadcast_select_fusion.1.refs_0_.a_ref, f32[1,1024]{1,0:T(1,128)S(1)} %copy-done.9, ...), custom_call_target="tpu_custom_call" | custom-call | flops 1073741824 | bytes 8388608 | tf_op jit(solution)/shard_map/pallas_call | solution.py:86
  103.4 86.2 %collective-permute-start.29 = (bf16[144,1024]{1,0:T(8,128)(2,1)S(1)}, bf16[144,1024]{1,0:T(8,128)(2,1)S(1)}, u32[]{:S(2)}, u32[]{:S(2)}) collective-permute-start(bf16[144,1024]{1,0:T(8,128)(2,1)S(1)} %get-tuple-element.201), channel_id=1, source_target_pairs={{16,18},{17,19},{18,16},{19,17},{20,22},{21,23},{22,20},{23,21},{2... | collective-permute-start | bytes 884744 | tf_op jit(solution)/shard_map/ppermute | solution.py:292
  189.6 7.0 %collective-permute-start.30 = (bf16[144,1024]{1,0:T(8,128)(2,1)S(1)}, bf16[144,1024]{1,0:T(8,128)(2,1)S(1)}, u32[]{:S(2)}, u32[]{:S(2)}) collective-permute-start(bf16[144,1024]{1,0:T(8,128)(2,1)S(1)} %get-tuple-element.202), channel_id=1, source_target_pairs={{16,19},{17,18},{18,17},{19,16},{20,23},{21,22},{22,21},{23,20},{2... | collective-permute-start | bytes 884744 | tf_op jit(solution)/shard_map/ppermute | solution.py:292
  199.1 6.9 %shard_map.72 = (f32[1024,128]{1,0:T(8,128)S(1)}, f32[8,128]{1,0:T(8,128)S(1)}) custom-call(s32[4]{0:T(128)S(1)} %pad_add_fusion.1.meta_ref, bf16[1024,8192]{1,0:T(8,128)(2,1)} %bitcast.63, bf16[144,1024]{1,0:T(8,128)(2,1)S(1)} %get-tuple-element.199.refs_0_, bf16[144,1024]{1,0:T(8,128)(2,1)S(1)} %collective-permute-done.28.refs_1_, ...), custom_call_target="tpu_custom_call" | custom-call | flops 1073741824 | bytes 8388608 | tf_op jit(solution)/shard_map/pallas_call | solution.py:223
  206.1 6.9 %shard_map.73 = (f32[1024,128]{1,0:T(8,128)S(1)}, f32[8,128]{1,0:T(8,128)S(1)}) custom-call(s32[4]{0:T(128)S(1)} %pad_add_fusion.2.meta_ref, bf16[1024,8192]{1,0:T(8,128)(2,1)} %bitcast.64, bf16[144,1024]{1,0:T(8,128)(2,1)S(1)} %collective-permute-done.31.refs_0_, bf16[144,1024]{1,0:T(8,128)(2,1)S(1)} %collective-permute-done.32.refs_1_, ...), custom_call_target="tpu_custom_call" | custom-call | flops 1073741824 | bytes 8388608 | tf_op jit(solution)/shard_map/pallas_call | solution.py:223
  220.4 4.3 %shard_map.78 = (f32[1024,128]{1,0:T(8,128)S(1)}, f32[8,128]{1,0:T(8,128)S(1)}) custom-call(s32[4]{0:T(128)S(1)} %pad_add_fusion.1.meta_ref, bf16[1024,8192]{1,0:T(8,128)(2,1)S(1)} %bitcast.67, bf16[144,1024]{1,0:T(8,128)(2,1)S(1)} %get-tuple-element.216.refs_0_, bf16[144,1024]{1,0:T(8,128)(2,1)S(1)} %collective-permute-done.36.refs_1_, ...), custom_call_target="tpu_custom_call" | custom-call | flops 1073741824 | bytes 8388608 | tf_op jit(solution)/shard_map/pallas_call | solution.py:223
  224.8 4.3 %shard_map.79 = (f32[1024,128]{1,0:T(8,128)S(1)}, f32[8,128]{1,0:T(8,128)S(1)}) custom-call(s32[4]{0:T(128)S(1)} %pad_add_fusion.2.meta_ref, bf16[1024,8192]{1,0:T(8,128)(2,1)S(1)} %bitcast.68, bf16[144,1024]{1,0:T(8,128)(2,1)S(1)} %collective-permute-done.39.refs_4_.refs_0_, bf16[144,1024]{1,0:T(8,128)(2,1)S(1)} %collective-permute-done.40.refs_1_, ...), custom_call_target="tpu_custom_call" | custom-call | flops 1073741824 | bytes 8388608 | tf_op jit(solution)/shard_map/pallas_call | solution.py:223
  230.8 33.1 %collective-permute-done.43.up_ref = bf16[128,1024]{1,0:T(8,128)(2,1)S(1)} collective-permute-done((bf16[128,1024]{1,0:T(8,128)(2,1)S(1)}, bf16[128,1024]{1,0:T(8,128)(2,1)S(1)}, u32[]{:S(2)}, u32[]{:S(2)}) %collective-permute-start.43) | collective-permute-done | bytes 262176 | tf_op jit(solution)/shard_map/ppermute | solution.py:292
  264.6 3.4 %collective-permute-start.47 = (bf16[144,1024]{1,0:T(8,128)(2,1)S(1)}, bf16[144,1024]{1,0:T(8,128)(2,1)S(1)}, u32[]{:S(2)}, u32[]{:S(2)}) collective-permute-start(bf16[144,1024]{1,0:T(8,128)(2,1)S(1)} %get-tuple-element.225.refs_0_), channel_id=1, source_target_pairs={{0,4},{1,5},{2,6},{3,7},{4,0},{5,1},{6,2},{7,3}} | collective-permute-start | bytes 884744 | tf_op jit(solution)/shard_map/ppermute | solution.py:292
  270.5 3.4 %collective-permute-start.45 = (bf16[144,1024]{1,0:T(8,128)(2,1)S(1)}, bf16[144,1024]{1,0:T(8,128)(2,1)S(1)}, u32[]{:S(2)}, u32[]{:S(2)}) collective-permute-start(bf16[144,1024]{1,0:T(8,128)(2,1)S(1)} %get-tuple-element.227), channel_id=1, source_target_pairs={{0,2},{1,3},{2,0},{3,1},{4,6},{5,7},{6,4},{7,5}} | collective-permute-start | bytes 884744 | tf_op jit(solution)/shard_map/ppermute | solution.py:292
  283.2 3.4 %collective-permute-start.50 = (bf16[144,1024]{1,0:T(8,128)(2,1)S(1)}, bf16[144,1024]{1,0:T(8,128)(2,1)S(1)}, u32[]{:S(2)}, u32[]{:S(2)}) collective-permute-start(bf16[144,1024]{1,0:T(8,128)(2,1)S(1)} %collective-permute-done.47.refs_0_), channel_id=1, source_target_pairs={{0,3},{1,2},{2,1},{3,0},{4,7},{5,6},{6,5},{7,4}} | collective-permute-start | bytes 884744 | tf_op jit(solution)/shard_map/ppermute | solution.py:292
  289.0 4.3 %shard_map.82 = (f32[1024,128]{1,0:T(8,128)S(1)}, f32[8,128]{1,0:T(8,128)S(1)}) custom-call(s32[4]{0:T(128)S(1)} %pad_add_fusion.1.meta_ref, bf16[1024,8192]{1,0:T(8,128)(2,1)S(1)} %bitcast.69, bf16[144,1024]{1,0:T(8,128)(2,1)S(1)} %get-tuple-element.225.refs_0_, bf16[144,1024]{1,0:T(8,128)(2,1)S(1)} %collective-permute-done.44.refs_1_, ...), custom_call_target="tpu_custom_call" | custom-call | flops 1073741824 | bytes 8388608 | tf_op jit(solution)/shard_map/pallas_call | solution.py:223
  293.3 4.3 %shard_map.83 = (f32[1024,128]{1,0:T(8,128)S(1)}, f32[8,128]{1,0:T(8,128)S(1)}) custom-call(s32[4]{0:T(128)S(1)} %pad_add_fusion.2.meta_ref, bf16[1024,8192]{1,0:T(8,128)(2,1)S(1)} %bitcast.70, bf16[144,1024]{1,0:T(8,128)(2,1)S(1)} %collective-permute-done.47.refs_0_, bf16[144,1024]{1,0:T(8,128)(2,1)S(1)} %collective-permute-done.48.refs_1_, ...), custom_call_target="tpu_custom_call" | custom-call | flops 1073741824 | bytes 8388608 | tf_op jit(solution)/shard_map/pallas_call | solution.py:223
  (164 shorter events, 68.9 us)
Async XLA Ops:
  8.5 24.1 %collective-permute-start.3 = (bf16[144,1024]{1,0:T(8,128)(2,1)S(1)}, bf16[144,1024]{1,0:T(8,128)(2,1)}, u32[]{:S(2)}, u32[]{:S(2)}) collective-permute-start(bf16[144,1024]{1,0:T(8,128)(2,1)S(1)} %get-tuple-element.164), channel_id=1, source_target_pairs={{0,1},{1,0},{2,3},{3,2},{4,5},{5,4},{6,7},{7,6},{24,25},{25,24},{2... | collective-permute-start | bytes 884744 | tf_op jit(solution)/shard_map/ppermute | solution.py:292
  13.3 21.2 %collective-permute-start.4 = (bf16[144,1024]{1,0:T(8,128)(2,1)S(1)}, bf16[144,1024]{1,0:T(8,128)(2,1)}, u32[]{:S(2)}, u32[]{:S(2)}) collective-permute-start(bf16[144,1024]{1,0:T(8,128)(2,1)S(1)} %get-tuple-element.165), channel_id=1, source_target_pairs={{0,2},{1,3},{2,0},{3,1},{4,6},{5,7},{6,4},{7,5},{24,26},{25,27},{2... | collective-permute-start | bytes 884744 | tf_op jit(solution)/shard_map/ppermute | solution.py:292
  16.8 17.7 %collective-permute-start.5 = (bf16[144,1024]{1,0:T(8,128)(2,1)S(1)}, bf16[144,1024]{1,0:T(8,128)(2,1)}, u32[]{:S(2)}, u32[]{:S(2)}) collective-permute-start(bf16[144,1024]{1,0:T(8,128)(2,1)S(1)} %get-tuple-element.166), channel_id=1, source_target_pairs={{0,3},{1,2},{2,1},{3,0},{4,7},{5,6},{6,5},{7,4},{24,27},{25,26},{2... | collective-permute-start | bytes 884744 | tf_op jit(solution)/shard_map/ppermute | solution.py:292
  25.3 15.5 %collective-permute-start = (bf16[144,1024]{1,0:T(8,128)(2,1)}, bf16[144,1024]{1,0:T(8,128)(2,1)S(1)}, u32[]{:S(2)}, u32[]{:S(2)}) collective-permute-start(bf16[144,1024]{1,0:T(8,128)(2,1)} %get-tuple-element.160), channel_id=1, source_target_pairs={{0,1},{1,0},{2,3},{3,2},{4,5},{5,4},{6,7},{7,6}} | collective-permute-start | bytes 884744 | tf_op jit(solution)/shard_map/ppermute | solution.py:292
  29.1 11.7 %collective-permute-start.1 = (bf16[144,1024]{1,0:T(8,128)(2,1)S(1)}, bf16[144,1024]{1,0:T(8,128)(2,1)S(1)}, u32[]{:S(2)}, u32[]{:S(2)}) collective-permute-start(bf16[144,1024]{1,0:T(8,128)(2,1)S(1)} %get-tuple-element.161), channel_id=1, source_target_pairs={{0,2},{1,3},{2,0},{3,1},{4,6},{5,7},{6,4},{7,5}} | collective-permute-start | bytes 884744 | tf_op jit(solution)/shard_map/ppermute | solution.py:292
  32.6 9.5 %collective-permute-start.2 = (bf16[144,1024]{1,0:T(8,128)(2,1)S(1)}, bf16[144,1024]{1,0:T(8,128)(2,1)S(1)}, u32[]{:S(2)}, u32[]{:S(2)}) collective-permute-start(bf16[144,1024]{1,0:T(8,128)(2,1)S(1)} %get-tuple-element.162), channel_id=1, source_target_pairs={{0,3},{1,2},{2,1},{3,0},{4,7},{5,6},{6,5},{7,4}} | collective-permute-start | bytes 884744 | tf_op jit(solution)/shard_map/ppermute | solution.py:292
  35.8 12.8 %collective-permute-start.6 = (bf16[144,1024]{1,0:T(8,128)(2,1)S(1)}, bf16[144,1024]{1,0:T(8,128)(2,1)S(1)}, u32[]{:S(2)}, u32[]{:S(2)}) collective-permute-start(bf16[144,1024]{1,0:T(8,128)(2,1)S(1)} %shard_map.61), channel_id=1, source_target_pairs={{0,4},{1,5},{2,6},{3,7},{4,0},{5,1},{6,2},{7,3},{24,28},{25,29},{2... | collective-permute-start | bytes 884744 | tf_op jit(solution)/shard_map/ppermute | solution.py:292
  58.0 10.6 %collective-permute-start.11 = (bf16[144,1024]{1,0:T(8,128)(2,1)S(1)}, bf16[144,1024]{1,0:T(8,128)(2,1)}, u32[]{:S(2)}, u32[]{:S(2)}) collective-permute-start(bf16[144,1024]{1,0:T(8,128)(2,1)S(1)} %get-tuple-element.173), channel_id=1, source_target_pairs={{8,9},{9,8},{10,11},{11,10},{12,13},{13,12},{14,15},{15,14},{24,25... | collective-permute-start | bytes 884744 | tf_op jit(solution)/shard_map/ppermute | solution.py:292
  59.4 9.9 %collective-permute-start.12 = (bf16[144,1024]{1,0:T(8,128)(2,1)S(1)}, bf16[144,1024]{1,0:T(8,128)(2,1)S(1)}, u32[]{:S(2)}, u32[]{:S(2)}) collective-permute-start(bf16[144,1024]{1,0:T(8,128)(2,1)S(1)} %get-tuple-element.174), channel_id=1, source_target_pairs={{8,10},{9,11},{10,8},{11,9},{12,14},{13,15},{14,12},{15,13},{24,26... | collective-permute-start | bytes 884744 | tf_op jit(solution)/shard_map/ppermute | solution.py:292
  80.4 10.1 %collective-permute-start.19 = (bf16[144,1024]{1,0:T(8,128)(2,1)S(1)}, bf16[144,1024]{1,0:T(8,128)(2,1)S(1)}, u32[]{:S(2)}, u32[]{:S(2)}) collective-permute-start(bf16[144,1024]{1,0:T(8,128)(2,1)S(1)} %get-tuple-element.185), channel_id=1, source_target_pairs={{16,17},{17,16},{18,19},{19,18},{20,21},{21,20},{22,23},{23,22}} | collective-permute-start | bytes 884744 | tf_op jit(solution)/shard_map/ppermute | solution.py:292
  81.1 10.1 %collective-permute-start.20 = (bf16[144,1024]{1,0:T(8,128)(2,1)S(1)}, bf16[144,1024]{1,0:T(8,128)(2,1)S(1)}, u32[]{:S(2)}, u32[]{:S(2)}) collective-permute-start(bf16[144,1024]{1,0:T(8,128)(2,1)S(1)} %get-tuple-element.186), channel_id=1, source_target_pairs={{16,18},{17,19},{18,16},{19,17},{20,22},{21,23},{22,20},{23,21}} | collective-permute-start | bytes 884744 | tf_op jit(solution)/shard_map/ppermute | solution.py:292
  81.8 9.4 %collective-permute-start.21 = (bf16[144,1024]{1,0:T(8,128)(2,1)S(1)}, bf16[144,1024]{1,0:T(8,128)(2,1)S(1)}, u32[]{:S(2)}, u32[]{:S(2)}) collective-permute-start(bf16[144,1024]{1,0:T(8,128)(2,1)S(1)} %get-tuple-element.187), channel_id=1, source_target_pairs={{16,19},{17,18},{18,17},{19,16},{20,23},{21,22},{22,21},{23,20}} | collective-permute-start | bytes 884744 | tf_op jit(solution)/shard_map/ppermute | solution.py:292
  102.0 94.6 %collective-permute-start.31 = (bf16[144,1024]{1,0:T(8,128)(2,1)S(1)}, bf16[144,1024]{1,0:T(8,128)(2,1)S(1)}, u32[]{:S(2)}, u32[]{:S(2)}) collective-permute-start(bf16[144,1024]{1,0:T(8,128)(2,1)S(1)} %get-tuple-element.199.refs_0_), channel_id=1, source_target_pairs={{16,20},{17,21},{18,22},{19,23},{20,16},{21,17},{22,18},{23,19}} | collective-permute-start | bytes 884744 | tf_op jit(solution)/shard_map/ppermute | solution.py:292
  102.7 95.3 %collective-permute-start.28 = (bf16[144,1024]{1,0:T(8,128)(2,1)S(1)}, bf16[144,1024]{1,0:T(8,128)(2,1)S(1)}, u32[]{:S(2)}, u32[]{:S(2)}) collective-permute-start(bf16[144,1024]{1,0:T(8,128)(2,1)S(1)} %get-tuple-element.200), channel_id=1, source_target_pairs={{16,17},{17,16},{18,19},{19,18},{20,21},{21,20},{22,23},{23,22},{2... | collective-permute-start | bytes 884744 | tf_op jit(solution)/shard_map/ppermute | solution.py:292
  103.4 95.7 %collective-permute-start.29 = (bf16[144,1024]{1,0:T(8,128)(2,1)S(1)}, bf16[144,1024]{1,0:T(8,128)(2,1)S(1)}, u32[]{:S(2)}, u32[]{:S(2)}) collective-permute-start(bf16[144,1024]{1,0:T(8,128)(2,1)S(1)} %get-tuple-element.201), channel_id=1, source_target_pairs={{16,18},{17,19},{18,16},{19,17},{20,22},{21,23},{22,20},{23,21},{2... | collective-permute-start | bytes 884744 | tf_op jit(solution)/shard_map/ppermute | solution.py:292
  189.6 9.5 %collective-permute-start.30 = (bf16[144,1024]{1,0:T(8,128)(2,1)S(1)}, bf16[144,1024]{1,0:T(8,128)(2,1)S(1)}, u32[]{:S(2)}, u32[]{:S(2)}) collective-permute-start(bf16[144,1024]{1,0:T(8,128)(2,1)S(1)} %get-tuple-element.202), channel_id=1, source_target_pairs={{16,19},{17,18},{18,17},{19,16},{20,23},{21,22},{22,21},{23,20},{2... | collective-permute-start | bytes 884744 | tf_op jit(solution)/shard_map/ppermute | solution.py:292
  229.5 34.4 %collective-permute-start.43 = (bf16[128,1024]{1,0:T(8,128)(2,1)S(1)}, bf16[128,1024]{1,0:T(8,128)(2,1)S(1)}, u32[]{:S(2)}, u32[]{:S(2)}) collective-permute-start(bf16[128,1024]{1,0:T(8,128)(2,1)S(1)} %get-tuple-element.224), channel_id=1, source_target_pairs={{8,0},{9,1},{10,2},{11,3},{12,4},{13,5},{14,6},{15,7}} | collective-permute-start | bytes 786440 | tf_op jit(solution)/shard_map/ppermute | solution.py:292
  264.6 12.8 %collective-permute-start.47 = (bf16[144,1024]{1,0:T(8,128)(2,1)S(1)}, bf16[144,1024]{1,0:T(8,128)(2,1)S(1)}, u32[]{:S(2)}, u32[]{:S(2)}) collective-permute-start(bf16[144,1024]{1,0:T(8,128)(2,1)S(1)} %get-tuple-element.225.refs_0_), channel_id=1, source_target_pairs={{0,4},{1,5},{2,6},{3,7},{4,0},{5,1},{6,2},{7,3}} | collective-permute-start | bytes 884744 | tf_op jit(solution)/shard_map/ppermute | solution.py:292
  268.1 15.2 %collective-permute-start.44 = (bf16[144,1024]{1,0:T(8,128)(2,1)S(1)}, bf16[144,1024]{1,0:T(8,128)(2,1)S(1)}, u32[]{:S(2)}, u32[]{:S(2)}) collective-permute-start(bf16[144,1024]{1,0:T(8,128)(2,1)S(1)} %get-tuple-element.226), channel_id=1, source_target_pairs={{0,1},{1,0},{2,3},{3,2},{4,5},{5,4},{6,7},{7,6}} | collective-permute-start | bytes 884744 | tf_op jit(solution)/shard_map/ppermute | solution.py:292
  270.5 18.4 %collective-permute-start.45 = (bf16[144,1024]{1,0:T(8,128)(2,1)S(1)}, bf16[144,1024]{1,0:T(8,128)(2,1)S(1)}, u32[]{:S(2)}, u32[]{:S(2)}) collective-permute-start(bf16[144,1024]{1,0:T(8,128)(2,1)S(1)} %get-tuple-element.227), channel_id=1, source_target_pairs={{0,2},{1,3},{2,0},{3,1},{4,6},{5,7},{6,4},{7,5}} | collective-permute-start | bytes 884744 | tf_op jit(solution)/shard_map/ppermute | solution.py:292
  274.0 15.0 %collective-permute-start.46 = (bf16[144,1024]{1,0:T(8,128)(2,1)S(1)}, bf16[144,1024]{1,0:T(8,128)(2,1)S(1)}, u32[]{:S(2)}, u32[]{:S(2)}) collective-permute-start(bf16[144,1024]{1,0:T(8,128)(2,1)S(1)} %get-tuple-element.228), channel_id=1, source_target_pairs={{0,3},{1,2},{2,1},{3,0},{4,7},{5,6},{6,5},{7,4}} | collective-permute-start | bytes 884744 | tf_op jit(solution)/shard_map/ppermute | solution.py:292
  277.4 15.9 %collective-permute-start.48 = (bf16[144,1024]{1,0:T(8,128)(2,1)S(1)}, bf16[144,1024]{1,0:T(8,128)(2,1)S(1)}, u32[]{:S(2)}, u32[]{:S(2)}) collective-permute-start(bf16[144,1024]{1,0:T(8,128)(2,1)S(1)} %collective-permute-done.47.refs_0_), channel_id=1, source_target_pairs={{0,1},{1,0},{2,3},{3,2},{4,5},{5,4},{6,7},{7,6}} | collective-permute-start | bytes 884744 | tf_op jit(solution)/shard_map/ppermute | solution.py:292
  279.8 13.5 %collective-permute-start.49 = (bf16[144,1024]{1,0:T(8,128)(2,1)S(1)}, bf16[144,1024]{1,0:T(8,128)(2,1)S(1)}, u32[]{:S(2)}, u32[]{:S(2)}) collective-permute-start(bf16[144,1024]{1,0:T(8,128)(2,1)S(1)} %collective-permute-done.47.refs_0_), channel_id=1, source_target_pairs={{0,2},{1,3},{2,0},{3,1},{4,6},{5,7},{6,4},{7,5}} | collective-permute-start | bytes 884744 | tf_op jit(solution)/shard_map/ppermute | solution.py:292
  283.2 10.1 %collective-permute-start.50 = (bf16[144,1024]{1,0:T(8,128)(2,1)S(1)}, bf16[144,1024]{1,0:T(8,128)(2,1)S(1)}, u32[]{:S(2)}, u32[]{:S(2)}) collective-permute-start(bf16[144,1024]{1,0:T(8,128)(2,1)S(1)} %collective-permute-done.47.refs_0_), channel_id=1, source_target_pairs={{0,3},{1,2},{2,1},{3,0},{4,7},{5,6},{6,5},{7,4}} | collective-permute-start | bytes 884744 | tf_op jit(solution)/shard_map/ppermute | solution.py:292
  (41 other events, 259.4 us)

commit v3 on v2

--- a/solution.py
+++ b/solution.py
@@ -47,57 +47,35 @@
 def forward_blocks(a, gain_row, w_rows, blocks, tail_row, other=None, use_other=None):
     rows, width = a.shape
     count = len(blocks)
+    tile = min(width, 512)
     with_other = other is not None
     meta = jnp.stack(blocks + [tail_row] + ([use_other] if with_other else []))
 
-    def kernel(meta_ref, *refs):
-        a_ref, gain_ref, w_ref = refs[:3]
-        other_ref = refs[3] if with_other else None
-        out_refs = refs[4 if with_other else 3 : -1]
-        scaled_ref = refs[-1]
-        step = pl.program_id(0)
-
-        @pl.when(step == 0)
-        def _():
-            wide = a_ref[...].astype(jnp.float32)
-            scaled_ref[...] = (wide * gain_ref[...]).astype(jnp.bfloat16)
-            line = as_line(jnp.sum(wide * wide, axis=1, keepdims=True))
-            for out_ref in out_refs:
-                store_tail(out_ref, rows, line, meta_ref[count])
-
-        partial = jnp.dot(scaled_ref[...], w_ref[...], preferred_element_type=jnp.float32)
-        for block in range(count):
-
-            @pl.when(step == block)
-            def _(block=block):
-                out_refs[block][:rows, :] = partial.astype(jnp.bfloat16)
-
+    def kernel(meta_ref, a_ref, gain_ref, w_ref, *refs):
+        other_ref = refs[0] if with_other else None
+        out_refs = refs[with_other:]
+        wide = a_ref[...].astype(jnp.float32)
+        scaled = (wide * gain_ref[...]).astype(jnp.bfloat16)
+        for block, out_ref in enumerate(out_refs):
+            for start in range(0, width, tile):
+                columns = pl.ds(pl.multiple_of(meta_ref[block] * width + start, tile), tile)
+                partial = jnp.dot(scaled, w_ref[:, columns], preferred_element_type=jnp.float32)
+                out_ref[:rows, start : start + tile] = partial.astype(jnp.bfloat16)
+        line = as_line(jnp.sum(wide * wide, axis=1, keepdims=True))
+        for out_ref in out_refs:
+            store_tail(out_ref, rows, line, meta_ref[count])
         if with_other:
 
-            @pl.when((step == count - 1) & (meta_ref[count + 1] == 1))
+            @pl.when(meta_ref[count + 1] == 1)
             def _():
                 for out_ref in out_refs:
                     out_ref[...] = other_ref[...]
 
-    def whole(shape):
-        return pl.BlockSpec(shape, lambda k, meta_ref: (0, 0))
-
-    chunk = (rows + TAIL, width)
-    return pl.pallas_call(
-        kernel,
-        out_shape=[jax.ShapeDtypeStruct(chunk, jnp.bfloat16)] * count,
-        grid_spec=pltpu.PrefetchScalarGridSpec(
-            num_scalar_prefetch=1,
-            grid=(count,),
-            in_specs=[
-                whole((rows, width)),
-                whole((1, width)),
-                pl.BlockSpec((width, width), lambda k, meta_ref: (0, meta_ref[k])),
-            ]
-            + [whole(chunk)] * with_other,
-            out_specs=[whole(chunk)] * count,
-            scratch_shapes=[pltpu.VMEM((rows, width), jnp.bfloat16)],
-        ),
+    return pl.pallas_call(
+        kernel,
+        out_shape=[jax.ShapeDtypeStruct((rows + TAIL, width), jnp.bfloat16)] * count,
+        in_specs=[SMEM_SPEC] + [VMEM_SPEC] * (3 + with_other),
+        out_specs=[VMEM_SPEC] * count,
         compiler_params=pltpu.CompilerParams(vmem_limit_bytes=VMEM_LIMIT),
         cost_estimate=matmul_cost(rows, width, count),
     )(meta, a, gain_row, w_rows, *([other] if with_other else []))
@@ -194,43 +172,32 @@
     rows = chunks[0].shape[0] - TAIL
     width = w_rows.shape[0]
     count = len(blocks)
+    tile = min(width, 256)
 
     def kernel(meta_ref, w_ref, *refs):
-        chunk_refs, (out_ref, sum_ref, held_ref) = refs[:count], refs[count:]
-        step = pl.program_id(0)
-        for block in range(count):
-
-            @pl.when(step == block)
-            def _(block=block):
-                held_ref[...] = chunk_refs[block][:rows, :]
-
-        product = lax.dot_general(
-            w_ref[...], held_ref[...], (((1,), (1,)), ((), ())), preferred_element_type=jnp.float32
-        )
-
-        @pl.when(step == 0)
-        def _():
-            out_ref[...] = product
-            sum_ref[...] = jnp.broadcast_to(tail_sum(chunk_refs, rows), (8, rows))
-
-        @pl.when(step > 0)
-        def _():
-            out_ref[...] += product
-
-    def whole(shape):
-        return pl.BlockSpec(shape, lambda k, meta_ref: (0, 0))
-
-    return pl.pallas_call(
-        kernel,
-        out_shape=[jax.ShapeDtypeStruct((width, rows), jnp.float32), jax.ShapeDtypeStruct((8, rows), jnp.float32)],
-        grid_spec=pltpu.PrefetchScalarGridSpec(
-            num_scalar_prefetch=1,
-            grid=(count,),
-            in_specs=[pl.BlockSpec((width, width), lambda k, meta_ref: (0, meta_ref[k]))]
-            + [whole((rows + TAIL, width))] * count,
-            out_specs=[whole((width, rows)), whole((8, rows))],
-            scratch_shapes=[pltpu.VMEM((rows, width), jnp.bfloat16)],
-        ),
+        chunk_refs, (out_ref, sum_ref) = refs[:count], refs[count:]
+        for start in range(0, width, tile):
+            total = None
+            for block, chunk in enumerate(chunk_refs):
+                columns = pl.ds(pl.multiple_of(meta_ref[block] * width, width), width)
+                product = lax.dot_general(
+                    w_ref[start : start + tile, columns],
+                    chunk[:rows, :],
+                    (((1,), (1,)), ((), ())),
+                    preferred_element_type=jnp.float32,
+                )
+                total = product if total is None else total + product
+            out_ref[start : start + tile, :] = total
+        sum_ref[...] = jnp.broadcast_to(tail_sum(chunk_refs, rows), (8, rows))
+
+    return pl.pallas_call(
+        kernel,
+        out_shape=[
+            jax.ShapeDtypeStruct((width, rows), jnp.float32),
+            jax.ShapeDtypeStruct((8, rows), jnp.float32),
+        ],
+        in_specs=[SMEM_SPEC] + [VMEM_SPEC] * (1 + count),
+        out_specs=[VMEM_SPEC] * 2,
         compiler_params=pltpu.CompilerParams(vmem_limit_bytes=VMEM_LIMIT),
         cost_estimate=matmul_cost(rows, width, count),
     )(jnp.stack(blocks), w_rows, *chunks)

time: 300 us -> 310 us (1.033)
  Pallas kernels: 80 us -> 85 us
    pallas_call x6, Pallas kernels: 36.6 us -> 44.8 us  [forward_blocks(): pl.pallas_call(kernel, out_shape=[jax.ShapeDtypeStruct((rows + TAIL, widt...]
    pallas_call x6, Pallas kernels: 31.1 us -> 27.9 us  [backward_blocks(): pl.pallas_call(kernel, out_shape=[jax.ShapeDtypeStruct((width, rows), jnp...]
  transfers between devices with their start and end apart: 51 -> 51, of which waited for: 5 -> 6; matrix products, arithmetic and copies ran while one was open for 0% -> 0% of each run, Pallas kernels for 13% -> 14%
where the time goes in v3:
time: 310 us; the launch traced here: 309 us
  starting transfers between devices  168 us (54%)
  Pallas kernels  85 us (27%)
  waiting for transfers between devices  44.4 us (14%)
  local copies, waits for them, and re-layouts  7.84 us (3%)
    ppermute x51, starting transfers between devices, send(): return lax.ppermute(value, ('section', 'tp'), pairs)  168 us
    pallas_call x6, Pallas kernels, forward_blocks(): pl.pallas_call(kernel, out_shape=[jax.ShapeDtypeStruct((rows + TAIL, widt...  44.8 us
    ppermute x51, waiting for transfers between devices, send(): return lax.ppermute(value, ('section', 'tp'), pairs)  44.4 us
    pallas_call x6, Pallas kernels, backward_blocks(): pl.pallas_call(kernel, out_shape=[jax.ShapeDtypeStruct((width, rows), jnp...  27.9 us
  transfers between devices with their start and end apart: 51, of which 6 were waited for; matrix products, arithmetic and copies ran while one was open for 0% of the time, Pallas kernels for 14%

profile of v3, /device:TPU:0, one launch (start us, length us, event | category | flops | bytes accessed | tf_op | source)
XLA Modules:
  0.0 308.7 jit_solution(15097234875288041331)
XLA Ops:
  2.8 7.1 %shard_map.60 = (bf16[144,1024]{1,0:T(8,128)(2,1)S(1)}, bf16[144,1024]{1,0:T(8,128)(2,1)S(1)}, bf16[144,1024]{1,0:T(8,128)(2,1)S(1)}, bf16[144,1024]{1,0:T(8,128)(2,1)S(1)}) custom-call(s32[6]{0:T(128)S(1)} %stack.127.meta_ref, bf16[128,1024]{1,0:T(8,128)(2,1)S(1)} %bitcast.52, f32[1,1024]{1,0:T(1,128)} %gain_ref.17, bf16[1024,8192]{1,0:T(8,128)(2,1)} %bitcast.55, ...), custom_call_target="tpu_custom_call" | custom-call | flops 1073741824 | bytes 8388608 | tf_op jit(solution)/shard_map/pallas_call | solution.py:74
  9.9 4.8 %collective-permute-start.3 = (bf16[144,1024]{1,0:T(8,128)(2,1)S(1)}, bf16[144,1024]{1,0:T(8,128)(2,1)}, u32[]{:S(2)}, u32[]{:S(2)}) collective-permute-start(bf16[144,1024]{1,0:T(8,128)(2,1)S(1)} %get-tuple-element.164), channel_id=1, source_target_pairs={{0,1},{1,0},{2,3},{3,2},{4,5},{5,4},{6,7},{7,6},{24,25},{25,24},{2... | collective-permute-start | bytes 884744 | tf_op jit(solution)/shard_map/ppermute | solution.py:259
  14.7 3.5 %collective-permute-start.4 = (bf16[144,1024]{1,0:T(8,128)(2,1)S(1)}, bf16[144,1024]{1,0:T(8,128)(2,1)}, u32[]{:S(2)}, u32[]{:S(2)}) collective-permute-start(bf16[144,1024]{1,0:T(8,128)(2,1)S(1)} %get-tuple-element.165), channel_id=1, source_target_pairs={{0,2},{1,3},{2,0},{3,1},{4,6},{5,7},{6,4},{7,5},{24,26},{25,27},{2... | collective-permute-start | bytes 884744 | tf_op jit(solution)/shard_map/ppermute | solution.py:259
  20.3 7.8 %shard_map.59 = (bf16[144,1024]{1,0:T(8,128)(2,1)S(1)}, bf16[144,1024]{1,0:T(8,128)(2,1)}, bf16[144,1024]{1,0:T(8,128)(2,1)S(1)}, bf16[144,1024]{1,0:T(8,128)(2,1)S(1)}) custom-call(s32[5]{0:T(128)S(1)} %stack.122.meta_ref, bf16[128,1024]{1,0:T(8,128)(2,1)S(1)} %bitcast.53, f32[1,1024]{1,0:T(1,128)S(1)} %copy-done.9, bf16[1024,8192]{1,0:T(8,128)(2,1)} %bitcast.56), custom_call_target="tpu_custom_call" | custom-call | flops 1073741824 | bytes 8388608 | tf_op jit(solution)/shard_map/pallas_call | solution.py:74
  28.0 3.8 %collective-permute-start = (bf16[144,1024]{1,0:T(8,128)(2,1)}, bf16[144,1024]{1,0:T(8,128)(2,1)S(1)}, u32[]{:S(2)}, u32[]{:S(2)}) collective-permute-start(bf16[144,1024]{1,0:T(8,128)(2,1)} %get-tuple-element.160), channel_id=1, source_target_pairs={{0,1},{1,0},{2,3},{3,2},{4,5},{5,4},{6,7},{7,6}} | collective-permute-start | bytes 884744 | tf_op jit(solution)/shard_map/ppermute | solution.py:259
  31.8 3.5 %collective-permute-start.1 = (bf16[144,1024]{1,0:T(8,128)(2,1)S(1)}, bf16[144,1024]{1,0:T(8,128)(2,1)S(1)}, u32[]{:S(2)}, u32[]{:S(2)}) collective-permute-start(bf16[144,1024]{1,0:T(8,128)(2,1)S(1)} %get-tuple-element.161), channel_id=1, source_target_pairs={{0,2},{1,3},{2,0},{3,1},{4,6},{5,7},{6,4},{7,5}} | collective-permute-start | bytes 884744 | tf_op jit(solution)/shard_map/ppermute | solution.py:259
  38.6 4.9 %collective-permute-start.6 = (bf16[144,1024]{1,0:T(8,128)(2,1)S(1)}, bf16[144,1024]{1,0:T(8,128)(2,1)S(1)}, u32[]{:S(2)}, u32[]{:S(2)}) collective-permute-start(bf16[144,1024]{1,0:T(8,128)(2,1)S(1)} %shard_map.61), channel_id=1, source_target_pairs={{0,4},{1,5},{2,6},{3,7},{4,0},{5,1},{6,2},{7,3},{24,28},{25,29},{2... | collective-permute-start | bytes 884744 | tf_op jit(solution)/shard_map/ppermute | solution.py:259
  44.9 6.5 %collective-permute-done.6.refs_4_.refs_0_ = bf16[144,1024]{1,0:T(8,128)(2,1)S(1)} collective-permute-done((bf16[144,1024]{1,0:T(8,128)(2,1)S(1)}, bf16[144,1024]{1,0:T(8,128)(2,1)S(1)}, u32[]{:S(2)}, u32[]{:S(2)}) %collective-permute-start.6) | collective-permute-done | bytes 294944 | tf_op jit(solution)/shard_map/ppermute | solution.py:259
  55.0 7.1 %shard_map.64 = (bf16[144,1024]{1,0:T(8,128)(2,1)S(1)}, bf16[144,1024]{1,0:T(8,128)(2,1)S(1)}, bf16[144,1024]{1,0:T(8,128)(2,1)S(1)}, bf16[144,1024]{1,0:T(8,128)(2,1)S(1)}) custom-call(s32[6]{0:T(128)S(1)} %stack.127.meta_ref, bf16[128,1024]{1,0:T(8,128)(2,1)S(1)} %broadcast_select_fusion.a_ref, f32[1,1024]{1,0:T(1,128)S(1)} %copy-done.9, ...), custom_call_target="tpu_custom_call" | custom-call | flops 1073741824 | bytes 8388608 | tf_op jit(solution)/shard_map/pallas_call | solution.py:74
  64.9 7.8 %shard_map.63 = (bf16[144,1024]{1,0:T(8,128)(2,1)S(1)}, bf16[144,1024]{1,0:T(8,128)(2,1)}, bf16[144,1024]{1,0:T(8,128)(2,1)S(1)}, bf16[144,1024]{1,0:T(8,128)(2,1)}) custom-call(s32[5]{0:T(128)S(1)} %stack.122.meta_ref, bf16[128,1024]{1,0:T(8,128)(2,1)S(1)} %broadcast_select_fusion.a_ref, f32[1,1024]{1,0:T(1,128)S(1)} %copy-done.9, bf16[1024,8192]{1,0:T(8,128)(2,1)} %bitcast.58), custom_call_target="tpu_custom_call" | custom-call | flops 1073741824 | bytes 8388608 | tf_op jit(solution)/shard_map/pallas_call | solution.py:74
  80.2 7.1 %shard_map.68 = (bf16[144,1024]{1,0:T(8,128)(2,1)S(1)}, bf16[144,1024]{1,0:T(8,128)(2,1)S(1)}, bf16[144,1024]{1,0:T(8,128)(2,1)S(1)}, bf16[144,1024]{1,0:T(8,128)(2,1)S(1)}) custom-call(s32[5]{0:T(128)S(1)} %stack.128.meta_ref, bf16[128,1024]{1,0:T(8,128)(2,1)S(1)} %broadcast_select_fusion.1.a_ref, f32[1,1024]{1,0:T(1,128)S(1)} %copy-done.9, ...), custom_call_target="tpu_custom_call" | custom-call | flops 1073741824 | bytes 8388608 | tf_op jit(solution)/shard_map/pallas_call | solution.py:74
  89.3 7.9 %shard_map.67 = (bf16[144,1024]{1,0:T(8,128)(2,1)S(1)}, bf16[144,1024]{1,0:T(8,128)(2,1)}, bf16[144,1024]{1,0:T(8,128)(2,1)}, bf16[144,1024]{1,0:T(8,128)(2,1)}) custom-call(s32[5]{0:T(128)S(1)} %stack.122.meta_ref, bf16[128,1024]{1,0:T(8,128)(2,1)S(1)} %broadcast_select_fusion.1.a_ref, f32[1,1024]{1,0:T(1,128)S(1)} %copy-done.9, bf16[1024,8192]{1,0:T(8,128)(2,1)} %bitcast.60), custom_call_target="tpu_custom_call" | custom-call | flops 1073741824 | bytes 8388608 | tf_op jit(solution)/shard_map/pallas_call | solution.py:74
  106.5 3.1 %conditional.3 = (bf16[144,1024]{1,0:T(8,128)(2,1)S(1)}, bf16[144,1024]{1,0:T(8,128)(2,1)S(1)}, bf16[144,1024]{1,0:T(8,128)(2,1)S(1)}, bf16[144,1024]{1,0:T(8,12...) conditional(s32[]{:T(128)} %convert_element_type.71, () %tuple.23, ...), branch_computations={%region_4.5_spmd, %region_5.6_spmd} | conditional | flops 2147483648 | bytes 16777360 | solution.py:340
  111.8 88.8 %collective-permute-start.29 = (bf16[144,1024]{1,0:T(8,128)(2,1)S(1)}, bf16[144,1024]{1,0:T(8,128)(2,1)S(1)}, u32[]{:S(2)}, u32[]{:S(2)}) collective-permute-start(bf16[144,1024]{1,0:T(8,128)(2,1)S(1)} %get-tuple-element.201), channel_id=1, source_target_pairs={{16,18},{17,19},{18,16},{19,17},{20,22},{21,23},{22,20},{23,21},{2... | collective-permute-start | bytes 884744 | tf_op jit(solution)/shard_map/ppermute | solution.py:259
  200.5 7.0 %collective-permute-start.30 = (bf16[144,1024]{1,0:T(8,128)(2,1)S(1)}, bf16[144,1024]{1,0:T(8,128)(2,1)S(1)}, u32[]{:S(2)}, u32[]{:S(2)}) collective-permute-start(bf16[144,1024]{1,0:T(8,128)(2,1)S(1)} %get-tuple-element.202), channel_id=1, source_target_pairs={{16,19},{17,18},{18,17},{19,16},{20,23},{21,22},{22,21},{23,20},{2... | collective-permute-start | bytes 884744 | tf_op jit(solution)/shard_map/ppermute | solution.py:259
  209.8 8.2 %shard_map.72 = (f32[1024,128]{1,0:T(8,128)S(1)}, f32[8,128]{1,0:T(8,128)S(1)}) custom-call(s32[4]{0:T(128)S(1)} %pad_add_fusion.1.meta_ref, bf16[1024,8192]{1,0:T(8,128)(2,1)} %bitcast.63, bf16[144,1024]{1,0:T(8,128)(2,1)S(1)} %get-tuple-element.199.refs_0_, bf16[144,1024]{1,0:T(8,128)(2,1)S(1)} %collective-permute-done.28.refs_1_, ...), custom_call_target="tpu_custom_call" | custom-call | flops 1073741824 | bytes 8388608 | tf_op jit(solution)/shard_map/pallas_call | solution.py:193
  218.1 8.2 %shard_map.73 = (f32[1024,128]{1,0:T(8,128)S(1)}, f32[8,128]{1,0:T(8,128)S(1)}) custom-call(s32[4]{0:T(128)S(1)} %pad_add_fusion.2.meta_ref, bf16[1024,8192]{1,0:T(8,128)(2,1)} %bitcast.64, bf16[144,1024]{1,0:T(8,128)(2,1)S(1)} %collective-permute-done.31.refs_0_, bf16[144,1024]{1,0:T(8,128)(2,1)S(1)} %collective-permute-done.32.refs_1_, ...), custom_call_target="tpu_custom_call" | custom-call | flops 1073741824 | bytes 8388608 | tf_op jit(solution)/shard_map/pallas_call | solution.py:193
  234.1 2.9 shard_map.78
  241.5 34.4 %collective-permute-done.43.up_ref = bf16[128,1024]{1,0:T(8,128)(2,1)S(1)} collective-permute-done((bf16[128,1024]{1,0:T(8,128)(2,1)S(1)}, bf16[128,1024]{1,0:T(8,128)(2,1)S(1)}, u32[]{:S(2)}, u32[]{:S(2)}) %collective-permute-start.43) | collective-permute-done | bytes 262176 | tf_op jit(solution)/shard_map/ppermute | solution.py:259
  276.6 3.4 %collective-permute-start.47 = (bf16[144,1024]{1,0:T(8,128)(2,1)S(1)}, bf16[144,1024]{1,0:T(8,128)(2,1)S(1)}, u32[]{:S(2)}, u32[]{:S(2)}) collective-permute-start(bf16[144,1024]{1,0:T(8,128)(2,1)S(1)} %get-tuple-element.225.refs_0_), channel_id=1, source_target_pairs={{0,4},{1,5},{2,6},{3,7},{4,0},{5,1},{6,2},{7,3}} | collective-permute-start | bytes 884744 | tf_op jit(solution)/shard_map/ppermute | solution.py:259
  282.6 3.4 %collective-permute-start.45 = (bf16[144,1024]{1,0:T(8,128)(2,1)S(1)}, bf16[144,1024]{1,0:T(8,128)(2,1)S(1)}, u32[]{:S(2)}, u32[]{:S(2)}) collective-permute-start(bf16[144,1024]{1,0:T(8,128)(2,1)S(1)} %get-tuple-element.227), channel_id=1, source_target_pairs={{0,2},{1,3},{2,0},{3,1},{4,6},{5,7},{6,4},{7,5}} | collective-permute-start | bytes 884744 | tf_op jit(solution)/shard_map/ppermute | solution.py:259
  285.9 3.3 %collective-permute-start.46 = (bf16[144,1024]{1,0:T(8,128)(2,1)S(1)}, bf16[144,1024]{1,0:T(8,128)(2,1)S(1)}, u32[]{:S(2)}, u32[]{:S(2)}) collective-permute-start(bf16[144,1024]{1,0:T(8,128)(2,1)S(1)} %get-tuple-element.228), channel_id=1, source_target_pairs={{0,3},{1,2},{2,1},{3,0},{4,7},{5,6},{6,5},{7,4}} | collective-permute-start | bytes 884744 | tf_op jit(solution)/shard_map/ppermute | solution.py:259
  291.8 3.4 %collective-permute-start.49 = (bf16[144,1024]{1,0:T(8,128)(2,1)S(1)}, bf16[144,1024]{1,0:T(8,128)(2,1)S(1)}, u32[]{:S(2)}, u32[]{:S(2)}) collective-permute-start(bf16[144,1024]{1,0:T(8,128)(2,1)S(1)} %collective-permute-done.47.refs_0_), channel_id=1, source_target_pairs={{0,2},{1,3},{2,0},{3,1},{4,6},{5,7},{6,4},{7,5}} | collective-permute-start | bytes 884744 | tf_op jit(solution)/shard_map/ppermute | solution.py:259
  295.2 3.4 %collective-permute-start.50 = (bf16[144,1024]{1,0:T(8,128)(2,1)S(1)}, bf16[144,1024]{1,0:T(8,128)(2,1)S(1)}, u32[]{:S(2)}, u32[]{:S(2)}) collective-permute-start(bf16[144,1024]{1,0:T(8,128)(2,1)S(1)} %collective-permute-done.47.refs_0_), channel_id=1, source_target_pairs={{0,3},{1,2},{2,1},{3,0},{4,7},{5,6},{6,5},{7,4}} | collective-permute-start | bytes 884744 | tf_op jit(solution)/shard_map/ppermute | solution.py:259
  (164 shorter events, 68.8 us)
Async XLA Ops:
  9.9 25.5 %collective-permute-start.3 = (bf16[144,1024]{1,0:T(8,128)(2,1)S(1)}, bf16[144,1024]{1,0:T(8,128)(2,1)}, u32[]{:S(2)}, u32[]{:S(2)}) collective-permute-start(bf16[144,1024]{1,0:T(8,128)(2,1)S(1)} %get-tuple-element.164), channel_id=1, source_target_pairs={{0,1},{1,0},{2,3},{3,2},{4,5},{5,4},{6,7},{7,6},{24,25},{25,24},{2... | collective-permute-start | bytes 884744 | tf_op jit(solution)/shard_map/ppermute | solution.py:259
  14.7 22.6 %collective-permute-start.4 = (bf16[144,1024]{1,0:T(8,128)(2,1)S(1)}, bf16[144,1024]{1,0:T(8,128)(2,1)}, u32[]{:S(2)}, u32[]{:S(2)}) collective-permute-start(bf16[144,1024]{1,0:T(8,128)(2,1)S(1)} %get-tuple-element.165), channel_id=1, source_target_pairs={{0,2},{1,3},{2,0},{3,1},{4,6},{5,7},{6,4},{7,5},{24,26},{25,27},{2... | collective-permute-start | bytes 884744 | tf_op jit(solution)/shard_map/ppermute | solution.py:259
  18.2 19.1 %collective-permute-start.5 = (bf16[144,1024]{1,0:T(8,128)(2,1)S(1)}, bf16[144,1024]{1,0:T(8,128)(2,1)}, u32[]{:S(2)}, u32[]{:S(2)}) collective-permute-start(bf16[144,1024]{1,0:T(8,128)(2,1)S(1)} %get-tuple-element.166), channel_id=1, source_target_pairs={{0,3},{1,2},{2,1},{3,0},{4,7},{5,6},{6,5},{7,4},{24,27},{25,26},{2... | collective-permute-start | bytes 884744 | tf_op jit(solution)/shard_map/ppermute | solution.py:259
  28.0 15.5 %collective-permute-start = (bf16[144,1024]{1,0:T(8,128)(2,1)}, bf16[144,1024]{1,0:T(8,128)(2,1)S(1)}, u32[]{:S(2)}, u32[]{:S(2)}) collective-permute-start(bf16[144,1024]{1,0:T(8,128)(2,1)} %get-tuple-element.160), channel_id=1, source_target_pairs={{0,1},{1,0},{2,3},{3,2},{4,5},{5,4},{6,7},{7,6}} | collective-permute-start | bytes 884744 | tf_op jit(solution)/shard_map/ppermute | solution.py:259
  31.8 11.7 %collective-permute-start.1 = (bf16[144,1024]{1,0:T(8,128)(2,1)S(1)}, bf16[144,1024]{1,0:T(8,128)(2,1)S(1)}, u32[]{:S(2)}, u32[]{:S(2)}) collective-permute-start(bf16[144,1024]{1,0:T(8,128)(2,1)S(1)} %get-tuple-element.161), channel_id=1, source_target_pairs={{0,2},{1,3},{2,0},{3,1},{4,6},{5,7},{6,4},{7,5}} | collective-permute-start | bytes 884744 | tf_op jit(solution)/shard_map/ppermute | solution.py:259
  38.6 12.8 %collective-permute-start.6 = (bf16[144,1024]{1,0:T(8,128)(2,1)S(1)}, bf16[144,1024]{1,0:T(8,128)(2,1)S(1)}, u32[]{:S(2)}, u32[]{:S(2)}) collective-permute-start(bf16[144,1024]{1,0:T(8,128)(2,1)S(1)} %shard_map.61), channel_id=1, source_target_pairs={{0,4},{1,5},{2,6},{3,7},{4,0},{5,1},{6,2},{7,3},{24,28},{25,29},{2... | collective-permute-start | bytes 884744 | tf_op jit(solution)/shard_map/ppermute | solution.py:259
  62.1 12.0 %collective-permute-start.11 = (bf16[144,1024]{1,0:T(8,128)(2,1)S(1)}, bf16[144,1024]{1,0:T(8,128)(2,1)}, u32[]{:S(2)}, u32[]{:S(2)}) collective-permute-start(bf16[144,1024]{1,0:T(8,128)(2,1)S(1)} %get-tuple-element.173), channel_id=1, source_target_pairs={{8,9},{9,8},{10,11},{11,10},{12,13},{13,12},{14,15},{15,14},{24,25... | collective-permute-start | bytes 884744 | tf_op jit(solution)/shard_map/ppermute | solution.py:259
  63.5 11.3 %collective-permute-start.12 = (bf16[144,1024]{1,0:T(8,128)(2,1)S(1)}, bf16[144,1024]{1,0:T(8,128)(2,1)S(1)}, u32[]{:S(2)}, u32[]{:S(2)}) collective-permute-start(bf16[144,1024]{1,0:T(8,128)(2,1)S(1)} %get-tuple-element.174), channel_id=1, source_target_pairs={{8,10},{9,11},{10,8},{11,9},{12,14},{13,15},{14,12},{15,13},{24,26... | collective-permute-start | bytes 884744 | tf_op jit(solution)/shard_map/ppermute | solution.py:259
  64.2 10.6 %collective-permute-start.13 = (bf16[144,1024]{1,0:T(8,128)(2,1)S(1)}, bf16[144,1024]{1,0:T(8,128)(2,1)S(1)}, u32[]{:S(2)}, u32[]{:S(2)}) collective-permute-start(bf16[144,1024]{1,0:T(8,128)(2,1)S(1)} %get-tuple-element.175), channel_id=1, source_target_pairs={{8,11},{9,10},{10,9},{11,8},{12,15},{13,14},{14,13},{15,12},{24,27... | collective-permute-start | bytes 884744 | tf_op jit(solution)/shard_map/ppermute | solution.py:259
  87.3 11.4 %collective-permute-start.19 = (bf16[144,1024]{1,0:T(8,128)(2,1)S(1)}, bf16[144,1024]{1,0:T(8,128)(2,1)S(1)}, u32[]{:S(2)}, u32[]{:S(2)}) collective-permute-start(bf16[144,1024]{1,0:T(8,128)(2,1)S(1)} %get-tuple-element.185), channel_id=1, source_target_pairs={{16,17},{17,16},{18,19},{19,18},{20,21},{21,20},{22,23},{23,22}} | collective-permute-start | bytes 884744 | tf_op jit(solution)/shard_map/ppermute | solution.py:259
  88.0 11.4 %collective-permute-start.20 = (bf16[144,1024]{1,0:T(8,128)(2,1)S(1)}, bf16[144,1024]{1,0:T(8,128)(2,1)S(1)}, u32[]{:S(2)}, u32[]{:S(2)}) collective-permute-start(bf16[144,1024]{1,0:T(8,128)(2,1)S(1)} %get-tuple-element.186), channel_id=1, source_target_pairs={{16,18},{17,19},{18,16},{19,17},{20,22},{21,23},{22,20},{23,21}} | collective-permute-start | bytes 884744 | tf_op jit(solution)/shard_map/ppermute | solution.py:259
  88.7 10.7 %collective-permute-start.21 = (bf16[144,1024]{1,0:T(8,128)(2,1)S(1)}, bf16[144,1024]{1,0:T(8,128)(2,1)S(1)}, u32[]{:S(2)}, u32[]{:S(2)}) collective-permute-start(bf16[144,1024]{1,0:T(8,128)(2,1)S(1)} %get-tuple-element.187), channel_id=1, source_target_pairs={{16,19},{17,18},{18,17},{19,16},{20,23},{21,22},{22,21},{23,20}} | collective-permute-start | bytes 884744 | tf_op jit(solution)/shard_map/ppermute | solution.py:259
  110.4 97.1 %collective-permute-start.31 = (bf16[144,1024]{1,0:T(8,128)(2,1)S(1)}, bf16[144,1024]{1,0:T(8,128)(2,1)S(1)}, u32[]{:S(2)}, u32[]{:S(2)}) collective-permute-start(bf16[144,1024]{1,0:T(8,128)(2,1)S(1)} %get-tuple-element.199.refs_0_), channel_id=1, source_target_pairs={{16,20},{17,21},{18,22},{19,23},{20,16},{21,17},{22,18},{23,19}} | collective-permute-start | bytes 884744 | tf_op jit(solution)/shard_map/ppermute | solution.py:259
  111.1 97.9 %collective-permute-start.28 = (bf16[144,1024]{1,0:T(8,128)(2,1)S(1)}, bf16[144,1024]{1,0:T(8,128)(2,1)S(1)}, u32[]{:S(2)}, u32[]{:S(2)}) collective-permute-start(bf16[144,1024]{1,0:T(8,128)(2,1)S(1)} %get-tuple-element.200), channel_id=1, source_target_pairs={{16,17},{17,16},{18,19},{19,18},{20,21},{21,20},{22,23},{23,22},{2... | collective-permute-start | bytes 884744 | tf_op jit(solution)/shard_map/ppermute | solution.py:259
  111.8 98.0 %collective-permute-start.29 = (bf16[144,1024]{1,0:T(8,128)(2,1)S(1)}, bf16[144,1024]{1,0:T(8,128)(2,1)S(1)}, u32[]{:S(2)}, u32[]{:S(2)}) collective-permute-start(bf16[144,1024]{1,0:T(8,128)(2,1)S(1)} %get-tuple-element.201), channel_id=1, source_target_pairs={{16,18},{17,19},{18,16},{19,17},{20,22},{21,23},{22,20},{23,21},{2... | collective-permute-start | bytes 884744 | tf_op jit(solution)/shard_map/ppermute | solution.py:259
  207.6 10.5 %collective-permute-start.32 = (bf16[144,1024]{1,0:T(8,128)(2,1)S(1)}, bf16[144,1024]{1,0:T(8,128)(2,1)S(1)}, u32[]{:S(2)}, u32[]{:S(2)}) collective-permute-start(bf16[144,1024]{1,0:T(8,128)(2,1)S(1)} %collective-permute-done.31.refs_0_), channel_id=1, source_target_pairs={{16,17},{17,16},{18,19},{19,18},{20,21},{21,20},{22,23},{23,22}} | collective-permute-start | bytes 884744 | tf_op jit(solution)/shard_map/ppermute | solution.py:259
  208.2 9.8 %collective-permute-start.33 = (bf16[144,1024]{1,0:T(8,128)(2,1)S(1)}, bf16[144,1024]{1,0:T(8,128)(2,1)S(1)}, u32[]{:S(2)}, u32[]{:S(2)}) collective-permute-start(bf16[144,1024]{1,0:T(8,128)(2,1)S(1)} %collective-permute-done.31.refs_0_), channel_id=1, source_target_pairs={{16,18},{17,19},{18,16},{19,17},{20,22},{21,23},{22,20},{23,21}} | collective-permute-start | bytes 884744 | tf_op jit(solution)/shard_map/ppermute | solution.py:259
  240.2 35.7 %collective-permute-start.43 = (bf16[128,1024]{1,0:T(8,128)(2,1)S(1)}, bf16[128,1024]{1,0:T(8,128)(2,1)S(1)}, u32[]{:S(2)}, u32[]{:S(2)}) collective-permute-start(bf16[128,1024]{1,0:T(8,128)(2,1)S(1)} %get-tuple-element.224), channel_id=1, source_target_pairs={{8,0},{9,1},{10,2},{11,3},{12,4},{13,5},{14,6},{15,7}} | collective-permute-start | bytes 786440 | tf_op jit(solution)/shard_map/ppermute | solution.py:259
  276.6 12.8 %collective-permute-start.47 = (bf16[144,1024]{1,0:T(8,128)(2,1)S(1)}, bf16[144,1024]{1,0:T(8,128)(2,1)S(1)}, u32[]{:S(2)}, u32[]{:S(2)}) collective-permute-start(bf16[144,1024]{1,0:T(8,128)(2,1)S(1)} %get-tuple-element.225.refs_0_), channel_id=1, source_target_pairs={{0,4},{1,5},{2,6},{3,7},{4,0},{5,1},{6,2},{7,3}} | collective-permute-start | bytes 884744 | tf_op jit(solution)/shard_map/ppermute | solution.py:259
  280.0 15.2 %collective-permute-start.44 = (bf16[144,1024]{1,0:T(8,128)(2,1)S(1)}, bf16[144,1024]{1,0:T(8,128)(2,1)S(1)}, u32[]{:S(2)}, u32[]{:S(2)}) collective-permute-start(bf16[144,1024]{1,0:T(8,128)(2,1)S(1)} %get-tuple-element.226), channel_id=1, source_target_pairs={{0,1},{1,0},{2,3},{3,2},{4,5},{5,4},{6,7},{7,6}} | collective-permute-start | bytes 884744 | tf_op jit(solution)/shard_map/ppermute | solution.py:259
  282.6 18.4 %collective-permute-start.45 = (bf16[144,1024]{1,0:T(8,128)(2,1)S(1)}, bf16[144,1024]{1,0:T(8,128)(2,1)S(1)}, u32[]{:S(2)}, u32[]{:S(2)}) collective-permute-start(bf16[144,1024]{1,0:T(8,128)(2,1)S(1)} %get-tuple-element.227), channel_id=1, source_target_pairs={{0,2},{1,3},{2,0},{3,1},{4,6},{5,7},{6,4},{7,5}} | collective-permute-start | bytes 884744 | tf_op jit(solution)/shard_map/ppermute | solution.py:259
  285.9 15.0 %collective-permute-start.46 = (bf16[144,1024]{1,0:T(8,128)(2,1)S(1)}, bf16[144,1024]{1,0:T(8,128)(2,1)S(1)}, u32[]{:S(2)}, u32[]{:S(2)}) collective-permute-start(bf16[144,1024]{1,0:T(8,128)(2,1)S(1)} %get-tuple-element.228), channel_id=1, source_target_pairs={{0,3},{1,2},{2,1},{3,0},{4,7},{5,6},{6,5},{7,4}} | collective-permute-start | bytes 884744 | tf_op jit(solution)/shard_map/ppermute | solution.py:259
  289.4 14.4 %collective-permute-start.48 = (bf16[144,1024]{1,0:T(8,128)(2,1)S(1)}, bf16[144,1024]{1,0:T(8,128)(2,1)S(1)}, u32[]{:S(2)}, u32[]{:S(2)}) collective-permute-start(bf16[144,1024]{1,0:T(8,128)(2,1)S(1)} %collective-permute-done.47.refs_0_), channel_id=1, source_target_pairs={{0,1},{1,0},{2,3},{3,2},{4,5},{5,4},{6,7},{7,6}} | collective-permute-start | bytes 884744 | tf_op jit(solution)/shard_map/ppermute | solution.py:259
  291.8 12.0 %collective-permute-start.49 = (bf16[144,1024]{1,0:T(8,128)(2,1)S(1)}, bf16[144,1024]{1,0:T(8,128)(2,1)S(1)}, u32[]{:S(2)}, u32[]{:S(2)}) collective-permute-start(bf16[144,1024]{1,0:T(8,128)(2,1)S(1)} %collective-permute-done.47.refs_0_), channel_id=1, source_target_pairs={{0,2},{1,3},{2,0},{3,1},{4,6},{5,7},{6,4},{7,5}} | collective-permute-start | bytes 884744 | tf_op jit(solution)/shard_map/ppermute | solution.py:259
  (41 other events, 275.6 us)

commit v4 on v3

v4 whole, which is shorter than its diff:
```python
import jax
import jax.numpy as jnp
from jax import lax
from jax.experimental import pallas as pl
from jax.experimental.pallas import tpu as pltpu
from jax.sharding import PartitionSpec as P

EPSILON = 1e-05
MIB = 1 << 20
TAIL = 16
LANES = 128
VMEM_LIMIT = 20 * MIB
SMEM_SPEC = pl.BlockSpec(memory_space=pltpu.SMEM)
VMEM_SPEC = pl.BlockSpec(memory_space=pltpu.VMEM)


def as_line(column):
    return jnp.broadcast_to(column, (column.shape[0], LANES)).T[:1]


def as_column(line):
    return jnp.broadcast_to(line, (LANES, line.shape[1])).T[:, :1]


def store_tail(out_ref, rows, line, row_no):
    row_ids = lax.broadcasted_iota(jnp.int32, (TAIL, rows), 0)
    tile = jnp.where(row_ids == row_no, jnp.broadcast_to(line, (TAIL, rows)), 0.0)
    out_ref[rows : rows + TAIL, :] = jnp.zeros((TAIL, out_ref.shape[1]), out_ref.dtype)
    out_ref[rows : rows + TAIL, :rows] = tile.astype(out_ref.dtype)


def tail_sum(chunk_refs, rows):
    total = chunk_refs[0][rows : rows + TAIL, :rows].astype(jnp.float32)
    for chunk in chunk_refs[1:]:
        total = total + chunk[rows : rows + TAIL, :rows].astype(jnp.float32)
    return jnp.sum(total, axis=0, keepdims=True)


def matmul_cost(rows, width, count):
    return pl.CostEstimate(
        flops=2 * rows * width * width * count,
        bytes_accessed=2 * width * width * count,
        transcendentals=0,
    )


def forward_blocks(a, gain_row, w_rows, blocks, tail_row, other=None, use_other=None, pack=None):
    rows, width = a.shape
    chunk_rows = rows + TAIL
    count = len(blocks)
    tile = min(width, 512)
    extras = [x for x in (other, pack) if x is not None]
    meta = jnp.stack(blocks + [tail_row] + ([use_other] if other is not None else []))

    def kernel(meta_ref, a_ref, gain_ref, w_ref, *refs):
        out_refs = refs[len(extras) :]
        wide = a_ref[...].astype(jnp.float32)
        scaled = (wide * gain_ref[...]).astype(jnp.bfloat16)
        for block, out_ref in enumerate(out_refs):
            for start in range(0, width, tile):
                columns = pl.ds(pl.multiple_of(meta_ref[block] * width + start, tile), tile)
                partial = jnp.dot(scaled, w_ref[:, columns], preferred_element_type=jnp.float32)
                out_ref[:rows, start : start + tile] = partial.astype(jnp.bfloat16)
        line = as_line(jnp.sum(wide * wide, axis=1, keepdims=True))
        for out_ref in out_refs:
            store_tail(out_ref, rows, line, meta_ref[count])
        if pack is not None:
            out_refs[0][chunk_rows : chunk_rows + rows, :] = a_ref[...]
            out_refs[0][chunk_rows + rows :, :] = refs[len(extras) - 1][...]
        if other is not None:

            @pl.when(meta_ref[count + 1] == 1)
            def _():
                for out_ref in out_refs:
                    out_ref[...] = refs[0][...]

    shapes = [(chunk_rows, width)] * count
    if pack is not None:
        shapes[0] = (2 * chunk_rows + rows, width)
    return pl.pallas_call(
        kernel,
        out_shape=[jax.ShapeDtypeStruct(shape, jnp.bfloat16) for shape in shapes],
        in_specs=[SMEM_SPEC] + [VMEM_SPEC] * (3 + len(extras)),
        out_specs=[VMEM_SPEC] * count,
        compiler_params=pltpu.CompilerParams(vmem_limit_bytes=VMEM_LIMIT),
        cost_estimate=matmul_cost(rows, width, count),
    )(meta, a, gain_row, w_rows, *extras)


def add_chunks(first, first_row, chunks, other=None, use_other=None):
    shape = chunks[0].shape

    def kernel(meta_ref, first_ref, *refs):
        total = first_ref[first_row : first_row + shape[0], :].astype(jnp.float32)
        for chunk in refs[: len(chunks)]:
            total = total + chunk[...].astype(jnp.float32)
        refs[-1][...] = total.astype(jnp.bfloat16)
        if other is not None:

            @pl.when(meta_ref[0] == 1)
            def _():
                refs[-1][...] = refs[len(chunks)][...]

    operands = [first] + chunks + ([other] if other is not None else [])
    meta = jnp.stack([use_other if other is not None else jnp.int32(0)])
    return pl.pallas_call(
        kernel,
        out_shape=jax.ShapeDtypeStruct(shape, jnp.bfloat16),
        in_specs=[SMEM_SPEC] + [VMEM_SPEC] * len(operands),
        out_specs=VMEM_SPEC,
        compiler_params=pltpu.CompilerParams(vmem_limit_bytes=VMEM_LIMIT),
    )(meta, *operands)


def finish_forward(first, chunks, a, full_width, kept, keep):
    chunk_rows, width = chunks[0].shape
    rows = chunk_rows - TAIL
    given = [] if a is None else [a]

    def kernel(meta_ref, first_ref, *refs):
        chunk_refs, rest = refs[: len(chunks)], refs[len(chunks) + len(given) :]
        old_refs, (out_ref, *new_refs) = rest[:3], rest[3:]
        source = first_ref[chunk_rows : chunk_rows + rows, :] if a is None else refs[len(chunks)][...]
        branch = first_ref[:rows, :].astype(jnp.float32)
        for chunk in chunk_refs:
            branch = branch + chunk[:rows, :].astype(jnp.float32)
        squares = as_column(tail_sum((first_ref,) + chunk_refs, rows))
        inv_rms = lax.rsqrt(squares / full_width + EPSILON)
        out_ref[...] = (source.astype(jnp.float32) + inv_rms * branch).astype(jnp.bfloat16)
        held = meta_ref[0] == 1

        @pl.when(held)
        def _():
            new_refs[0][...] = out_ref[...]
            new_refs[1][...] = branch
            new_refs[2][...] = jnp.broadcast_to(inv_rms, (rows, LANES))

        @pl.when(jnp.logical_not(held))
        def _():
            for new, old in zip(new_refs, old_refs):
                new[...] = old[...]

    out = jax.ShapeDtypeStruct((rows, width), jnp.bfloat16)
    return pl.pallas_call(
        kernel,
        out_shape=[
            out,
            out,
            jax.ShapeDtypeStruct((rows, width), jnp.float32),
            jax.ShapeDtypeStruct((rows, LANES), jnp.float32),
        ],
        in_specs=[SMEM_SPEC] + [VMEM_SPEC] * (1 + len(chunks) + len(given) + 3),
        out_specs=[VMEM_SPEC] * 4,
        compiler_params=pltpu.CompilerParams(vmem_limit_bytes=VMEM_LIMIT),
    )(jnp.stack([keep]), first, *chunks, *given, *kept)


def gradient_chunks(upstream, kept, others, use_other):
    rows, width = upstream.shape
    chunk_rows = rows + TAIL
    replaced = [other for other in others if other is not None]

    def kernel(meta_ref, up_ref, act_ref, branch_ref, rms_ref, *refs):
        other_refs, out_refs = list(refs[: len(replaced)]), refs[len(replaced) :]
        up = up_ref[...]
        dots = jnp.sum(up.astype(jnp.float32) * branch_ref[...], axis=1, keepdims=True)
        rms_line = rms_ref[...].T[:1]
        rms_high = rms_line.astype(jnp.bfloat16).astype(jnp.float32)
        row_ids = lax.broadcasted_iota(jnp.int32, (TAIL, rows), 0)
        tile = jnp.where(row_ids == 0, as_line(dots), 0.0)
        tile = jnp.where(row_ids == 1, rms_high, tile)
        tile = jnp.where(row_ids == 2, rms_line - rms_high, tile).astype(jnp.bfloat16)
        for out_ref in out_refs:
            out_ref[:rows, :] = up
            out_ref[rows:chunk_rows, :] = jnp.zeros((TAIL, width), jnp.bfloat16)
            out_ref[rows:chunk_rows, :rows] = tile
        out_refs[-1][chunk_rows:, :] = act_ref[...]

        @pl.when(meta_ref[0] == 1)
        def _():
            for other, out_ref in zip(others, out_refs):
                if other is not None:
                    out_ref[...] = other_refs.pop(0)[...]

    chunk = jax.ShapeDtypeStruct((chunk_rows, width), jnp.bfloat16)
    return pl.pallas_call(
        kernel,
        out_shape=[chunk] * len(others)
        + [jax.ShapeDtypeStruct((chunk_rows + rows, width), jnp.bfloat16)],
        in_specs=[SMEM_SPEC] + [VMEM_SPEC] * (4 + len(replaced)),
        out_specs=[VMEM_SPEC] * (len(others) + 1),
        compiler_params=pltpu.CompilerParams(vmem_limit_bytes=VMEM_LIMIT),
    )(jnp.stack([use_other]), upstream, *kept, *replaced)


def block_products(meta_ref, w_ref, chunk_refs, rows, start, tile):
    width = w_ref.shape[0]
    total = None
    for block, chunk in enumerate(chunk_refs):
        columns = pl.ds(pl.multiple_of(meta_ref[block] * width, width), width)
        product = lax.dot_general(
            w_ref[start : start + tile, columns],
            chunk[:rows, :],
            (((1,), (1,)), ((), ())),
            preferred_element_type=jnp.float32,
        )
        total = product if total is None else total + product
    return total


def backward_blocks(chunks, w_rows, blocks, rows):
    width = w_rows.shape[0]
    count = len(blocks)
    tile = min(width, 256)

    def kernel(meta_ref, w_ref, *refs):
        chunk_refs, (out_ref, sum_ref) = refs[:count], refs[count:]
        for start in range(0, width, tile):
            out_ref[start : start + tile, :] = block_products(
                meta_ref, w_ref, chunk_refs, rows, start, tile
            )
        sum_ref[...] = jnp.broadcast_to(first_sum(chunk_refs, rows), (8, rows))

    return pl.pallas_call(
        kernel,
        out_shape=[
            jax.ShapeDtypeStruct((width, rows), jnp.float32),
            jax.ShapeDtypeStruct((8, rows), jnp.float32),
        ],
        in_specs=[SMEM_SPEC] + [VMEM_SPEC] * (1 + count),
        out_specs=[VMEM_SPEC] * 2,
        compiler_params=pltpu.CompilerParams(vmem_limit_bytes=VMEM_LIMIT),
        cost_estimate=matmul_cost(rows, width, count),
    )(jnp.stack(blocks), w_rows, *chunks)


def first_sum(chunk_refs, rows):
    total = chunk_refs[0][rows : rows + TAIL, :rows].astype(jnp.float32)
    for chunk in chunk_refs[1:]:
        total = total + chunk[rows : rows + TAIL, :rows].astype(jnp.float32)
    return total[:1]


def finish_backward(chunks, w_rows, blocks, half, pack, gain_row, a, full_width, kept, keep):
    rows, width = a.shape
    chunk_rows = rows + TAIL
    count = len(blocks)
    tile = min(width, 256)

    def kernel(meta_ref, w_ref, *refs):
        chunk_refs = refs[:count]
        half_ref, sum_ref, pack_ref, gain_ref, a_ref = refs[count : count + 5]
        old_refs, (out_ref, *new_refs) = refs[count + 5 : count + 7], refs[count + 7 :]
        row_dot = as_column(sum_ref[:1] + first_sum(chunk_refs, rows))
        tail = pack_ref[rows:chunk_rows, :rows].astype(jnp.float32)
        rms = as_column(tail[1:2] + tail[2:3])
        scale = rms * rms * rms / full_width * row_dot
        for start in range(0, width, tile):
            products = block_products(meta_ref, w_ref, chunk_refs, rows, start, tile)
            back = (products + half_ref[start : start + tile, :]).T
            columns = slice(start, start + tile)
            out_ref[:, columns] = (
                pack_ref[:rows, columns].astype(jnp.float32)
                + rms * gain_ref[:, columns] * back
                - scale * a_ref[:, columns].astype(jnp.float32)
            ).astype(jnp.bfloat16)
        held = meta_ref[count] == 1

        @pl.when(held)
        def _():
            new_refs[0][...] = out_ref[...]
            new_refs[1][...] = pack_ref[chunk_rows:, :]

        @pl.when(jnp.logical_not(held))
        def _():
            for new, old in zip(new_refs, old_refs):
                new[...] = old[...]

    out = jax.ShapeDtypeStruct((rows, width), jnp.bfloat16)
    return pl.pallas_call(
        kernel,
        out_shape=[out] * 3,
        in_specs=[SMEM_SPEC] + [VMEM_SPEC] * (1 + count + 7),
        out_specs=[VMEM_SPEC] * 3,
        compiler_params=pltpu.CompilerParams(vmem_limit_bytes=VMEM_LIMIT),
        cost_estimate=matmul_cost(rows, width, count),
    )(jnp.stack(blocks + [keep]), w_rows, *chunks, *half, pack, gain_row, a, *kept)


def on_device(inputs, cotangent, weights, gains):
    section_no = lax.axis_index("section")
    section_count = lax.axis_size("section")
    tp_no = lax.axis_index("tp")
    tp_count = lax.axis_size("tp")
    micro_count, row_count, width = inputs.shape
    rows = micro_count * row_count
    chunk_rows = rows + TAIL
    full_width = weights.shape[2]
    w_rows = pltpu.with_memory_space_constraint(weights[0], pltpu.VMEM)
    last = section_count - 1
    across = tp_count // 2
    near = list(range(1, across))
    tail_row = tp_no % TAIL

    def send(value, routes, step=0):
        pairs = [
            (source * tp_count + t, target * tp_count + (t ^ step))
            for source, target in routes
            for t in range(tp_count)
        ]
        return lax.ppermute(value, ("section", "tp"), pairs)

    def is_section(section):
        return (section_no == section).astype(jnp.int32)

    def row_sum(value):
        return jnp.sum(value, axis=1).astype(jnp.bfloat16).astype(jnp.float32)

    cot = cotangent.reshape(rows, width)
    block_in = inputs.reshape(rows, width)
    kept = (
        jnp.zeros_like(block_in),
        jnp.zeros((rows, width), jnp.float32),
        jnp.zeros((rows, LANES), jnp.float32),
    )
    far_blocks = [tp_no ^ across ^ e for e in [0] + near]
    near_blocks = [tp_no ^ e for e in [0] + near]
    at_last = is_section(last)
    inside = [(last, last)]

    cot_chunk = jnp.pad(cot, ((0, TAIL), (0, 0)))
    other = cot_chunk
    cot_found = {0: cot_chunk}
    for section in range(last):
        beside = section ^ 1
        route = [(section, beside)]
        shared = section < 2
        far = forward_blocks(
            block_in, gains, w_rows, far_blocks, tail_row, other if shared else None, at_last
        )
        far_route = route + inside if shared else route
        arrived = [send(chunk, far_route, e) for e, chunk in zip(near, far[1:])]
        own = forward_blocks(block_in, gains, w_rows, near_blocks, tail_row, pack=far[0])
        pack = send(own[0], route)
        if shared:
            for e, chunk in zip(near, arrived):
                cot_found[e if section == 0 else across ^ e] = chunk
        first_pass = section == 0
        combined = add_chunks(
            pack, chunk_rows + rows, arrived, other if first_pass else None, at_last
        )
        crossed = send(combined, [(beside, beside)] + (inside if first_pass else []), across)
        if first_pass:
            cot_found[across] = other = crossed
        parts = own[1:]
        if not shared:
            parts, combined = lax.optimization_barrier((parts, combined))
        direct = [send(chunk, route, e) for e, chunk in zip(near, parts)]
        output, *kept = finish_forward(
            pack, direct + [crossed], None, full_width, kept, is_section(beside)
        )
        if section % 2:
            output = send(output, [(beside, section + 1)])
        block_in = jnp.where(section_no == section + 1, output, block_in)
        if section == 1:
            order = sorted(cot_found)

            def cotangent_rows():
                chunks = [cot_found[e] for e in order]
                back, _ = backward_blocks(chunks, w_rows, [tp_no ^ e for e in order], rows)
                return gains * back.T

            last_back = lax.cond(
                section_no == last, cotangent_rows, lambda: jnp.zeros((rows, width), jnp.float32)
            )

    wide = block_in.astype(jnp.float32)
    sums = jnp.stack([row_sum(wide * wide), row_sum(wide * last_back)])
    step = 1
    while step < tp_count:
        sums = sums + send(sums, ([(0, 1)] if step < across else [(1, 1)]) + inside, step)
        step *= 2
    last_rms = lax.rsqrt(sums[0] / full_width + EPSILON)[:, None]
    grad = (
        cot.astype(jnp.float32)
        + last_rms * last_back
        - (last_rms**3 / full_width * sums[1][:, None]) * wide
    ).astype(jnp.bfloat16)
    results = (grad, jnp.zeros_like(grad))

    chunk_zero = jnp.zeros((chunk_rows, width), jnp.bfloat16)
    last_in, grad = lax.optimization_barrier((block_in, grad))
    parts = lax.cond(
        section_no == last,
        lambda: tuple(forward_blocks(last_in, gains, w_rows, far_blocks, tail_row))
        + tuple(forward_blocks(last_in, gains, w_rows, near_blocks, tail_row)),
        lambda: (chunk_zero,) * tp_count,
    )
    last_far, last_own = list(parts[:across]), list(parts[across:])
    for section in range(last - 1, -1, -1):
        turn = last - 1 - section
        beside = section ^ 1
        route = [(beside, section)]
        upstream = send(grad, [(section + 1, beside)]) if section % 2 else grad
        if turn == 1:
            others = [None] + last_far[1:]
        elif turn == 2:
            others = [last_combined] + last_own[1:]
        else:
            others = [None]
        riding = inside if turn in (1, 2) else []
        *chunks, pack = gradient_chunks(upstream, kept, others, at_last)
        crossed = send(chunks[0], [(beside, beside)] + (inside if turn == 2 else []), across)
        near_chunks = chunks[1:] if riding else chunks * len(near)
        pack = send(pack, route)
        direct = [send(chunk, route + riding, e) for e, chunk in zip(near, near_chunks)]
        far_chunk, pack, direct = lax.optimization_barrier((crossed, pack, direct))
        forwarded = [send(far_chunk, route)]
        forwarded += [send(far_chunk, route + riding, e) for e in near]
        half = backward_blocks([pack] + direct, w_rows, near_blocks, rows)
        if turn == 1:
            last_combined = add_chunks(last_far[0], 0, direct)
        if turn == 2:
            last_output, *_ = finish_forward(
                last_own[0], direct + [crossed], block_in, full_width, kept, at_last
            )
        grad, *results = finish_backward(
            forwarded, w_rows, far_blocks, half, pack, gains, block_in, full_width, results, is_section(section)
        )
    grads, outputs = results
    outputs = jnp.where(section_no == last, last_output, outputs)
    shape = (1, micro_count, row_count, width)
    return outputs.reshape(shape), grads.reshape(shape)


def solution(mesh):
    placed = (
        P(None, None, "tp"),
        P(None, None, "tp"),
        P("section", "tp", None),
        P("section", "tp"),
    )
    return jax.shard_map(
        on_device,
        mesh=mesh,
        in_specs=placed,
        out_specs=(P("section", None, None, "tp"), P("section", None, None, "tp")),
        check_vma=False,
    )
```

time: 310 us -> 302 us (0.974)
  the two profiles are of different devices: /device:TPU:0 before, /device:TPU:7 now
where the time goes in v4:
time: 302 us; the launch traced here: 300 us
  starting transfers between devices  104 us (34%)
  waiting for transfers between devices  66.5 us (22%)
  local copies, waits for them, and re-layouts  65 us (22%)
  Pallas kernels  56.7 us (19%)
  other arithmetic  5.21 us (2%)
    ppermute x56, starting transfers between devices, send(): return lax.ppermute(value, ('section', 'tp'), pairs)  104 us
    ppermute x56, waiting for transfers between devices, send(): return lax.ppermute(value, ('section', 'tp'), pairs)  66.5 us
    unnamed x76, local copies, waits for them, and re-layouts  43.7 us
    pallas_call x8, Pallas kernels, forward_blocks(): pl.pallas_call(kernel, out_shape=[jax.ShapeDtypeStruct(shape, jnp.bfloat1...  20.4 us
    cond x6, local copies, waits for them, and re-layouts  17.4 us
    pallas_call x4, Pallas kernels, backward_blocks(): pl.pallas_call(kernel, out_shape=[jax.ShapeDtypeStruct((width, rows), jnp...  15.1 us
    pallas_call x3, Pallas kernels, finish_backward(): pl.pallas_call(kernel, out_shape=[out] * 3, in_specs=[SMEM_SPEC] + [VMEM_...  11.5 us
  transfers between devices with their start and end apart: 56, of which 17 were waited for; matrix products, arithmetic and copies ran while one was open for 1% of the time, Pallas kernels for 9%

profile of v4, /device:TPU:7, one launch (start us, length us, event | category | flops | bytes accessed | tf_op | source)
XLA Modules:
  0.0 299.8 jit_solution(14112581491666706490)
XLA Ops:
  1.9 5.8 %copy-done = bf16[1,1024,8192]{2,1,0:T(8,128)(2,1)S(1)} copy-done((bf16[1,1024,8192]{2,1,0:T(8,128)(2,1)S(1)}, bf16[1,1024,8192]{2,1,0:T(8,128)(2,1)}, u32[]{:S(2)}) %copy-start) | copy-done | bytes 16777240
  28.5 4.2 %collective-permute-start.7 = (bf16[144,1024]{1,0:T(8,128)(2,1)S(1)}, bf16[144,1024]{1,0:T(8,128)(2,1)}, u32[]{:S(2)}, u32[]{:S(2)}) collective-permute-start(bf16[144,1024]{1,0:T(8,128)(2,1)S(1)} %shard_map.61), channel_id=1, source_target_pairs={{8,12},{9,13},{10,14},{11,15},{12,8},{13,9},{14,10},{15,11},{24,28... | collective-permute-start | bytes 884744 | tf_op jit(solution)/shard_map/ppermute | solution.py:311
  32.8 7.4 %collective-permute-done.7.refs_3_.refs_0_ = bf16[144,1024]{1,0:T(8,128)(2,1)} collective-permute-done((bf16[144,1024]{1,0:T(8,128)(2,1)S(1)}, bf16[144,1024]{1,0:T(8,128)(2,1)}, u32[]{:S(2)}, u32[]{:S(2)}) %collective-permute-start.7) | collective-permute-done | bytes 294944 | tf_op jit(solution)/shard_map/ppermute | solution.py:311
  42.4 5.8 %copy-done.1 = bf16[1,1024,8192]{2,1,0:T(8,128)(2,1)S(1)} copy-done((bf16[1,1024,8192]{2,1,0:T(8,128)(2,1)S(1)}, bf16[1,1024,8192]{2,1,0:T(8,128)(2,1)}, u32[]{:S(2)}) %copy-start.1) | copy-done | bytes 16777240
  59.1 3.3 %collective-permute-start.14 = (bf16[144,1024]{1,0:T(8,128)(2,1)S(1)}, bf16[144,1024]{1,0:T(8,128)(2,1)S(1)}, u32[]{:S(2)}, u32[]{:S(2)}) collective-permute-start(bf16[144,1024]{1,0:T(8,128)(2,1)S(1)} %get-tuple-element.190), channel_id=1, source_target_pairs={{8,3},{9,2},{10,1},{11,0},{12,7},{13,6},{14,5},{15,4},{24,27},{25,... | collective-permute-start | bytes 884744 | tf_op jit(solution)/shard_map/ppermute | solution.py:311
  75.3 5.8 %copy-done.2 = bf16[1,1024,8192]{2,1,0:T(8,128)(2,1)S(1)} copy-done((bf16[1,1024,8192]{2,1,0:T(8,128)(2,1)S(1)}, bf16[1,1024,8192]{2,1,0:T(8,128)(2,1)}, u32[]{:S(2)}) %copy-start.2) | copy-done | bytes 16777240
  90.8 17.7 %collective-permute-done.18.refs_0_ = bf16[144,1024]{1,0:T(8,128)(2,1)S(1)} collective-permute-done((bf16[144,1024]{1,0:T(8,128)(2,1)S(1)}, bf16[144,1024]{1,0:T(8,128)(2,1)S(1)}, u32[]{:S(2)}, u32[]{:S(2)}) %collective-permute-start.18) | collective-permute-done | bytes 294944 | tf_op jit(solution)/shard_map/ppermute | solution.py:311
  118.3 4.9 %collective-permute-start.24 = (bf16[144,1024]{1,0:T(8,128)(2,1)}, bf16[144,1024]{1,0:T(8,128)(2,1)}, u32[]{:S(2)}, u32[]{:S(2)}) collective-permute-start(bf16[144,1024]{1,0:T(8,128)(2,1)} %shard_map.69), channel_id=1, source_target_pairs={{24,28},{25,29},{26,30},{27,31},{28,24},{29,25},{30,26},{31,27}} | collective-permute-start | bytes 884744 | tf_op jit(solution)/shard_map/ppermute | solution.py:311
  123.2 15.6 %conditional.2 = (f32[128,1024]{1,0:T(8,128)}) conditional(s32[]{:T(128)} %convert_element_type.66, () %tuple.29, (f32[1,1024]{1,0:T(1,128)S(1)}, s32[]{:T(128)}, bf16[1024,8192]{1,0:T(8,128)(2,1)}, bf16[144,1024]{1,0:T(8,128)(2,1)}, bf16[144,1024]{1,0:T(8,128)(2,1)}, /*index=5*/bf16[144,1024]{1,0:T(8,128)(2,1)}, bf16[144,1024]{1,0:T(8,128)(2,1)}, ...), branch_computations={%region_1.2_spmd, %region_2.3_spmd} | conditional | flops 2147614720 | bytes 85987512 | solution.py:373
  123.4 5.8 %copy-done.6 = bf16[1024,8192]{1,0:T(8,128)(2,1)S(1)} copy-done((bf16[1024,8192]{1,0:T(8,128)(2,1)S(1)}, bf16[1024,8192]{1,0:T(8,128)(2,1)}, u32[]{:S(2)}) %copy-start.6) | copy-done | bytes 16777240 | tf_op jit(solution)/shard_map/cond
  129.2 6.5 %branch_1_fun.3 = (f32[1024,128]{1,0:T(8,128)S(1)}, f32[8,128]{1,0:T(8,128)}) custom-call(s32[8]{0:T(128)S(1)} %stack.22.meta_ref, bf16[1024,8192]{1,0:T(8,128)(2,1)S(1)} %copy-done.6, bf16[144,1024]{1,0:T(8,128)(2,1)} %get-tuple-element.52.refs_0_, bf16[144,1024]{1,0:T(8,128)(2,1)} %get-tuple-element.53.refs_1_, ...), custom_call_target="tpu_custom_call" | custom-call | flops 2147483648 | bytes 16777216 | tf_op jit(solution)/shard_map/cond/branch_1_fun/pallas_call | solution.py:224
  155.2 3.3 %collective-permute-done.27 = f32[2,128]{1,0:T(2,128)S(1)} collective-permute-done((f32[2,128]{1,0:T(2,128)S(1)}, f32[2,128]{1,0:T(2,128)S(1)}, u32[]{:S(2)}, u32[]{:S(2)}) %collective-permute-start.27) | collective-permute-done | bytes 1056 | tf_op jit(solution)/shard_map/ppermute | solution.py:311
  169.5 7.2 %collective-permute-done.28 = bf16[144,1024]{1,0:T(8,128)(2,1)} collective-permute-done((bf16[144,1024]{1,0:T(8,128)(2,1)S(1)}, bf16[144,1024]{1,0:T(8,128)(2,1)}, u32[]{:S(2)}, u32[]{:S(2)}) %collective-permute-start.28) | collective-permute-done | bytes 294944 | tf_op jit(solution)/shard_map/ppermute | solution.py:311
  183.5 5.8 %copy-done.3 = bf16[1,1024,8192]{2,1,0:T(8,128)(2,1)S(1)} copy-done((bf16[1,1024,8192]{2,1,0:T(8,128)(2,1)S(1)}, bf16[1,1024,8192]{2,1,0:T(8,128)(2,1)}, u32[]{:S(2)}) %copy-start.3) | copy-done | bytes 16777240
  192.2 3.6 %shard_map.73 = (bf16[128,1024]{1,0:T(8,128)(2,1)S(1)}, bf16[128,1024]{1,0:T(8,128)(2,1)S(1)}, bf16[128,1024]{1,0:T(8,128)(2,1)S(1)}) custom-call(s32[5]{0:T(128)S(1)} %stack.217.meta_ref, bf16[1024,8192]{1,0:T(8,128)(2,1)S(1)} %bitcast.60, bf16[144,1024]{1,0:T(8,128)(2,1)} %collective-permute-done.33.refs_0_, ...), custom_call_target="tpu_custom_call" | custom-call | flops 1073741824 | bytes 8388608 | tf_op jit(solution)/shard_map/pallas_call | solution.py:280
  196.6 17.9 %conditional.3 = (bf16[144,1024]{1,0:T(8,128)(2,1)}, bf16[144,1024]{1,0:T(8,128)(2,1)S(1)}, bf16[144,1024]{1,0:T(8,128)(2,1)S(1)}, bf16[144,1024]{1,0:T(8,128)(2...) conditional(s32[]{:T(128)} %convert_element_type.66, () %tuple.27, ...), branch_computations={%region_4.5_spmd, %region_5.6_spmd} | conditional | flops 2147483648 | bytes 150995136 | solution.py:393
  196.6 5.8 %copy-done.7 = bf16[1024,8192]{1,0:T(8,128)(2,1)} copy-done((bf16[1024,8192]{1,0:T(8,128)(2,1)}, bf16[1024,8192]{1,0:T(8,128)(2,1)S(1)}, u32[]{:S(2)}) %copy-start.7) | copy-done | bytes 16777240 | tf_op jit(solution)/shard_map/cond
  202.6 5.8 %copy-done.8 = bf16[1024,8192]{1,0:T(8,128)(2,1)S(1)} copy-done((bf16[1024,8192]{1,0:T(8,128)(2,1)S(1)}, bf16[1024,8192]{1,0:T(8,128)(2,1)}, u32[]{:S(2)}) %copy-start.8) | copy-done | bytes 16777240 | tf_op jit(solution)/shard_map/cond
  241.6 5.8 %copy-done.4 = bf16[1,1024,8192]{2,1,0:T(8,128)(2,1)S(1)} copy-done((bf16[1,1024,8192]{2,1,0:T(8,128)(2,1)S(1)}, bf16[1,1024,8192]{2,1,0:T(8,128)(2,1)}, u32[]{:S(2)}) %copy-start.4) | copy-done | bytes 16777240
  250.3 3.5 %shard_map.76 = (bf16[128,1024]{1,0:T(8,128)(2,1)S(1)}, bf16[128,1024]{1,0:T(8,128)(2,1)S(1)}, bf16[128,1024]{1,0:T(8,128)(2,1)S(1)}) custom-call(s32[5]{0:T(128)S(1)} %stack.214.meta_ref, bf16[1024,8192]{1,0:T(8,128)(2,1)S(1)} %bitcast.63, bf16[144,1024]{1,0:T(8,128)(2,1)} %collective-permute-done.43.refs_0_, ...), custom_call_target="tpu_custom_call" | custom-call | flops 1073741824 | bytes 8388608 | tf_op jit(solution)/shard_map/pallas_call | solution.py:280
  269.3 4.3 %collective-permute-done.51.refs_2_.refs_3_ = bf16[144,1024]{1,0:T(8,128)(2,1)S(1)} collective-permute-done((bf16[144,1024]{1,0:T(8,128)(2,1)S(1)}, bf16[144,1024]{1,0:T(8,128)(2,1)S(1)}, u32[]{:S(2)}, u32[]{:S(2)}) %collective-permute-start.51) | collective-permute-done | bytes 294944 | tf_op jit(solution)/shard_map/ppermute | solution.py:311
  278.7 3.4 %collective-permute-start.53 = (bf16[144,1024]{1,0:T(8,128)(2,1)S(1)}, bf16[144,1024]{1,0:T(8,128)(2,1)}, u32[]{:S(2)}, u32[]{:S(2)}) collective-permute-start(bf16[144,1024]{1,0:T(8,128)(2,1)S(1)} %collective-permute-done.47.refs_3_), channel_id=1, source_target_pairs={{8,1},{9,0},{10,3},{11,2},{12,5},{13,4},{14,7},{15,6},{24,25},{25,... | collective-permute-start | bytes 884744 | tf_op jit(solution)/shard_map/ppermute | solution.py:311
  286.0 5.8 %copy-done.5 = bf16[1,1024,8192]{2,1,0:T(8,128)(2,1)S(1)} copy-done((bf16[1,1024,8192]{2,1,0:T(8,128)(2,1)S(1)}, bf16[1,1024,8192]{2,1,0:T(8,128)(2,1)}, u32[]{:S(2)}) %copy-start.5) | copy-done | bytes 16777240
  294.7 4.4 %shard_map.81 = (bf16[128,1024]{1,0:T(8,128)(2,1)}, bf16[128,1024]{1,0:T(8,128)(2,1)}, bf16[128,1024]{1,0:T(8,128)(2,1)S(1)}) custom-call(s32[5]{0:T(128)S(1)} %stack.219.meta_ref, bf16[1024,8192]{1,0:T(8,128)(2,1)S(1)} %bitcast.65, bf16[144,1024]{1,0:T(8,128)(2,1)} %collective-permute-done.52.refs_0_, bf16[144,1024]{1,0:T(8,128)(2,1)} %collective-permute-done.53.refs_1_, ...), custom_call_target="tpu_custom_call" | custom-call | flops 1073741824 | bytes 8388608 | tf_op jit(solution)/shard_map/pallas_call | solution.py:280
  (225 shorter events, 172.2 us)
Async XLA Ops:
  13.3 14.5 %collective-permute-start = (bf16[416,1024]{1,0:T(8,128)(2,1)S(1)}, bf16[416,1024]{1,0:T(8,128)(2,1)S(1)}, u32[]{:S(2)}, u32[]{:S(2)}) collective-permute-start(bf16[416,1024]{1,0:T(8,128)(2,1)S(1)} %get-tuple-element.175), channel_id=1, source_target_pairs={{0,8},{1,9},{2,10},{3,11},{4,12},{5,13},{6,14},{7,15}} | collective-permute-start | bytes 2555912 | tf_op jit(solution)/shard_map/ppermute | solution.py:311
  53.3 14.4 %collective-permute-start.8 = (bf16[416,1024]{1,0:T(8,128)(2,1)S(1)}, bf16[416,1024]{1,0:T(8,128)(2,1)S(1)}, u32[]{:S(2)}, u32[]{:S(2)}) collective-permute-start(bf16[416,1024]{1,0:T(8,128)(2,1)S(1)} %get-tuple-element.184), channel_id=1, source_target_pairs={{8,0},{9,1},{10,2},{11,3},{12,4},{13,5},{14,6},{15,7}} | collective-permute-start | bytes 2555912 | tf_op jit(solution)/shard_map/ppermute | solution.py:311
  85.7 27.8 %collective-permute-start.17 = (bf16[416,1024]{1,0:T(8,128)(2,1)S(1)}, bf16[416,1024]{1,0:T(8,128)(2,1)S(1)}, u32[]{:S(2)}, u32[]{:S(2)}) collective-permute-start(bf16[416,1024]{1,0:T(8,128)(2,1)S(1)} %get-tuple-element.196), channel_id=1, source_target_pairs={{16,24},{17,25},{18,26},{19,27},{20,28},{21,29},{22,30},{23,31}} | collective-permute-start | bytes 2555912 | tf_op jit(solution)/shard_map/ppermute | solution.py:311
  86.9 21.6 %collective-permute-start.18 = (bf16[144,1024]{1,0:T(8,128)(2,1)S(1)}, bf16[144,1024]{1,0:T(8,128)(2,1)S(1)}, u32[]{:S(2)}, u32[]{:S(2)}) collective-permute-start(bf16[144,1024]{1,0:T(8,128)(2,1)S(1)} %get-tuple-element.200), channel_id=1, source_target_pairs={{16,25},{17,24},{18,27},{19,26},{20,29},{21,28},{22,31},{23,30}} | collective-permute-start | bytes 884744 | tf_op jit(solution)/shard_map/ppermute | solution.py:311
  88.2 22.0 %collective-permute-start.19 = (bf16[144,1024]{1,0:T(8,128)(2,1)S(1)}, bf16[144,1024]{1,0:T(8,128)(2,1)S(1)}, u32[]{:S(2)}, u32[]{:S(2)}) collective-permute-start(bf16[144,1024]{1,0:T(8,128)(2,1)S(1)} %get-tuple-element.201), channel_id=1, source_target_pairs={{16,26},{17,27},{18,24},{19,25},{20,30},{21,31},{22,28},{23,29}} | collective-permute-start | bytes 884744 | tf_op jit(solution)/shard_map/ppermute | solution.py:311
  89.5 23.9 %collective-permute-start.20 = (bf16[144,1024]{1,0:T(8,128)(2,1)S(1)}, bf16[144,1024]{1,0:T(8,128)(2,1)S(1)}, u32[]{:S(2)}, u32[]{:S(2)}) collective-permute-start(bf16[144,1024]{1,0:T(8,128)(2,1)S(1)} %get-tuple-element.202), channel_id=1, source_target_pairs={{16,27},{17,26},{18,25},{19,24},{20,31},{21,30},{22,29},{23,28}} | collective-permute-start | bytes 884744 | tf_op jit(solution)/shard_map/ppermute | solution.py:311
  114.4 24.4 %collective-permute-start.21 = (bf16[144,1024]{1,0:T(8,128)(2,1)}, bf16[144,1024]{1,0:T(8,128)(2,1)S(1)}, u32[]{:S(2)}, u32[]{:S(2)}) collective-permute-start(bf16[144,1024]{1,0:T(8,128)(2,1)} %get-tuple-element.203), channel_id=1, source_target_pairs={{16,25},{17,24},{18,27},{19,26},{20,29},{21,28},{22,31},{23,30}} | collective-permute-start | bytes 884744 | tf_op jit(solution)/shard_map/ppermute | solution.py:311
  115.7 23.1 %collective-permute-start.22 = (bf16[144,1024]{1,0:T(8,128)(2,1)}, bf16[144,1024]{1,0:T(8,128)(2,1)S(1)}, u32[]{:S(2)}, u32[]{:S(2)}) collective-permute-start(bf16[144,1024]{1,0:T(8,128)(2,1)} %get-tuple-element.204), channel_id=1, source_target_pairs={{16,26},{17,27},{18,24},{19,25},{20,30},{21,31},{22,28},{23,29}} | collective-permute-start | bytes 884744 | tf_op jit(solution)/shard_map/ppermute | solution.py:311
  117.0 21.8 %collective-permute-start.23 = (bf16[144,1024]{1,0:T(8,128)(2,1)}, bf16[144,1024]{1,0:T(8,128)(2,1)S(1)}, u32[]{:S(2)}, u32[]{:S(2)}) collective-permute-start(bf16[144,1024]{1,0:T(8,128)(2,1)} %get-tuple-element.205), channel_id=1, source_target_pairs={{16,27},{17,26},{18,25},{19,24},{20,31},{21,30},{22,29},{23,28}} | collective-permute-start | bytes 884744 | tf_op jit(solution)/shard_map/ppermute | solution.py:311
  118.3 21.3 %collective-permute-start.24 = (bf16[144,1024]{1,0:T(8,128)(2,1)}, bf16[144,1024]{1,0:T(8,128)(2,1)}, u32[]{:S(2)}, u32[]{:S(2)}) collective-permute-start(bf16[144,1024]{1,0:T(8,128)(2,1)} %shard_map.69), channel_id=1, source_target_pairs={{24,28},{25,29},{26,30},{27,31},{28,24},{29,25},{30,26},{31,27}} | collective-permute-start | bytes 884744 | tf_op jit(solution)/shard_map/ppermute | solution.py:311
  160.1 16.7 %collective-permute-start.29 = (bf16[272,1024]{1,0:T(8,128)(2,1)S(1)}, bf16[272,1024]{1,0:T(8,128)(2,1)S(1)}, u32[]{:S(2)}, u32[]{:S(2)}) collective-permute-start(bf16[272,1024]{1,0:T(8,128)(2,1)S(1)} %get-tuple-element.217), channel_id=1, source_target_pairs={{24,16},{25,17},{26,18},{27,19},{28,20},{29,21},{30,22},{31,23}} | collective-permute-start | bytes 1671176 | tf_op jit(solution)/shard_map/ppermute | solution.py:311
  176.7 15.4 %collective-permute-start.36 = (bf16[144,1024]{1,0:T(8,128)(2,1)}, bf16[144,1024]{1,0:T(8,128)(2,1)S(1)}, u32[]{:S(2)}, u32[]{:S(2)}) collective-permute-start(bf16[144,1024]{1,0:T(8,128)(2,1)} %collective-permute-done.28), channel_id=1, source_target_pairs={{24,19},{25,18},{26,17},{27,16},{28,23},{29,22},{30,21},{31,20}} | collective-permute-start | bytes 884744 | tf_op jit(solution)/shard_map/ppermute | solution.py:311
  178.1 14.1 %collective-permute-start.35 = (bf16[144,1024]{1,0:T(8,128)(2,1)}, bf16[144,1024]{1,0:T(8,128)(2,1)S(1)}, u32[]{:S(2)}, u32[]{:S(2)}) collective-permute-start(bf16[144,1024]{1,0:T(8,128)(2,1)} %collective-permute-done.28), channel_id=1, source_target_pairs={{24,18},{25,19},{26,16},{27,17},{28,22},{29,23},{30,20},{31,21}} | collective-permute-start | bytes 884744 | tf_op jit(solution)/shard_map/ppermute | solution.py:311
  179.4 12.8 %collective-permute-start.34 = (bf16[144,1024]{1,0:T(8,128)(2,1)}, bf16[144,1024]{1,0:T(8,128)(2,1)}, u32[]{:S(2)}, u32[]{:S(2)}) collective-permute-start(bf16[144,1024]{1,0:T(8,128)(2,1)} %collective-permute-done.28), channel_id=1, source_target_pairs={{24,17},{25,16},{26,19},{27,18},{28,21},{29,20},{30,23},{31,22}} | collective-permute-start | bytes 884744 | tf_op jit(solution)/shard_map/ppermute | solution.py:311
  195.8 18.7 %collective-permute-start.37 = (bf16[128,1024]{1,0:T(8,128)(2,1)S(1)}, bf16[128,1024]{1,0:T(8,128)(2,1)S(1)}, u32[]{:S(2)}, u32[]{:S(2)}) collective-permute-start(bf16[128,1024]{1,0:T(8,128)(2,1)S(1)} %get-tuple-element.225), channel_id=1, source_target_pairs={{16,0},{17,1},{18,2},{19,3},{20,4},{21,5},{22,6},{23,7}} | collective-permute-start | bytes 786440 | tf_op jit(solution)/shard_map/ppermute | solution.py:311
  214.7 15.9 %collective-permute-start.39 = (bf16[272,1024]{1,0:T(8,128)(2,1)S(1)}, bf16[272,1024]{1,0:T(8,128)(2,1)S(1)}, u32[]{:S(2)}, u32[]{:S(2)}) collective-permute-start(bf16[272,1024]{1,0:T(8,128)(2,1)S(1)} %get-tuple-element.230), channel_id=1, source_target_pairs={{0,8},{1,9},{2,10},{3,11},{4,12},{5,13},{6,14},{7,15}} | collective-permute-start | bytes 1671176 | tf_op jit(solution)/shard_map/ppermute | solution.py:311
  230.6 19.6 %collective-permute-start.46 = (bf16[144,1024]{1,0:T(8,128)(2,1)}, bf16[144,1024]{1,0:T(8,128)(2,1)S(1)}, u32[]{:S(2)}, u32[]{:S(2)}) collective-permute-start(bf16[144,1024]{1,0:T(8,128)(2,1)} %collective-permute-done.38), channel_id=1, source_target_pairs={{0,11},{1,10},{2,9},{3,8},{4,15},{5,14},{6,13},{7,12},{24,27},{25,... | collective-permute-start | bytes 884744 | tf_op jit(solution)/shard_map/ppermute | solution.py:311
  233.8 16.5 %collective-permute-start.45 = (bf16[144,1024]{1,0:T(8,128)(2,1)}, bf16[144,1024]{1,0:T(8,128)(2,1)S(1)}, u32[]{:S(2)}, u32[]{:S(2)}) collective-permute-start(bf16[144,1024]{1,0:T(8,128)(2,1)} %collective-permute-done.38), channel_id=1, source_target_pairs={{0,10},{1,11},{2,8},{3,9},{4,14},{5,15},{6,12},{7,13},{24,26},{25,... | collective-permute-start | bytes 884744 | tf_op jit(solution)/shard_map/ppermute | solution.py:311
  236.9 13.4 %collective-permute-start.44 = (bf16[144,1024]{1,0:T(8,128)(2,1)}, bf16[144,1024]{1,0:T(8,128)(2,1)S(1)}, u32[]{:S(2)}, u32[]{:S(2)}) collective-permute-start(bf16[144,1024]{1,0:T(8,128)(2,1)} %collective-permute-done.38), channel_id=1, source_target_pairs={{0,9},{1,8},{2,11},{3,10},{4,13},{5,12},{6,15},{7,14},{24,25},{25,... | collective-permute-start | bytes 884744 | tf_op jit(solution)/shard_map/ppermute | solution.py:311
  254.1 19.5 %collective-permute-start.48 = (bf16[272,1024]{1,0:T(8,128)(2,1)S(1)}, bf16[272,1024]{1,0:T(8,128)(2,1)S(1)}, u32[]{:S(2)}, u32[]{:S(2)}) collective-permute-start(bf16[272,1024]{1,0:T(8,128)(2,1)S(1)} %get-tuple-element.249), channel_id=1, source_target_pairs={{8,0},{9,1},{10,2},{11,3},{12,4},{13,5},{14,6},{15,7}} | collective-permute-start | bytes 1671176 | tf_op jit(solution)/shard_map/ppermute | solution.py:311
  273.6 21.0 %collective-permute-start.55 = (bf16[144,1024]{1,0:T(8,128)(2,1)S(1)}, bf16[144,1024]{1,0:T(8,128)(2,1)S(1)}, u32[]{:S(2)}, u32[]{:S(2)}) collective-permute-start(bf16[144,1024]{1,0:T(8,128)(2,1)S(1)} %collective-permute-done.47.refs_3_), channel_id=1, source_target_pairs={{8,3},{9,2},{10,1},{11,0},{12,7},{13,6},{14,5},{15,4},{24,27},{25,... | collective-permute-start | bytes 884744 | tf_op jit(solution)/shard_map/ppermute | solution.py:311
  275.6 19.1 %collective-permute-start.54 = (bf16[144,1024]{1,0:T(8,128)(2,1)S(1)}, bf16[144,1024]{1,0:T(8,128)(2,1)S(1)}, u32[]{:S(2)}, u32[]{:S(2)}) collective-permute-start(bf16[144,1024]{1,0:T(8,128)(2,1)S(1)} %collective-permute-done.47.refs_3_), channel_id=1, source_target_pairs={{8,2},{9,3},{10,0},{11,1},{12,6},{13,7},{14,4},{15,5},{24,26},{25,... | collective-permute-start | bytes 884744 | tf_op jit(solution)/shard_map/ppermute | solution.py:311
  278.7 16.0 %collective-permute-start.53 = (bf16[144,1024]{1,0:T(8,128)(2,1)S(1)}, bf16[144,1024]{1,0:T(8,128)(2,1)}, u32[]{:S(2)}, u32[]{:S(2)}) collective-permute-start(bf16[144,1024]{1,0:T(8,128)(2,1)S(1)} %collective-permute-done.47.refs_3_), channel_id=1, source_target_pairs={{8,1},{9,0},{10,3},{11,2},{12,5},{13,4},{14,7},{15,6},{24,25},{25,... | collective-permute-start | bytes 884744 | tf_op jit(solution)/shard_map/ppermute | solution.py:311
  282.1 12.6 %collective-permute-start.52 = (bf16[144,1024]{1,0:T(8,128)(2,1)S(1)}, bf16[144,1024]{1,0:T(8,128)(2,1)}, u32[]{:S(2)}, u32[]{:S(2)}) collective-permute-start(bf16[144,1024]{1,0:T(8,128)(2,1)S(1)} %collective-permute-done.47.refs_3_), channel_id=1, source_target_pairs={{8,0},{9,1},{10,2},{11,3},{12,4},{13,5},{14,6},{15,7}} | collective-permute-start | bytes 884744 | tf_op jit(solution)/shard_map/ppermute | solution.py:311
  (73 other events, 544.6 us)

commit v5 on v4

--- a/solution.py
+++ b/solution.py
@@ -9,7 +9,7 @@
 MIB = 1 << 20
 TAIL = 16
 LANES = 128
-VMEM_LIMIT = 20 * MIB
+VMEM_LIMIT = 12 * MIB
 SMEM_SPEC = pl.BlockSpec(memory_space=pltpu.SMEM)
 VMEM_SPEC = pl.BlockSpec(memory_space=pltpu.VMEM)
 
@@ -44,12 +44,29 @@
     )
 
 
-def forward_blocks(a, gain_row, w_rows, blocks, tail_row, other=None, use_other=None, pack=None):
+def load_weights(w_rows):
+    def kernel(source_ref, out_ref, done):
+        copy = pltpu.make_async_copy(source_ref, out_ref, done)
+        copy.start()
+        copy.wait()
+
+    return pl.pallas_call(
+        kernel,
+        out_shape=pltpu.VMEM(w_rows.shape, w_rows.dtype),
+        in_specs=[pl.BlockSpec(memory_space=pl.ANY)],
+        out_specs=VMEM_SPEC,
+        scratch_shapes=[pltpu.SemaphoreType.DMA],
+        compiler_params=pltpu.CompilerParams(vmem_limit_bytes=MIB),
+        cost_estimate=pl.CostEstimate(flops=0, bytes_accessed=2 * w_rows.size, transcendentals=0),
+    )(w_rows)
+
+
+def forward_blocks(a, gain_row, w_rows, blocks, tail_row, other=None, use_other=None, pack=False):
     rows, width = a.shape
     chunk_rows = rows + TAIL
     count = len(blocks)
     tile = min(width, 512)
-    extras = [x for x in (other, pack) if x is not None]
+    extras = [x for x in (other,) if x is not None]
     meta = jnp.stack(blocks + [tail_row] + ([use_other] if other is not None else []))
 
     def kernel(meta_ref, a_ref, gain_ref, w_ref, *refs):
@@ -64,9 +81,8 @@
         line = as_line(jnp.sum(wide * wide, axis=1, keepdims=True))
         for out_ref in out_refs:
             store_tail(out_ref, rows, line, meta_ref[count])
-        if pack is not None:
-            out_refs[0][chunk_rows : chunk_rows + rows, :] = a_ref[...]
-            out_refs[0][chunk_rows + rows :, :] = refs[len(extras) - 1][...]
+        if pack:
+            out_refs[0][chunk_rows:, :] = a_ref[...]
         if other is not None:
 
             @pl.when(meta_ref[count + 1] == 1)
@@ -75,8 +91,8 @@
                     out_ref[...] = refs[0][...]
 
     shapes = [(chunk_rows, width)] * count
-    if pack is not None:
-        shapes[0] = (2 * chunk_rows + rows, width)
+    if pack:
+        shapes[0] = (chunk_rows + rows, width)
     return pl.pallas_call(
         kernel,
         out_shape=[jax.ShapeDtypeStruct(shape, jnp.bfloat16) for shape in shapes],
@@ -87,12 +103,10 @@
     )(meta, a, gain_row, w_rows, *extras)
 
 
-def add_chunks(first, first_row, chunks, other=None, use_other=None):
-    shape = chunks[0].shape
-
-    def kernel(meta_ref, first_ref, *refs):
-        total = first_ref[first_row : first_row + shape[0], :].astype(jnp.float32)
-        for chunk in refs[: len(chunks)]:
+def add_chunks(chunks, other=None, use_other=None):
+    def kernel(meta_ref, *refs):
+        total = refs[0][...].astype(jnp.float32)
+        for chunk in refs[1 : len(chunks)]:
             total = total + chunk[...].astype(jnp.float32)
         refs[-1][...] = total.astype(jnp.bfloat16)
         if other is not None:
@@ -101,61 +115,48 @@
             def _():
                 refs[-1][...] = refs[len(chunks)][...]
 
-    operands = [first] + chunks + ([other] if other is not None else [])
+    operands = chunks + ([other] if other is not None else [])
     meta = jnp.stack([use_other if other is not None else jnp.int32(0)])
     return pl.pallas_call(
         kernel,
-        out_shape=jax.ShapeDtypeStruct(shape, jnp.bfloat16),
+        out_shape=jax.ShapeDtypeStruct(chunks[0].shape, jnp.bfloat16),
         in_specs=[SMEM_SPEC] + [VMEM_SPEC] * len(operands),
         out_specs=VMEM_SPEC,
         compiler_params=pltpu.CompilerParams(vmem_limit_bytes=VMEM_LIMIT),
     )(meta, *operands)
 
 
-def finish_forward(first, chunks, a, full_width, kept, keep):
+def finish_forward(first, chunks, a, full_width):
     chunk_rows, width = chunks[0].shape
     rows = chunk_rows - TAIL
     given = [] if a is None else [a]
 
-    def kernel(meta_ref, first_ref, *refs):
-        chunk_refs, rest = refs[: len(chunks)], refs[len(chunks) + len(given) :]
-        old_refs, (out_ref, *new_refs) = rest[:3], rest[3:]
-        source = first_ref[chunk_rows : chunk_rows + rows, :] if a is None else refs[len(chunks)][...]
+    def kernel(first_ref, *refs):
+        chunk_refs, (out_ref, branch_ref, rms_ref) = refs[: len(chunks)], refs[-3:]
+        source = first_ref[chunk_rows:, :] if a is None else refs[len(chunks)][...]
         branch = first_ref[:rows, :].astype(jnp.float32)
         for chunk in chunk_refs:
             branch = branch + chunk[:rows, :].astype(jnp.float32)
         squares = as_column(tail_sum((first_ref,) + chunk_refs, rows))
         inv_rms = lax.rsqrt(squares / full_width + EPSILON)
         out_ref[...] = (source.astype(jnp.float32) + inv_rms * branch).astype(jnp.bfloat16)
-        held = meta_ref[0] == 1
-
-        @pl.when(held)
-        def _():
-            new_refs[0][...] = out_ref[...]
-            new_refs[1][...] = branch
-            new_refs[2][...] = jnp.broadcast_to(inv_rms, (rows, LANES))
-
-        @pl.when(jnp.logical_not(held))
-        def _():
-            for new, old in zip(new_refs, old_refs):
-                new[...] = old[...]
-
-    out = jax.ShapeDtypeStruct((rows, width), jnp.bfloat16)
+        branch_ref[...] = branch
+        rms_ref[...] = jnp.broadcast_to(inv_rms, (rows, LANES))
+
     return pl.pallas_call(
         kernel,
         out_shape=[
-            out,
-            out,
+            jax.ShapeDtypeStruct((rows, width), jnp.bfloat16),
             jax.ShapeDtypeStruct((rows, width), jnp.float32),
             jax.ShapeDtypeStruct((rows, LANES), jnp.float32),
         ],
-        in_specs=[SMEM_SPEC] + [VMEM_SPEC] * (1 + len(chunks) + len(given) + 3),
-        out_specs=[VMEM_SPEC] * 4,
-        compiler_params=pltpu.CompilerParams(vmem_limit_bytes=VMEM_LIMIT),
-    )(jnp.stack([keep]), first, *chunks, *given, *kept)
-
-
-def gradient_chunks(upstream, kept, others, use_other):
+        in_specs=[VMEM_SPEC] * (1 + len(chunks) + len(given)),
+        out_specs=[VMEM_SPEC] * 3,
+        compiler_params=pltpu.CompilerParams(vmem_limit_bytes=VMEM_LIMIT),
+    )(first, *chunks, *given)
+
+
+def gradient_chunks(upstream, passed, others, use_other):
     rows, width = upstream.shape
     chunk_rows = rows + TAIL
     replaced = [other for other in others if other is not None]
@@ -190,7 +191,7 @@
         in_specs=[SMEM_SPEC] + [VMEM_SPEC] * (4 + len(replaced)),
         out_specs=[VMEM_SPEC] * (len(others) + 1),
         compiler_params=pltpu.CompilerParams(vmem_limit_bytes=VMEM_LIMIT),
-    )(jnp.stack([use_other]), upstream, *kept, *replaced)
+    )(jnp.stack([use_other]), upstream, *passed, *replaced)
 
 
 def block_products(meta_ref, w_ref, chunk_refs, rows, start, tile):
@@ -296,10 +297,10 @@
     rows = micro_count * row_count
     chunk_rows = rows + TAIL
     full_width = weights.shape[2]
-    w_rows = pltpu.with_memory_space_constraint(weights[0], pltpu.VMEM)
+    w_rows = pltpu.with_memory_space_constraint(load_weights(weights[0]), pltpu.VMEM)
     last = section_count - 1
     across = tp_count // 2
-    near = list(range(1, across))
+    near = list(range(across - 1, 0, -1))
     tail_row = tp_no % TAIL
 
     def send(value, routes, step=0):
@@ -318,11 +319,8 @@
 
     cot = cotangent.reshape(rows, width)
     block_in = inputs.reshape(rows, width)
-    kept = (
-        jnp.zeros_like(block_in),
-        jnp.zeros((rows, width), jnp.float32),
-        jnp.zeros((rows, LANES), jnp.float32),
-    )
+    block_ins = []
+    passed = []
     far_blocks = [tp_no ^ across ^ e for e in [0] + near]
     near_blocks = [tp_no ^ e for e in [0] + near]
     at_last = is_section(last)
@@ -340,28 +338,24 @@
         )
         far_route = route + inside if shared else route
         arrived = [send(chunk, far_route, e) for e, chunk in zip(near, far[1:])]
-        own = forward_blocks(block_in, gains, w_rows, near_blocks, tail_row, pack=far[0])
-        pack = send(own[0], route)
+        own = forward_blocks(block_in, gains, w_rows, near_blocks, tail_row, pack=True)
         if shared:
             for e, chunk in zip(near, arrived):
                 cot_found[e if section == 0 else across ^ e] = chunk
         first_pass = section == 0
         combined = add_chunks(
-            pack, chunk_rows + rows, arrived, other if first_pass else None, at_last
+            [send(far[0], route)] + arrived, other if first_pass else None, at_last
         )
         crossed = send(combined, [(beside, beside)] + (inside if first_pass else []), across)
         if first_pass:
             cot_found[across] = other = crossed
-        parts = own[1:]
-        if not shared:
-            parts, combined = lax.optimization_barrier((parts, combined))
-        direct = [send(chunk, route, e) for e, chunk in zip(near, parts)]
-        output, *kept = finish_forward(
-            pack, direct + [crossed], None, full_width, kept, is_section(beside)
+        direct = [send(chunk, route, e) for e, chunk in zip(near, own[1:])]
+        output, branch, inv_rms = finish_forward(
+            send(own[0], route), direct + [crossed], None, full_width
         )
-        if section % 2:
-            output = send(output, [(beside, section + 1)])
-        block_in = jnp.where(section_no == section + 1, output, block_in)
+        block_ins.append(block_in)
+        passed.append((output, branch, inv_rms))
+        block_in = send(output, [(beside, section + 1)]) if section % 2 else output
         if section == 1:
             order = sorted(cot_found)
 
@@ -409,23 +403,30 @@
         else:
             others = [None]
         riding = inside if turn in (1, 2) else []
-        *chunks, pack = gradient_chunks(upstream, kept, others, at_last)
+        *chunks, pack = gradient_chunks(upstream, passed[section], others, at_last)
         crossed = send(chunks[0], [(beside, beside)] + (inside if turn == 2 else []), across)
         near_chunks = chunks[1:] if riding else chunks * len(near)
         pack = send(pack, route)
         direct = [send(chunk, route + riding, e) for e, chunk in zip(near, near_chunks)]
-        far_chunk, pack, direct = lax.optimization_barrier((crossed, pack, direct))
-        forwarded = [send(far_chunk, route)]
-        forwarded += [send(far_chunk, route + riding, e) for e in near]
+        forwarded = [send(crossed, route)] + [send(crossed, route, e) for e in near]
         half = backward_blocks([pack] + direct, w_rows, near_blocks, rows)
         if turn == 1:
-            last_combined = add_chunks(last_far[0], 0, direct)
+            last_combined = add_chunks([last_far[0]] + direct)
         if turn == 2:
-            last_output, *_ = finish_forward(
-                last_own[0], direct + [crossed], block_in, full_width, kept, at_last
+            last_output, _, _ = finish_forward(
+                last_own[0], direct + [crossed], last_in, full_width
             )
         grad, *results = finish_backward(
-            forwarded, w_rows, far_blocks, half, pack, gains, block_in, full_width, results, is_section(section)
+            forwarded,
+            w_rows,
+            far_blocks,
+            half,
+            pack,
+            gains,
+            block_ins[section],
+            full_width,
+            results,
+            is_section(section),
         )
     grads, outputs = results
     outputs = jnp.where(section_no == last, last_output, outputs)

time: 302 us -> 288 us (0.954)
  the two profiles are of different devices: /device:TPU:7 before, /device:TPU:5 now
where the time goes in v5:
time: 288 us; the launch traced here: 286 us
  starting transfers between devices  97.9 us (34%)
  local copies, waits for them, and re-layouts  86.5 us (30%)
  Pallas kernels  56.4 us (20%)
  waiting for transfers between devices  38.3 us (13%)
  other arithmetic  4.49 us (2%)
    ppermute x59, starting transfers between devices, send(): return lax.ppermute(value, ('section', 'tp'), pairs)  97.9 us
    unnamed x88, local copies, waits for them, and re-layouts  60.6 us
    ppermute x59, waiting for transfers between devices, send(): return lax.ppermute(value, ('section', 'tp'), pairs)  38.3 us
    cond x10, local copies, waits for them, and re-layouts  23.1 us
    pallas_call x8, Pallas kernels, forward_blocks(): pl.pallas_call(kernel, out_shape=[jax.ShapeDtypeStruct(shape, jnp.bfloat1...  18.1 us
    pallas_call x4, Pallas kernels, backward_blocks(): pl.pallas_call(kernel, out_shape=[jax.ShapeDtypeStruct((width, rows), jnp...  15.1 us
    pallas_call x3, Pallas kernels, finish_backward(): pl.pallas_call(kernel, out_shape=[out] * 3, in_specs=[SMEM_SPEC] + [VMEM_...  11.6 us
  transfers between devices with their start and end apart: 59, of which 14 were waited for; matrix products, arithmetic and copies ran while one was open for 1% of the time, Pallas kernels for 11%

profile of v5, /device:TPU:5, one launch (start us, length us, event | category | flops | bytes accessed | tf_op | source)
XLA Modules:
  0.0 285.6 jit_solution(14684037809045859282)
XLA Ops:
  0.7 5.8 %copy-done.12 = bf16[1,1024,8192]{2,1,0:T(8,128)(2,1)S(1)} copy-done((bf16[1,1024,8192]{2,1,0:T(8,128)(2,1)S(1)}, bf16[1,1024,8192]{2,1,0:T(8,128)(2,1)}, u32[]{:S(2)}) %copy-start.12) | copy-done | bytes 16777240
  7.6 5.8 %copy-done = bf16[1024,8192]{1,0:T(8,128)(2,1)} copy-done((bf16[1024,8192]{1,0:T(8,128)(2,1)}, bf16[1024,8192]{1,0:T(8,128)(2,1)S(1)}, u32[]{:S(2)}) %copy-start) | copy-done | bytes 16777240
  13.6 5.8 %copy-done.1 = bf16[1024,8192]{1,0:T(8,128)(2,1)S(1)} copy-done((bf16[1024,8192]{1,0:T(8,128)(2,1)S(1)}, bf16[1024,8192]{1,0:T(8,128)(2,1)}, u32[]{:S(2)}) %copy-start.1) | copy-done | bytes 16777240
  21.9 4.1 %collective-permute-start.5 = (bf16[144,1024]{1,0:T(8,128)(2,1)S(1)}, bf16[144,1024]{1,0:T(8,128)(2,1)S(1)}, u32[]{:S(2)}, u32[]{:S(2)}) collective-permute-start(bf16[144,1024]{1,0:T(8,128)(2,1)S(1)} %get-tuple-element.158), channel_id=1, source_target_pairs={{0,11},{1,10},{2,9},{3,8},{4,15},{5,14},{6,13},{7,12},{24,27},{25,... | collective-permute-start | bytes 884744 | tf_op jit(solution)/shard_map/ppermute | solution.py:312
  30.4 5.8 %copy-done.2 = bf16[1024,8192]{1,0:T(8,128)(2,1)S(1)} copy-done((bf16[1024,8192]{1,0:T(8,128)(2,1)S(1)}, bf16[1024,8192]{1,0:T(8,128)(2,1)}, u32[]{:S(2)}) %copy-start.2) | copy-done | bytes 16777240
  41.1 4.2 %collective-permute-start.8 = (bf16[144,1024]{1,0:T(8,128)(2,1)S(1)}, bf16[144,1024]{1,0:T(8,128)(2,1)S(1)}, u32[]{:S(2)}, u32[]{:S(2)}) collective-permute-start(bf16[144,1024]{1,0:T(8,128)(2,1)S(1)} %shard_map.62), channel_id=1, source_target_pairs={{8,12},{9,13},{10,14},{11,15},{12,8},{13,9},{14,10},{15,11},{24,28... | collective-permute-start | bytes 884744 | tf_op jit(solution)/shard_map/ppermute | solution.py:312
  45.3 7.3 %collective-permute-done.8.refs_3_.refs_0_ = bf16[144,1024]{1,0:T(8,128)(2,1)S(1)} collective-permute-done((bf16[144,1024]{1,0:T(8,128)(2,1)S(1)}, bf16[144,1024]{1,0:T(8,128)(2,1)S(1)}, u32[]{:S(2)}, u32[]{:S(2)}) %collective-permute-start.8) | collective-permute-done | bytes 294944 | tf_op jit(solution)/shard_map/ppermute | solution.py:312
  52.9 5.8 %copy-done.3 = bf16[1024,8192]{1,0:T(8,128)(2,1)S(1)} copy-done((bf16[1024,8192]{1,0:T(8,128)(2,1)S(1)}, bf16[1024,8192]{1,0:T(8,128)(2,1)}, u32[]{:S(2)}) %copy-start.3) | copy-done | bytes 16777240
  77.0 5.8 %copy-done.4 = bf16[1024,8192]{1,0:T(8,128)(2,1)S(1)} copy-done((bf16[1024,8192]{1,0:T(8,128)(2,1)S(1)}, bf16[1024,8192]{1,0:T(8,128)(2,1)}, u32[]{:S(2)}) %copy-start.4) | copy-done | bytes 16777240
  94.0 7.4 %collective-permute-done.23.refs_0_ = bf16[144,1024]{1,0:T(8,128)(2,1)S(1)} collective-permute-done((bf16[144,1024]{1,0:T(8,128)(2,1)S(1)}, bf16[144,1024]{1,0:T(8,128)(2,1)S(1)}, u32[]{:S(2)}, u32[]{:S(2)}) %collective-permute-start.23) | collective-permute-done | bytes 294944 | tf_op jit(solution)/shard_map/ppermute | solution.py:312
  110.6 5.1 %collective-permute-start.27 = (bf16[144,1024]{1,0:T(8,128)(2,1)}, bf16[144,1024]{1,0:T(8,128)(2,1)}, u32[]{:S(2)}, u32[]{:S(2)}) collective-permute-start(bf16[144,1024]{1,0:T(8,128)(2,1)} %shard_map.70), channel_id=1, source_target_pairs={{24,28},{25,29},{26,30},{27,31},{28,24},{29,25},{30,26},{31,27}} | collective-permute-start | bytes 884744 | tf_op jit(solution)/shard_map/ppermute | solution.py:312
  115.7 15.7 %conditional.2 = (f32[128,1024]{1,0:T(8,128)}) conditional(s32[]{:T(128)} %convert_element_type.63, () %tuple.24, (f32[1,1024]{1,0:T(1,128)S(1)}, s32[]{:T(128)}, bf16[1024,8192]{1,0:T(8,128)(2,1)}, bf16[144,1024]{1,0:T(8,128)(2,1)}, bf16[144,1024]{1,0:T(8,128)(2,1)}, /*index=5*/bf16[144,1024]{1,0:T(8,128)(2,1)}, bf16[144,1024]{1,0:T(8,128)(2,1)}, ...), branch_computations={%region_1.2_spmd, %region_2.3_spmd} | conditional | flops 2147614720 | bytes 85987512 | solution.py:367
  116.0 5.8 %copy-done.8 = bf16[1024,8192]{1,0:T(8,128)(2,1)S(1)} copy-done((bf16[1024,8192]{1,0:T(8,128)(2,1)S(1)}, bf16[1024,8192]{1,0:T(8,128)(2,1)}, u32[]{:S(2)}) %copy-start.8) | copy-done | bytes 16777240 | tf_op jit(solution)/shard_map/cond
  121.8 6.5 %branch_1_fun.3 = (f32[1024,128]{1,0:T(8,128)S(1)}, f32[8,128]{1,0:T(8,128)}) custom-call(s32[8]{0:T(128)S(1)} %stack.34.meta_ref, bf16[1024,8192]{1,0:T(8,128)(2,1)S(1)} %copy-done.8, bf16[144,1024]{1,0:T(8,128)(2,1)} %get-tuple-element.52.refs_0_, bf16[144,1024]{1,0:T(8,128)(2,1)} %get-tuple-element.53.refs_1_, ...), custom_call_target="tpu_custom_call" | custom-call | flops 2147483648 | bytes 16777216 | tf_op jit(solution)/shard_map/cond/branch_1_fun/pallas_call | solution.py:225
  160.7 5.7 %collective-permute-done.31 = bf16[144,1024]{1,0:T(8,128)(2,1)} collective-permute-done((bf16[144,1024]{1,0:T(8,128)(2,1)S(1)}, bf16[144,1024]{1,0:T(8,128)(2,1)}, u32[]{:S(2)}, u32[]{:S(2)}) %collective-permute-start.31) | collective-permute-done | bytes 294944 | tf_op jit(solution)/shard_map/ppermute | solution.py:312
  176.9 5.8 %copy-done.5 = bf16[1024,8192]{1,0:T(8,128)(2,1)S(1)} copy-done((bf16[1024,8192]{1,0:T(8,128)(2,1)S(1)}, bf16[1024,8192]{1,0:T(8,128)(2,1)}, u32[]{:S(2)}) %copy-start.5) | copy-done | bytes 16777240
  188.5 4.3 %shard_map.74 = (bf16[128,1024]{1,0:T(8,128)(2,1)}, bf16[128,1024]{1,0:T(8,128)(2,1)S(1)}, bf16[128,1024]{1,0:T(8,128)(2,1)S(1)}) custom-call(s32[5]{0:T(128)S(1)} %stack.213.meta_ref, bf16[1024,8192]{1,0:T(8,128)(2,1)S(1)} %copy-done.5, bf16[144,1024]{1,0:T(8,128)(2,1)S(1)} %collective-permute-done.32.refs_0_, ...), custom_call_target="tpu_custom_call" | custom-call | flops 1073741824 | bytes 8388608 | tf_op jit(solution)/shard_map/pallas_call | solution.py:281
  193.6 23.4 %conditional.3 = (bf16[144,1024]{1,0:T(8,128)(2,1)}, bf16[144,1024]{1,0:T(8,128)(2,1)S(1)}, bf16[144,1024]{1,0:T(8,128)(2,1)S(1)}, bf16[144,1024]{1,0:T(8,128)(2...) conditional(s32[]{:T(128)} %convert_element_type.63, () %tuple.23, ...), branch_computations={%region_4.5_spmd, %region_5.6_spmd} | conditional | flops 2147483648 | bytes 219152640 | solution.py:387
  193.6 5.8 %copy-done.9 = bf16[1024,8192]{1,0:T(8,128)(2,1)} copy-done((bf16[1024,8192]{1,0:T(8,128)(2,1)}, bf16[1024,8192]{1,0:T(8,128)(2,1)S(1)}, u32[]{:S(2)}) %copy-start.9) | copy-done | bytes 16777240 | tf_op jit(solution)/shard_map/cond
  199.4 5.8 %copy-done.10 = bf16[1024,8192]{1,0:T(8,128)(2,1)S(1)} copy-done((bf16[1024,8192]{1,0:T(8,128)(2,1)S(1)}, bf16[1024,8192]{1,0:T(8,128)(2,1)}, u32[]{:S(2)}) %copy-start.10) | copy-done | bytes 16777240 | tf_op jit(solution)/shard_map/cond
  208.4 5.8 %copy-done.11 = bf16[1024,8192]{1,0:T(8,128)(2,1)S(1)} copy-done((bf16[1024,8192]{1,0:T(8,128)(2,1)S(1)}, bf16[1024,8192]{1,0:T(8,128)(2,1)}, u32[]{:S(2)}) %copy-start.11) | copy-done | bytes 16777240 | tf_op jit(solution)/shard_map/cond
  237.1 5.8 %copy-done.6 = bf16[1024,8192]{1,0:T(8,128)(2,1)S(1)} copy-done((bf16[1024,8192]{1,0:T(8,128)(2,1)S(1)}, bf16[1024,8192]{1,0:T(8,128)(2,1)}, u32[]{:S(2)}) %copy-start.6) | copy-done | bytes 16777240
  251.1 4.5 %collective-permute-start.53 = (bf16[144,1024]{1,0:T(8,128)(2,1)S(1)}, bf16[144,1024]{1,0:T(8,128)(2,1)S(1)}, u32[]{:S(2)}, u32[]{:S(2)}) collective-permute-start(bf16[144,1024]{1,0:T(8,128)(2,1)S(1)} %get-tuple-element.214), channel_id=1, source_target_pairs={{8,12},{9,13},{10,14},{11,15},{12,8},{13,9},{14,10},{15,11},{24,28... | collective-permute-start | bytes 884744 | tf_op jit(solution)/shard_map/ppermute | solution.py:312
  272.3 5.8 %copy-done.7 = bf16[1024,8192]{1,0:T(8,128)(2,1)S(1)} copy-done((bf16[1024,8192]{1,0:T(8,128)(2,1)S(1)}, bf16[1024,8192]{1,0:T(8,128)(2,1)}, u32[]{:S(2)}) %copy-start.7) | copy-done | bytes 16777240
  (244 shorter events, 159.5 us)
Async XLA Ops:
  21.3 17.5 %collective-permute-start.4 = (bf16[144,1024]{1,0:T(8,128)(2,1)S(1)}, bf16[144,1024]{1,0:T(8,128)(2,1)S(1)}, u32[]{:S(2)}, u32[]{:S(2)}) collective-permute-start(bf16[144,1024]{1,0:T(8,128)(2,1)S(1)} %get-tuple-element.157), channel_id=1, source_target_pairs={{0,8},{1,9},{2,10},{3,11},{4,12},{5,13},{6,14},{7,15}} | collective-permute-start | bytes 884744 | tf_op jit(solution)/shard_map/ppermute | solution.py:312
  21.9 17.5 %collective-permute-start.5 = (bf16[144,1024]{1,0:T(8,128)(2,1)S(1)}, bf16[144,1024]{1,0:T(8,128)(2,1)S(1)}, u32[]{:S(2)}, u32[]{:S(2)}) collective-permute-start(bf16[144,1024]{1,0:T(8,128)(2,1)S(1)} %get-tuple-element.158), channel_id=1, source_target_pairs={{0,11},{1,10},{2,9},{3,8},{4,15},{5,14},{6,13},{7,12},{24,27},{25,... | collective-permute-start | bytes 884744 | tf_op jit(solution)/shard_map/ppermute | solution.py:312
  26.1 14.1 %collective-permute-start.6 = (bf16[144,1024]{1,0:T(8,128)(2,1)S(1)}, bf16[144,1024]{1,0:T(8,128)(2,1)S(1)}, u32[]{:S(2)}, u32[]{:S(2)}) collective-permute-start(bf16[144,1024]{1,0:T(8,128)(2,1)S(1)} %get-tuple-element.159), channel_id=1, source_target_pairs={{0,10},{1,11},{2,8},{3,9},{4,14},{5,15},{6,12},{7,13},{24,26},{25,... | collective-permute-start | bytes 884744 | tf_op jit(solution)/shard_map/ppermute | solution.py:312
  84.6 16.8 %collective-permute-start.23 = (bf16[144,1024]{1,0:T(8,128)(2,1)S(1)}, bf16[144,1024]{1,0:T(8,128)(2,1)S(1)}, u32[]{:S(2)}, u32[]{:S(2)}) collective-permute-start(bf16[144,1024]{1,0:T(8,128)(2,1)S(1)} %get-tuple-element.175), channel_id=1, source_target_pairs={{16,24},{17,25},{18,26},{19,27},{20,28},{21,29},{22,30},{23,31}} | collective-permute-start | bytes 884744 | tf_op jit(solution)/shard_map/ppermute | solution.py:312
  85.9 20.6 %collective-permute-start.24 = (bf16[144,1024]{1,0:T(8,128)(2,1)S(1)}, bf16[144,1024]{1,0:T(8,128)(2,1)S(1)}, u32[]{:S(2)}, u32[]{:S(2)}) collective-permute-start(bf16[144,1024]{1,0:T(8,128)(2,1)S(1)} %get-tuple-element.176), channel_id=1, source_target_pairs={{16,27},{17,26},{18,25},{19,24},{20,31},{21,30},{22,29},{23,28}} | collective-permute-start | bytes 884744 | tf_op jit(solution)/shard_map/ppermute | solution.py:312
  87.2 21.3 %collective-permute-start.25 = (bf16[144,1024]{1,0:T(8,128)(2,1)S(1)}, bf16[144,1024]{1,0:T(8,128)(2,1)S(1)}, u32[]{:S(2)}, u32[]{:S(2)}) collective-permute-start(bf16[144,1024]{1,0:T(8,128)(2,1)S(1)} %get-tuple-element.177), channel_id=1, source_target_pairs={{16,26},{17,27},{18,24},{19,25},{20,30},{21,31},{22,28},{23,29}} | collective-permute-start | bytes 884744 | tf_op jit(solution)/shard_map/ppermute | solution.py:312
  88.5 21.3 %collective-permute-start.26 = (bf16[144,1024]{1,0:T(8,128)(2,1)S(1)}, bf16[144,1024]{1,0:T(8,128)(2,1)S(1)}, u32[]{:S(2)}, u32[]{:S(2)}) collective-permute-start(bf16[144,1024]{1,0:T(8,128)(2,1)S(1)} %get-tuple-element.178), channel_id=1, source_target_pairs={{16,25},{17,24},{18,27},{19,26},{20,29},{21,28},{22,31},{23,30}} | collective-permute-start | bytes 884744 | tf_op jit(solution)/shard_map/ppermute | solution.py:312
  92.7 40.1 %collective-permute-start.19 = (bf16[272,1024]{1,0:T(8,128)(2,1)}, bf16[272,1024]{1,0:T(8,128)(2,1)S(1)}, u32[]{:S(2)}, u32[]{:S(2)}) collective-permute-start(bf16[272,1024]{1,0:T(8,128)(2,1)} %get-tuple-element.171), channel_id=1, source_target_pairs={{16,24},{17,25},{18,26},{19,27},{20,28},{21,29},{22,30},{23,31}} | collective-permute-start | bytes 1671176 | tf_op jit(solution)/shard_map/ppermute | solution.py:312
  101.4 30.0 %collective-permute-start.20 = (bf16[144,1024]{1,0:T(8,128)(2,1)}, bf16[144,1024]{1,0:T(8,128)(2,1)S(1)}, u32[]{:S(2)}, u32[]{:S(2)}) collective-permute-start(bf16[144,1024]{1,0:T(8,128)(2,1)} %get-tuple-element.172), channel_id=1, source_target_pairs={{16,27},{17,26},{18,25},{19,24},{20,31},{21,30},{22,29},{23,28}} | collective-permute-start | bytes 884744 | tf_op jit(solution)/shard_map/ppermute | solution.py:312
  106.5 24.9 %collective-permute-start.21 = (bf16[144,1024]{1,0:T(8,128)(2,1)}, bf16[144,1024]{1,0:T(8,128)(2,1)S(1)}, u32[]{:S(2)}, u32[]{:S(2)}) collective-permute-start(bf16[144,1024]{1,0:T(8,128)(2,1)} %get-tuple-element.173), channel_id=1, source_target_pairs={{16,26},{17,27},{18,24},{19,25},{20,30},{21,31},{22,28},{23,29}} | collective-permute-start | bytes 884744 | tf_op jit(solution)/shard_map/ppermute | solution.py:312
  108.5 23.6 %collective-permute-start.22 = (bf16[144,1024]{1,0:T(8,128)(2,1)}, bf16[144,1024]{1,0:T(8,128)(2,1)S(1)}, u32[]{:S(2)}, u32[]{:S(2)}) collective-permute-start(bf16[144,1024]{1,0:T(8,128)(2,1)} %get-tuple-element.174), channel_id=1, source_target_pairs={{16,25},{17,24},{18,27},{19,26},{20,29},{21,28},{22,31},{23,30}} | collective-permute-start | bytes 884744 | tf_op jit(solution)/shard_map/ppermute | solution.py:312
  110.6 22.2 %collective-permute-start.27 = (bf16[144,1024]{1,0:T(8,128)(2,1)}, bf16[144,1024]{1,0:T(8,128)(2,1)}, u32[]{:S(2)}, u32[]{:S(2)}) collective-permute-start(bf16[144,1024]{1,0:T(8,128)(2,1)} %shard_map.70), channel_id=1, source_target_pairs={{24,28},{25,29},{26,30},{27,31},{28,24},{29,25},{30,26},{31,27}} | collective-permute-start | bytes 884744 | tf_op jit(solution)/shard_map/ppermute | solution.py:312
  153.5 23.4 %collective-permute-start.36 = (bf16[272,1024]{1,0:T(8,128)(2,1)}, bf16[272,1024]{1,0:T(8,128)(2,1)S(1)}, u32[]{:S(2)}, u32[]{:S(2)}) collective-permute-start(bf16[272,1024]{1,0:T(8,128)(2,1)} %get-tuple-element.186), channel_id=1, source_target_pairs={{24,16},{25,17},{26,18},{27,19},{28,20},{29,21},{30,22},{31,23}} | collective-permute-start | bytes 1671176 | tf_op jit(solution)/shard_map/ppermute | solution.py:312
  166.4 22.0 %collective-permute-start.32 = (bf16[144,1024]{1,0:T(8,128)(2,1)}, bf16[144,1024]{1,0:T(8,128)(2,1)S(1)}, u32[]{:S(2)}, u32[]{:S(2)}) collective-permute-start(bf16[144,1024]{1,0:T(8,128)(2,1)} %collective-permute-done.31), channel_id=1, source_target_pairs={{24,16},{25,17},{26,18},{27,19},{28,20},{29,21},{30,22},{31,23}} | collective-permute-start | bytes 884744 | tf_op jit(solution)/shard_map/ppermute | solution.py:312
  168.5 20.0 %collective-permute-start.33 = (bf16[144,1024]{1,0:T(8,128)(2,1)}, bf16[144,1024]{1,0:T(8,128)(2,1)S(1)}, u32[]{:S(2)}, u32[]{:S(2)}) collective-permute-start(bf16[144,1024]{1,0:T(8,128)(2,1)} %collective-permute-done.31), channel_id=1, source_target_pairs={{24,19},{25,18},{26,17},{27,16},{28,23},{29,22},{30,21},{31,20}} | collective-permute-start | bytes 884744 | tf_op jit(solution)/shard_map/ppermute | solution.py:312
  170.5 18.0 %collective-permute-start.34 = (bf16[144,1024]{1,0:T(8,128)(2,1)}, bf16[144,1024]{1,0:T(8,128)(2,1)}, u32[]{:S(2)}, u32[]{:S(2)}) collective-permute-start(bf16[144,1024]{1,0:T(8,128)(2,1)} %collective-permute-done.31), channel_id=1, source_target_pairs={{24,18},{25,19},{26,16},{27,17},{28,22},{29,23},{30,20},{31,21}} | collective-permute-start | bytes 884744 | tf_op jit(solution)/shard_map/ppermute | solution.py:312
  173.5 15.0 %collective-permute-start.35 = (bf16[144,1024]{1,0:T(8,128)(2,1)}, bf16[144,1024]{1,0:T(8,128)(2,1)}, u32[]{:S(2)}, u32[]{:S(2)}) collective-permute-start(bf16[144,1024]{1,0:T(8,128)(2,1)} %collective-permute-done.31), channel_id=1, source_target_pairs={{24,17},{25,16},{26,19},{27,18},{28,21},{29,20},{30,23},{31,22}} | collective-permute-start | bytes 884744 | tf_op jit(solution)/shard_map/ppermute | solution.py:312
  192.8 24.2 %collective-permute-start.40 = (bf16[128,1024]{1,0:T(8,128)(2,1)}, bf16[128,1024]{1,0:T(8,128)(2,1)S(1)}, u32[]{:S(2)}, u32[]{:S(2)}) collective-permute-start(bf16[128,1024]{1,0:T(8,128)(2,1)} %get-tuple-element.189), channel_id=1, source_target_pairs={{16,0},{17,1},{18,2},{19,3},{20,4},{21,5},{22,6},{23,7}} | collective-permute-start | bytes 786440 | tf_op jit(solution)/shard_map/ppermute | solution.py:312
  219.0 18.1 %collective-permute-start.46 = (bf16[272,1024]{1,0:T(8,128)(2,1)}, bf16[272,1024]{1,0:T(8,128)(2,1)S(1)}, u32[]{:S(2)}, u32[]{:S(2)}) collective-permute-start(bf16[272,1024]{1,0:T(8,128)(2,1)} %get-tuple-element.196), channel_id=1, source_target_pairs={{0,8},{1,9},{2,10},{3,11},{4,12},{5,13},{6,14},{7,15}} | collective-permute-start | bytes 1671176 | tf_op jit(solution)/shard_map/ppermute | solution.py:312
  229.7 16.1 %collective-permute-start.42 = (bf16[144,1024]{1,0:T(8,128)(2,1)}, bf16[144,1024]{1,0:T(8,128)(2,1)S(1)}, u32[]{:S(2)}, u32[]{:S(2)}) collective-permute-start(bf16[144,1024]{1,0:T(8,128)(2,1)} %collective-permute-done.41), channel_id=1, source_target_pairs={{0,8},{1,9},{2,10},{3,11},{4,12},{5,13},{6,14},{7,15}} | collective-permute-start | bytes 884744 | tf_op jit(solution)/shard_map/ppermute | solution.py:312
  230.4 15.4 %collective-permute-start.43 = (bf16[144,1024]{1,0:T(8,128)(2,1)}, bf16[144,1024]{1,0:T(8,128)(2,1)S(1)}, u32[]{:S(2)}, u32[]{:S(2)}) collective-permute-start(bf16[144,1024]{1,0:T(8,128)(2,1)} %collective-permute-done.41), channel_id=1, source_target_pairs={{0,11},{1,10},{2,9},{3,8},{4,15},{5,14},{6,13},{7,12}} | collective-permute-start | bytes 884744 | tf_op jit(solution)/shard_map/ppermute | solution.py:312
  250.4 22.0 %collective-permute-start.58 = (bf16[272,1024]{1,0:T(8,128)(2,1)}, bf16[272,1024]{1,0:T(8,128)(2,1)S(1)}, u32[]{:S(2)}, u32[]{:S(2)}) collective-permute-start(bf16[272,1024]{1,0:T(8,128)(2,1)} %get-tuple-element.216), channel_id=1, source_target_pairs={{8,0},{9,1},{10,2},{11,3},{12,4},{13,5},{14,6},{15,7}} | collective-permute-start | bytes 1671176 | tf_op jit(solution)/shard_map/ppermute | solution.py:312
  264.0 17.0 %collective-permute-start.54 = (bf16[144,1024]{1,0:T(8,128)(2,1)S(1)}, bf16[144,1024]{1,0:T(8,128)(2,1)S(1)}, u32[]{:S(2)}, u32[]{:S(2)}) collective-permute-start(bf16[144,1024]{1,0:T(8,128)(2,1)S(1)} %collective-permute-done.53.refs_3_), channel_id=1, source_target_pairs={{8,0},{9,1},{10,2},{11,3},{12,4},{13,5},{14,6},{15,7}} | collective-permute-start | bytes 884744 | tf_op jit(solution)/shard_map/ppermute | solution.py:312
  266.3 14.7 %collective-permute-start.55 = (bf16[144,1024]{1,0:T(8,128)(2,1)S(1)}, bf16[144,1024]{1,0:T(8,128)(2,1)S(1)}, u32[]{:S(2)}, u32[]{:S(2)}) collective-permute-start(bf16[144,1024]{1,0:T(8,128)(2,1)S(1)} %collective-permute-done.53.refs_3_), channel_id=1, source_target_pairs={{8,3},{9,2},{10,1},{11,0},{12,7},{13,6},{14,5},{15,4}} | collective-permute-start | bytes 884744 | tf_op jit(solution)/shard_map/ppermute | solution.py:312
  (84 other events, 734.2 us)

commit v6 on v5

v6 whole, which is shorter than its diff:
```python
import jax
import jax.numpy as jnp
from jax import lax
from jax.experimental import pallas as pl
from jax.experimental.pallas import tpu as pltpu
from jax.sharding import PartitionSpec as P

EPSILON = 1e-05
MIB = 1 << 20
TAIL = 16
LANES = 128
SMEM_SPEC = pl.BlockSpec(memory_space=pltpu.SMEM)
VMEM_SPEC = pl.BlockSpec(memory_space=pltpu.VMEM)


def local_kernel(kernel, place, operands, out_shapes, limit=12 * MIB, cost=None, **options):
    def body(place_ref, *refs):
        kernel(place_ref[0], place_ref[1], *refs)

    options.setdefault("in_specs", [SMEM_SPEC] + [VMEM_SPEC] * len(operands))
    call = pl.pallas_call(
        body,
        out_shape=out_shapes,
        out_specs=[VMEM_SPEC] * len(out_shapes),
        compiler_params=pltpu.CompilerParams(vmem_limit_bytes=limit),
        cost_estimate=cost,
        **options,
    )
    return list(call(place, *operands))


def bf16(*shape):
    return jax.ShapeDtypeStruct(shape, jnp.bfloat16)


def f32(*shape):
    return jax.ShapeDtypeStruct(shape, jnp.float32)


def as_line(column):
    return jnp.broadcast_to(column, (column.shape[0], LANES)).T[:1]


def as_column(line):
    return jnp.broadcast_to(line, (LANES, line.shape[1])).T[:, :1]


def row_sum(value):
    return jnp.sum(value, axis=1, keepdims=True).astype(jnp.bfloat16).astype(jnp.float32)


def tail_sum(chunk_refs, rows):
    total = chunk_refs[0][rows : rows + TAIL, :rows].astype(jnp.float32)
    for chunk in chunk_refs[1:]:
        total = total + chunk[rows : rows + TAIL, :rows].astype(jnp.float32)
    return total


def matmul_cost(rows, width, count):
    return pl.CostEstimate(
        flops=2 * rows * width * width * count,
        bytes_accessed=2 * width * width * count,
        transcendentals=0,
    )


def block_columns(tp, code, width, start=0, size=None):
    size = size or width
    return pl.ds(pl.multiple_of((tp ^ code) * width + start, size), size)


def load(place, weights, cot):
    rows, width = cot.shape

    def kernel(tp, section, w_ref, cot_ref, out_ref, chunk_ref, done):
        copy = pltpu.make_async_copy(w_ref, out_ref, done)
        copy.start()
        chunk_ref[:rows, :] = cot_ref[...]
        chunk_ref[rows:, :] = jnp.zeros((TAIL, width), jnp.bfloat16)
        copy.wait()

    return local_kernel(
        kernel,
        place,
        [pltpu.with_memory_space_constraint(weights, pltpu.HBM), cot],
        [pltpu.VMEM(weights.shape, weights.dtype), bf16(rows + TAIL, width)],
        limit=2 * MIB,
        in_specs=[SMEM_SPEC, pl.BlockSpec(memory_space=pltpu.HBM), VMEM_SPEC],
        scratch_shapes=[pltpu.SemaphoreType.DMA],
        cost=pl.CostEstimate(flops=0, bytes_accessed=2 * weights.size, transcendentals=0),
    )


def forward_blocks(place, a, gain_row, w_rows, codes, pack=False, only=None, other=None, other_at=None):
    rows, width = a.shape
    chunk_rows = rows + TAIL
    tile = min(width, 512)
    others = [] if other is None else [other]

    def kernel(tp, section, a_ref, gain_ref, w_ref, *refs):
        out_refs = refs[len(others) :]

        def work():
            wide = a_ref[...].astype(jnp.float32)
            scaled = (wide * gain_ref[...]).astype(jnp.bfloat16)
            for code, out_ref in zip(codes, out_refs):
                for start in range(0, width, tile):
                    partial = jnp.dot(
                        scaled,
                        w_ref[:, block_columns(tp, code, width, start, tile)],
                        preferred_element_type=jnp.float32,
                    )
                    out_ref[:rows, start : start + tile] = partial.astype(jnp.bfloat16)
            line = as_line(jnp.sum(wide * wide, axis=1, keepdims=True))
            row_ids = lax.broadcasted_iota(jnp.int32, (TAIL, rows), 0)
            own_row = jnp.where(row_ids == tp % TAIL, jnp.broadcast_to(line, (TAIL, rows)), 0.0)
            for out_ref in out_refs:
                out_ref[rows:chunk_rows, :] = jnp.zeros((TAIL, width), jnp.bfloat16)
                out_ref[rows:chunk_rows, :rows] = own_row.astype(jnp.bfloat16)
            if pack:
                out_refs[0][chunk_rows:, :] = a_ref[...]

        if only is not None:
            pl.when(section == only)(work)
        else:
            work()
        if others:

            @pl.when(section == other_at)
            def _():
                for out_ref in out_refs:
                    out_ref[...] = refs[0][...]

    shapes = [bf16(chunk_rows, width)] * len(codes)
    if pack:
        shapes[0] = bf16(chunk_rows + rows, width)
    return local_kernel(
        kernel,
        place,
        [a, gain_row, w_rows] + others,
        shapes,
        cost=matmul_cost(rows, width, len(codes)),
    )


def add_chunks(place, chunks, other=None, other_at=None):
    def kernel(tp, section, *refs):
        total = refs[0][...].astype(jnp.float32)
        for chunk in refs[1 : len(chunks)]:
            total = total + chunk[...].astype(jnp.float32)
        refs[-1][...] = total.astype(refs[-1].dtype)
        if other is not None:

            @pl.when(section == other_at)
            def _():
                refs[-1][...] = refs[len(chunks)][...]

    operands = chunks + ([] if other is None else [other])
    shape = jax.ShapeDtypeStruct(chunks[0].shape, chunks[0].dtype)
    return local_kernel(kernel, place, operands, [shape])[0]


def finish_forward(place, first, chunks, a, full_width):
    chunk_rows, width = chunks[0].shape
    rows = chunk_rows - TAIL
    given = [] if a is None else [a]

    def kernel(tp, section, first_ref, *refs):
        chunk_refs, (out_ref, branch_ref, rms_ref) = refs[: len(chunks)], refs[-3:]
        source = first_ref[chunk_rows:, :] if a is None else refs[len(chunks)][...]
        branch = first_ref[:rows, :].astype(jnp.float32)
        for chunk in chunk_refs:
            branch = branch + chunk[:rows, :].astype(jnp.float32)
        squares = jnp.sum(tail_sum((first_ref,) + chunk_refs, rows), axis=0, keepdims=True)
        inv_rms = lax.rsqrt(as_column(squares) / full_width + EPSILON)
        out_ref[...] = (source.astype(jnp.float32) + inv_rms * branch).astype(jnp.bfloat16)
        branch_ref[...] = branch
        rms_ref[...] = jnp.broadcast_to(inv_rms, (rows, LANES))

    return local_kernel(
        kernel,
        place,
        [first] + chunks + given,
        [bf16(rows, width), f32(rows, width), f32(rows, LANES)],
    )


def store_gradient_chunks(out_refs, grad, act_ref, branch_ref, rms_ref):
    rows, width = grad.shape
    chunk_rows = rows + TAIL
    dots = jnp.sum(grad.astype(jnp.float32) * branch_ref[...], axis=1, keepdims=True)
    rms_line = rms_ref[...].T[:1]
    rms_high = rms_line.astype(jnp.bfloat16).astype(jnp.float32)
    row_ids = lax.broadcasted_iota(jnp.int32, (TAIL, rows), 0)
    tile = jnp.where(row_ids == 0, as_line(dots), 0.0)
    tile = jnp.where(row_ids == 1, rms_high, tile)
    tile = jnp.where(row_ids == 2, rms_line - rms_high, tile).astype(jnp.bfloat16)
    for out_ref in out_refs:
        out_ref[:rows, :] = grad
        out_ref[rows:chunk_rows, :] = jnp.zeros((TAIL, width), jnp.bfloat16)
        out_ref[rows:chunk_rows, :rows] = tile
    out_refs[-1][chunk_rows:, :] = act_ref[...]


def gradient_chunks(place, upstream, passed, others, other_at):
    rows, width = upstream.shape
    replaced = [other for other in others if other is not None]

    def kernel(tp, section, up_ref, act_ref, branch_ref, rms_ref, *refs):
        other_refs, out_refs = list(refs[: len(replaced)]), refs[len(replaced) :]
        store_gradient_chunks(out_refs, up_ref[...], act_ref, branch_ref, rms_ref)
        if replaced:

            @pl.when(section == other_at)
            def _():
                for other, out_ref in zip(others, out_refs):
                    if other is not None:
                        out_ref[...] = other_refs.pop(0)[...]

    shapes = [bf16(rows + TAIL, width)] * len(others) + [bf16(2 * rows + TAIL, width)]
    return local_kernel(kernel, place, [upstream, *passed, *replaced], shapes)


def row_statistics(place, a, back):
    rows, _ = a.shape

    def kernel(tp, section, a_ref, back_ref, out_ref):
        wide = a_ref[...].astype(jnp.float32)
        row_ids = lax.broadcasted_iota(jnp.int32, (8, rows), 0)
        lines = jnp.where(row_ids == 0, as_line(row_sum(wide * wide)), 0.0)
        out_ref[...] = jnp.where(row_ids == 1, as_line(row_sum(wide * back_ref[...])), lines)

    return local_kernel(kernel, place, [a, back], [f32(8, rows)])[0]


def last_gradient(place, cot, back, a, sums, passed, full_width):
    rows, width = a.shape

    def kernel(tp, section, cot_ref, back_ref, a_ref, sums_ref, act_ref, branch_ref, rms_ref, grad_ref, *out_refs):
        squares = as_column(sums_ref[0:1, :])
        row_dot = as_column(sums_ref[1:2, :])
        rms = lax.rsqrt(squares / full_width + EPSILON)
        grad = (
            cot_ref[...].astype(jnp.float32)
            + rms * back_ref[...]
            - (rms * rms * rms / full_width * row_dot) * a_ref[...].astype(jnp.float32)
        ).astype(jnp.bfloat16)
        grad_ref[...] = grad
        store_gradient_chunks(out_refs, grad, act_ref, branch_ref, rms_ref)

    return local_kernel(
        kernel,
        place,
        [cot, back, a, sums, *passed],
        [bf16(rows, width), bf16(rows + TAIL, width), bf16(2 * rows + TAIL, width)],
    )


def block_products(tp, w_ref, codes, chunk_refs, rows, start, tile):
    width = w_ref.shape[0]
    total = None
    for code, chunk in zip(codes, chunk_refs):
        product = lax.dot_general(
            w_ref[start : start + tile, block_columns(tp, code, width)],
            chunk[:rows, :],
            (((1,), (1,)), ((), ())),
            preferred_element_type=jnp.float32,
        )
        total = product if total is None else total + product
    return total


def scaled_back(place, chunks, w_rows, codes, gain_row, only):
    width = w_rows.shape[0]
    rows = chunks[0].shape[0] - TAIL
    tile = min(width, 256)

    def kernel(tp, section, w_ref, gain_ref, *refs):
        @pl.when(section == only)
        def _():
            for start in range(0, width, tile):
                products = block_products(tp, w_ref, codes, refs[:-1], rows, start, tile)
                columns = slice(start, start + tile)
                refs[-1][:, columns] = gain_ref[:, columns] * products.T

    return local_kernel(
        kernel,
        place,
        [w_rows, gain_row] + chunks,
        [f32(rows, width)],
        cost=matmul_cost(rows, width, len(codes)),
    )[0]


def backward_half(place, chunks, w_rows, codes, rows):
    width = w_rows.shape[0]
    tile = min(width, 256)

    def kernel(tp, section, w_ref, *refs):
        chunk_refs, (out_ref, sum_ref) = refs[:-2], refs[-2:]
        for start in range(0, width, tile):
            out_ref[start : start + tile, :] = block_products(
                tp, w_ref, codes, chunk_refs, rows, start, tile
            )
        sum_ref[...] = tail_sum(chunk_refs, rows)

    return local_kernel(
        kernel,
        place,
        [w_rows] + chunks,
        [f32(width, rows), f32(TAIL, rows)],
        cost=matmul_cost(rows, width, len(codes)),
    )


def finish_backward(place, chunks, w_rows, codes, half, pack, gain_row, a, full_width, results, at, last_output=None, last=None):
    rows, width = a.shape
    chunk_rows = rows + TAIL
    count = len(codes)
    tile = min(width, 256)
    given = [] if last_output is None else [last_output]

    def kernel(tp, section, w_ref, *refs):
        chunk_refs = refs[:count]
        half_ref, sum_ref, pack_ref, gain_ref, a_ref, *old_refs = refs[count : count + 7]
        out_ref, *new_refs = refs[-3:]
        row_dot = as_column((sum_ref[...] + tail_sum(chunk_refs, rows))[:1])
        tail = pack_ref[rows:chunk_rows, :rows].astype(jnp.float32)
        rms = as_column(tail[1:2] + tail[2:3])
        scale = rms * rms * rms / full_width * row_dot
        for start in range(0, width, tile):
            products = block_products(tp, w_ref, codes, chunk_refs, rows, start, tile)
            back = (products + half_ref[start : start + tile, :]).T
            columns = slice(start, start + tile)
            out_ref[:, columns] = (
                pack_ref[:rows, columns].astype(jnp.float32)
                + rms * gain_ref[:, columns] * back
                - scale * a_ref[:, columns].astype(jnp.float32)
            ).astype(jnp.bfloat16)

        @pl.when(section == at)
        def _():
            new_refs[0][...] = out_ref[...]
            new_refs[1][...] = pack_ref[chunk_rows:, :]

        @pl.when(section != at)
        def _():
            for new, old in zip(new_refs, old_refs):
                new[...] = old[...]

        if given:

            @pl.when(section == last)
            def _():
                new_refs[1][...] = refs[count + 7][...]

    return local_kernel(
        kernel,
        place,
        [w_rows, *chunks, *half, pack, gain_row, a, *results] + given,
        [bf16(rows, width)] * 3,
        cost=matmul_cost(rows, width, count),
    )


def on_device(inputs, cotangent, weights, gains):
    section_count = lax.axis_size("section")
    tp_count = lax.axis_size("tp")
    micro_count, row_count, width = inputs.shape
    rows = micro_count * row_count
    full_width = weights.shape[2]
    last = section_count - 1
    place = jnp.stack([lax.axis_index("tp"), lax.axis_index("section")])
    across = tp_count // 2
    near = list(range(across - 1, 0, -1))
    near_codes = [0] + near
    far_codes = [across ^ e for e in near_codes]
    inside = [(last, last)]

    def across_route(beside, riding):
        if beside == last:
            return [(1, 1)] + inside
        return [(beside, beside)] + (inside if riding else [])

    def send(value, routes, step=0):
        pairs = [
            (source * tp_count + t, target * tp_count + (t ^ step))
            for source, target in routes
            for t in range(tp_count)
        ]
        return lax.ppermute(value, ("section", "tp"), pairs)

    cot = cotangent.reshape(rows, width)
    w_rows, cot_chunk = load(place, weights[0], cot)
    w_rows = pltpu.with_memory_space_constraint(w_rows, pltpu.VMEM)

    block_in = inputs.reshape(rows, width)
    block_ins = []
    passed = []
    other = cot_chunk
    cot_found = {0: cot_chunk}
    for section in range(last):
        beside = section ^ 1
        route = [(section, beside)]
        shared = section < 2
        first_pass = section == 0
        far = forward_blocks(
            place, block_in, gains, w_rows, far_codes, other=other if shared else None, other_at=last
        )
        far_route = route + inside if shared else route
        arrived = [send(chunk, far_route, e) for e, chunk in zip(near, far[1:])]
        own = forward_blocks(place, block_in, gains, w_rows, near_codes, pack=True)
        if shared:
            for e, chunk in zip(near, arrived):
                cot_found[e if first_pass else across ^ e] = chunk
        combined = add_chunks(
            place, [send(far[0], route)] + arrived, other if first_pass else None, last
        )
        crossed = send(combined, across_route(beside, first_pass), across)
        if first_pass:
            cot_found[across] = other = crossed
        direct = [send(chunk, route, e) for e, chunk in zip(near, own[1:])]
        passed.append(
            finish_forward(place, send(own[0], route), direct + [crossed], None, full_width)
        )
        block_ins.append(block_in)
        output = passed[-1][0]
        block_in = send(output, [(beside, section + 1)]) if section % 2 else output
        if section == 1:
            codes = sorted(cot_found)
            last_back = scaled_back(
                place, [cot_found[e] for e in codes], w_rows, codes, gains, last
            )

    sums = row_statistics(place, block_in, last_back)
    step = 1
    while step < tp_count:
        arriving = send(sums, ([(0, 1)] if step < across else [(1, 1)]) + inside, step)
        sums = add_chunks(place, [sums, arriving])
        step *= 2
    last_in = block_in
    grad, *first_chunks = last_gradient(
        place, cot, last_back, block_in, sums, passed[-1], full_width
    )
    results = (grad, grad)

    last_in, first_chunks = lax.optimization_barrier((last_in, first_chunks))
    last_far = forward_blocks(place, last_in, gains, w_rows, far_codes, only=last)
    last_own = forward_blocks(place, last_in, gains, w_rows, near_codes, only=last)
    last_output = None
    for section in range(last - 1, -1, -1):
        turn = last - 1 - section
        beside = section ^ 1
        route = [(beside, section)]
        if turn == 0:
            chunk, pack = first_chunks
        else:
            upstream = send(grad, [(section + 1, beside)]) if section % 2 else grad
            others = [None]
            if turn == 1:
                others = [None] + last_far[1:]
            if turn == 2:
                others = [last_combined] + last_own[1:]
            chunk, *near_chunks, pack = gradient_chunks(
                place, upstream, passed[section], others, last
            )
        riding = inside if turn in (1, 2) else []
        if not riding:
            near_chunks = [chunk] * len(near)
        crossed = send(chunk, across_route(beside, turn == 2), across)
        pack = send(pack, route)
        direct = [send(chunk, route + riding, e) for e, chunk in zip(near, near_chunks)]
        forwarded = [send(crossed, route)] + [send(crossed, route, e) for e in near]
        half = backward_half(place, [pack] + direct, w_rows, near_codes, rows)
        if turn == 1:
            last_combined = add_chunks(place, [last_far[0]] + direct)
        if turn == 2:
            last_output, _, _ = finish_forward(
                place, last_own[0], direct + [crossed], last_in, full_width
            )
        grad, *results = finish_backward(
            place,
            forwarded,
            w_rows,
            far_codes,
            half,
            pack,
            gains,
            block_ins[section],
            full_width,
            results,
            section,
            last_output if section == 0 else None,
            last,
        )
    grads, outputs = results
    shape = (1, micro_count, row_count, width)
    return outputs.reshape(shape), grads.reshape(shape)


def solution(mesh):
    placed = (
        P(None, None, "tp"),
        P(None, None, "tp"),
        P("section", "tp", None),
        P("section", "tp"),
    )
    return jax.shard_map(
        on_device,
        mesh=mesh,
        in_specs=placed,
        out_specs=(P("section", None, None, "tp"), P("section", None, None, "tp")),
        check_vma=False,
    )
```

time: 288 us -> 216 us (0.75)
  the two profiles are of different devices: /device:TPU:5 before, /device:TPU:0 now
where the time goes in v6:
time: 216 us; the launch traced here: 215 us
  waiting for transfers between devices  84.4 us (39%)
  starting transfers between devices  77.9 us (36%)
  Pallas kernels  49.8 us (23%)
    ppermute x59, waiting for transfers between devices, send(): return lax.ppermute(value, ('section', 'tp'), pairs)  84.4 us
    ppermute x59, starting transfers between devices, send(): return lax.ppermute(value, ('section', 'tp'), pairs)  77.9 us
    pallas_call x31, Pallas kernels, local_kernel(): return list(call(place, *operands))  49.8 us
  transfers between devices with their start and end apart: 59, of which 15 were waited for; matrix products, arithmetic and copies ran while one was open for 0% of the time, Pallas kernels for 10%

profile of v6, /device:TPU:0, one launch (start us, length us, event | category | flops | bytes accessed | tf_op | source)
XLA Modules:
  0.0 214.8 jit_solution(17004843480369683419)
XLA Ops:
  1.7 6.3 %shard_map.59 = (bf16[1024,8192]{1,0:T(8,128)(2,1)S(1)}, bf16[144,1024]{1,0:T(8,128)(2,1)S(1)}) custom-call(s32[2]{0:T(128)S(1)} %pad_add_fusion.place_ref, bf16[1024,8192]{1,0:T(8,128)(2,1)} %bitcast.12, bf16[128,1024]{1,0:T(8,128)(2,1)S(1)} %bitcast.10), custom_call_target="tpu_custom_call" | custom-call | bytes 16777216 | tf_op jit(solution)/shard_map/pallas_call | solution.py:29
  9.9 2.4 %collective-permute-start.4 = (bf16[144,1024]{1,0:T(8,128)(2,1)S(1)}, bf16[144,1024]{1,0:T(8,128)(2,1)S(1)}, u32[]{:S(2)}, u32[]{:S(2)}) collective-permute-start(bf16[144,1024]{1,0:T(8,128)(2,1)S(1)} %get-tuple-element.82), channel_id=1, source_target_pairs={{0,8},{1,9},{2,10},{3,11},{4,12},{5,13},{6,14},{7,15}} | collective-permute-start | bytes 884744 | tf_op jit(solution)/shard_map/ppermute | solution.py:391
  12.3 4.2 %collective-permute-start.5 = (bf16[144,1024]{1,0:T(8,128)(2,1)S(1)}, bf16[144,1024]{1,0:T(8,128)(2,1)S(1)}, u32[]{:S(2)}, u32[]{:S(2)}) collective-permute-start(bf16[144,1024]{1,0:T(8,128)(2,1)S(1)} %get-tuple-element.83), channel_id=1, source_target_pairs={{0,11},{1,10},{2,9},{3,8},{4,15},{5,14},{6,13},{7,12},{24,27},{25,... | collective-permute-start | bytes 884744 | tf_op jit(solution)/shard_map/ppermute | solution.py:391
  19.1 1.9 shard_map.60
  28.0 3.0 %collective-permute-done.2.refs_2_ = bf16[144,1024]{1,0:T(8,128)(2,1)S(1)} collective-permute-done((bf16[144,1024]{1,0:T(8,128)(2,1)S(1)}, bf16[144,1024]{1,0:T(8,128)(2,1)S(1)}, u32[]{:S(2)}, u32[]{:S(2)}) %collective-permute-start.2) | collective-permute-done | bytes 294944 | tf_op jit(solution)/shard_map/ppermute | solution.py:391
  44.5 4.0 %collective-permute-done.14.refs_1_.refs_9_ = bf16[144,1024]{1,0:T(8,128)(2,1)S(1)} collective-permute-done((bf16[144,1024]{1,0:T(8,128)(2,1)S(1)}, bf16[144,1024]{1,0:T(8,128)(2,1)S(1)}, u32[]{:S(2)}, u32[]{:S(2)}) %collective-permute-start.14) | collective-permute-done | bytes 294944 | tf_op jit(solution)/shard_map/ppermute | solution.py:391
  53.5 5.0 %collective-permute-start.17 = (bf16[144,1024]{1,0:T(8,128)(2,1)S(1)}, bf16[144,1024]{1,0:T(8,128)(2,1)S(1)}, u32[]{:S(2)}, u32[]{:S(2)}) collective-permute-start(bf16[144,1024]{1,0:T(8,128)(2,1)S(1)} %shard_map.66), channel_id=1, source_target_pairs={{0,4},{1,5},{2,6},{3,7},{4,0},{5,1},{6,2},{7,3}} | collective-permute-start | bytes 884744 | tf_op jit(solution)/shard_map/ppermute | solution.py:391
  59.6 6.9 %collective-permute-done.17.refs_4_ = bf16[144,1024]{1,0:T(8,128)(2,1)S(1)} collective-permute-done((bf16[144,1024]{1,0:T(8,128)(2,1)S(1)}, bf16[144,1024]{1,0:T(8,128)(2,1)S(1)}, u32[]{:S(2)}, u32[]{:S(2)}) %collective-permute-start.17) | collective-permute-done | bytes 294944 | tf_op jit(solution)/shard_map/ppermute | solution.py:391
  68.6 3.9 %collective-permute-done.18.refs_0_.refs_9_ = bf16[128,1024]{1,0:T(8,128)(2,1)S(1)} collective-permute-done((bf16[128,1024]{1,0:T(8,128)(2,1)S(1)}, bf16[128,1024]{1,0:T(8,128)(2,1)S(1)}, u32[]{:S(2)}, u32[]{:S(2)}) %collective-permute-start.18) | collective-permute-done | bytes 262176 | tf_op jit(solution)/shard_map/ppermute | solution.py:391
  72.5 1.8 shard_map.69
  88.7 3.1 %collective-permute-start.29 = (f32[8,128]{1,0:T(8,128)S(1)}, f32[8,128]{1,0:T(8,128)S(1)}, u32[]{:S(2)}, u32[]{:S(2)}) collective-permute-start(f32[8,128]{1,0:T(8,128)S(1)} %shard_map.74.refs_0_), channel_id=1, source_target_pairs={{0,10},{1,11},{2,8},{3,9},{4,14},{5,15},{6,12},{7,13},{24,26},{25,... | collective-permute-start | bytes 12296 | tf_op jit(solution)/shard_map/ppermute | solution.py:391
  102.1 2.9 %shard_map.78 = (f32[1024,128]{1,0:T(8,128)S(1)}, f32[16,128]{1,0:T(8,128)S(1)}) custom-call(s32[2]{0:T(128)S(1)} %pad_add_fusion.place_ref, bf16[1024,8192]{1,0:T(8,128)(2,1)S(1)} %get-tuple-element.76.refs_2_.refs_0_, bf16[272,1024]{1,0:T(8,128)(2,1)S(1)} %collective-permute-done.36.refs_1_.refs_7_, bf16[144,1024]{1,0:T(8,128)(2,1)S(1)} %collective-permute-done.37.refs_2_, ...), custom_call_target="tpu_custom_call" | custom-call | flops 1073741824 | bytes 8388608 | tf_op jit(solution)/shard_map/pallas_call | solution.py:29
  105.0 3.0 %shard_map.79 = (bf16[128,1024]{1,0:T(8,128)(2,1)S(1)}, bf16[128,1024]{1,0:T(8,128)(2,1)S(1)}, bf16[128,1024]{1,0:T(8,128)(2,1)S(1)}) custom-call(s32[2]{0:T(128)S(1)} %pad_add_fusion.place_ref, bf16[1024,8192]{1,0:T(8,128)(2,1)S(1)} %get-tuple-element.76.refs_2_.refs_0_, bf16[144,1024]{1,0:T(8,128)(2,1)S(1)} %collective-permute-done.32.refs_1_, ...), custom_call_target="tpu_custom_call" | custom-call | flops 1073741824 | bytes 8388608 | tf_op jit(solution)/shard_map/pallas_call | solution.py:29
  109.9 44.7 %collective-permute-done.40.refs_0_ = bf16[128,1024]{1,0:T(8,128)(2,1)S(1)} collective-permute-done((bf16[128,1024]{1,0:T(8,128)(2,1)S(1)}, bf16[128,1024]{1,0:T(8,128)(2,1)S(1)}, u32[]{:S(2)}, u32[]{:S(2)}) %collective-permute-start.40) | collective-permute-done | bytes 262176 | tf_op jit(solution)/shard_map/ppermute | solution.py:391
  156.7 3.1 %collective-permute-start.41 = (bf16[144,1024]{1,0:T(8,128)(2,1)S(1)}, bf16[144,1024]{1,0:T(8,128)(2,1)S(1)}, u32[]{:S(2)}, u32[]{:S(2)}) collective-permute-start(bf16[144,1024]{1,0:T(8,128)(2,1)S(1)} %get-tuple-element.121), channel_id=1, source_target_pairs={{0,4},{1,5},{2,6},{3,7},{4,0},{5,1},{6,2},{7,3}} | collective-permute-start | bytes 884744 | tf_op jit(solution)/shard_map/ppermute | solution.py:391
  163.7 4.8 %collective-permute-done.41 = bf16[144,1024]{1,0:T(8,128)(2,1)S(1)} collective-permute-done((bf16[144,1024]{1,0:T(8,128)(2,1)S(1)}, bf16[144,1024]{1,0:T(8,128)(2,1)S(1)}, u32[]{:S(2)}, u32[]{:S(2)}) %collective-permute-start.41) | collective-permute-done | bytes 294944 | tf_op jit(solution)/shard_map/ppermute | solution.py:391
  169.9 2.2 %collective-permute-start.44 = (bf16[144,1024]{1,0:T(8,128)(2,1)S(1)}, bf16[144,1024]{1,0:T(8,128)(2,1)S(1)}, u32[]{:S(2)}, u32[]{:S(2)}) collective-permute-start(bf16[144,1024]{1,0:T(8,128)(2,1)S(1)} %collective-permute-done.41), channel_id=1, source_target_pairs={{0,10},{1,11},{2,8},{3,9},{4,14},{5,15},{6,12},{7,13}} | collective-permute-start | bytes 884744 | tf_op jit(solution)/shard_map/ppermute | solution.py:391
  172.1 3.1 %collective-permute-start.43 = (bf16[144,1024]{1,0:T(8,128)(2,1)S(1)}, bf16[144,1024]{1,0:T(8,128)(2,1)S(1)}, u32[]{:S(2)}, u32[]{:S(2)}) collective-permute-start(bf16[144,1024]{1,0:T(8,128)(2,1)S(1)} %collective-permute-done.41), channel_id=1, source_target_pairs={{0,11},{1,10},{2,9},{3,8},{4,15},{5,14},{6,13},{7,12}} | collective-permute-start | bytes 884744 | tf_op jit(solution)/shard_map/ppermute | solution.py:391
  178.0 2.9 %shard_map.82 = (f32[1024,128]{1,0:T(8,128)S(1)}, f32[16,128]{1,0:T(8,128)S(1)}) custom-call(s32[2]{0:T(128)S(1)} %pad_add_fusion.place_ref, bf16[1024,8192]{1,0:T(8,128)(2,1)S(1)} %get-tuple-element.76.refs_2_.refs_0_, bf16[272,1024]{1,0:T(8,128)(2,1)S(1)} %collective-permute-done.46.refs_1_.refs_7_, ...), custom_call_target="tpu_custom_call" | custom-call | flops 1073741824 | bytes 8388608 | tf_op jit(solution)/shard_map/pallas_call | solution.py:29
  180.9 3.0 %shard_map.83 = (bf16[128,1024]{1,0:T(8,128)(2,1)S(1)}, bf16[128,1024]{1,0:T(8,128)(2,1)S(1)}, bf16[128,1024]{1,0:T(8,128)(2,1)S(1)}) custom-call(s32[2]{0:T(128)S(1)} %pad_add_fusion.place_ref, bf16[1024,8192]{1,0:T(8,128)(2,1)S(1)} %get-tuple-element.76.refs_2_.refs_0_, bf16[144,1024]{1,0:T(8,128)(2,1)S(1)} %collective-permute-done.42.refs_1_, ...), custom_call_target="tpu_custom_call" | custom-call | flops 1073741824 | bytes 8388608 | tf_op jit(solution)/shard_map/pallas_call | solution.py:29
  191.8 5.2 %collective-permute-done.56.refs_2_.refs_1_ = bf16[144,1024]{1,0:T(8,128)(2,1)S(1)} collective-permute-done((bf16[144,1024]{1,0:T(8,128)(2,1)S(1)}, bf16[144,1024]{1,0:T(8,128)(2,1)S(1)}, u32[]{:S(2)}, u32[]{:S(2)}) %collective-permute-start.56) | collective-permute-done | bytes 294944 | tf_op jit(solution)/shard_map/ppermute | solution.py:391
  198.3 3.7 %collective-permute-done.57.refs_3_.refs_2_ = bf16[144,1024]{1,0:T(8,128)(2,1)S(1)} collective-permute-done((bf16[144,1024]{1,0:T(8,128)(2,1)S(1)}, bf16[144,1024]{1,0:T(8,128)(2,1)S(1)}, u32[]{:S(2)}, u32[]{:S(2)}) %collective-permute-start.57) | collective-permute-done | bytes 294944 | tf_op jit(solution)/shard_map/ppermute | solution.py:391
  206.2 2.8 %shard_map.87 = (f32[1024,128]{1,0:T(8,128)S(1)}, f32[16,128]{1,0:T(8,128)S(1)}) custom-call(s32[2]{0:T(128)S(1)} %pad_add_fusion.place_ref, bf16[1024,8192]{1,0:T(8,128)(2,1)S(1)} %get-tuple-element.76.refs_2_.refs_0_, bf16[272,1024]{1,0:T(8,128)(2,1)S(1)} %collective-permute-done.55.refs_1_.refs_7_, ...), custom_call_target="tpu_custom_call" | custom-call | flops 1073741824 | bytes 8388608 | tf_op jit(solution)/shard_map/pallas_call | solution.py:29
  210.9 3.9 %shard_map.89 = (bf16[128,1024]{1,0:T(8,128)(2,1)}, bf16[128,1024]{1,0:T(8,128)(2,1)}, bf16[128,1024]{1,0:T(8,128)(2,1)}) custom-call(s32[2]{0:T(128)S(1)} %pad_add_fusion.place_ref, bf16[1024,8192]{1,0:T(8,128)(2,1)S(1)} %get-tuple-element.76.refs_2_.refs_0_, bf16[144,1024]{1,0:T(8,128)(2,1)S(1)} %collective-permute-done.51.refs_1_, ...), custom_call_target="tpu_custom_call" | custom-call | flops 1073741824 | bytes 8388608 | tf_op jit(solution)/shard_map/pallas_call | solution.py:29
  (132 shorter events, 85.5 us)
Async XLA Ops:
  9.9 12.4 %collective-permute-start.4 = (bf16[144,1024]{1,0:T(8,128)(2,1)S(1)}, bf16[144,1024]{1,0:T(8,128)(2,1)S(1)}, u32[]{:S(2)}, u32[]{:S(2)}) collective-permute-start(bf16[144,1024]{1,0:T(8,128)(2,1)S(1)} %get-tuple-element.82), channel_id=1, source_target_pairs={{0,8},{1,9},{2,10},{3,11},{4,12},{5,13},{6,14},{7,15}} | collective-permute-start | bytes 884744 | tf_op jit(solution)/shard_map/ppermute | solution.py:391
  12.3 11.4 %collective-permute-start.5 = (bf16[144,1024]{1,0:T(8,128)(2,1)S(1)}, bf16[144,1024]{1,0:T(8,128)(2,1)S(1)}, u32[]{:S(2)}, u32[]{:S(2)}) collective-permute-start(bf16[144,1024]{1,0:T(8,128)(2,1)S(1)} %get-tuple-element.83), channel_id=1, source_target_pairs={{0,11},{1,10},{2,9},{3,8},{4,15},{5,14},{6,13},{7,12},{24,27},{25,... | collective-permute-start | bytes 884744 | tf_op jit(solution)/shard_map/ppermute | solution.py:391
  21.0 10.0 %collective-permute-start = (bf16[272,1024]{1,0:T(8,128)(2,1)S(1)}, bf16[272,1024]{1,0:T(8,128)(2,1)S(1)}, u32[]{:S(2)}, u32[]{:S(2)}) collective-permute-start(bf16[272,1024]{1,0:T(8,128)(2,1)S(1)} %get-tuple-element.77), channel_id=1, source_target_pairs={{0,8},{1,9},{2,10},{3,11},{4,12},{5,13},{6,14},{7,15}} | collective-permute-start | bytes 1671176 | tf_op jit(solution)/shard_map/ppermute | solution.py:391
  35.0 13.4 %collective-permute-start.14 = (bf16[144,1024]{1,0:T(8,128)(2,1)S(1)}, bf16[144,1024]{1,0:T(8,128)(2,1)S(1)}, u32[]{:S(2)}, u32[]{:S(2)}) collective-permute-start(bf16[144,1024]{1,0:T(8,128)(2,1)S(1)} %get-tuple-element.92), channel_id=1, source_target_pairs={{8,3},{9,2},{10,1},{11,0},{12,7},{13,6},{14,5},{15,4},{24,27},{25,... | collective-permute-start | bytes 884744 | tf_op jit(solution)/shard_map/ppermute | solution.py:391
  36.3 15.2 %collective-permute-start.15 = (bf16[144,1024]{1,0:T(8,128)(2,1)S(1)}, bf16[144,1024]{1,0:T(8,128)(2,1)S(1)}, u32[]{:S(2)}, u32[]{:S(2)}) collective-permute-start(bf16[144,1024]{1,0:T(8,128)(2,1)S(1)} %get-tuple-element.93), channel_id=1, source_target_pairs={{8,2},{9,3},{10,0},{11,1},{12,6},{13,7},{14,4},{15,5},{24,26},{25,... | collective-permute-start | bytes 884744 | tf_op jit(solution)/shard_map/ppermute | solution.py:391
  37.6 15.2 %collective-permute-start.16 = (bf16[144,1024]{1,0:T(8,128)(2,1)S(1)}, bf16[144,1024]{1,0:T(8,128)(2,1)S(1)}, u32[]{:S(2)}, u32[]{:S(2)}) collective-permute-start(bf16[144,1024]{1,0:T(8,128)(2,1)S(1)} %get-tuple-element.94), channel_id=1, source_target_pairs={{8,1},{9,0},{10,3},{11,2},{12,5},{13,4},{14,7},{15,6},{24,25},{25,... | collective-permute-start | bytes 884744 | tf_op jit(solution)/shard_map/ppermute | solution.py:391
  40.8 18.8 %collective-permute-start.9 = (bf16[272,1024]{1,0:T(8,128)(2,1)S(1)}, bf16[272,1024]{1,0:T(8,128)(2,1)S(1)}, u32[]{:S(2)}, u32[]{:S(2)}) collective-permute-start(bf16[272,1024]{1,0:T(8,128)(2,1)S(1)} %get-tuple-element.87), channel_id=1, source_target_pairs={{8,0},{9,1},{10,2},{11,3},{12,4},{13,5},{14,6},{15,7}} | collective-permute-start | bytes 1671176 | tf_op jit(solution)/shard_map/ppermute | solution.py:391
  43.2 15.4 %collective-permute-start.10 = (bf16[144,1024]{1,0:T(8,128)(2,1)S(1)}, bf16[144,1024]{1,0:T(8,128)(2,1)S(1)}, u32[]{:S(2)}, u32[]{:S(2)}) collective-permute-start(bf16[144,1024]{1,0:T(8,128)(2,1)S(1)} %get-tuple-element.88), channel_id=1, source_target_pairs={{8,3},{9,2},{10,1},{11,0},{12,7},{13,6},{14,5},{15,4}} | collective-permute-start | bytes 884744 | tf_op jit(solution)/shard_map/ppermute | solution.py:391
  48.5 10.2 %collective-permute-start.11 = (bf16[144,1024]{1,0:T(8,128)(2,1)S(1)}, bf16[144,1024]{1,0:T(8,128)(2,1)S(1)}, u32[]{:S(2)}, u32[]{:S(2)}) collective-permute-start(bf16[144,1024]{1,0:T(8,128)(2,1)S(1)} %get-tuple-element.89), channel_id=1, source_target_pairs={{8,2},{9,3},{10,0},{11,1},{12,6},{13,7},{14,4},{15,5}} | collective-permute-start | bytes 884744 | tf_op jit(solution)/shard_map/ppermute | solution.py:391
  53.5 12.9 %collective-permute-start.17 = (bf16[144,1024]{1,0:T(8,128)(2,1)S(1)}, bf16[144,1024]{1,0:T(8,128)(2,1)S(1)}, u32[]{:S(2)}, u32[]{:S(2)}) collective-permute-start(bf16[144,1024]{1,0:T(8,128)(2,1)S(1)} %shard_map.66), channel_id=1, source_target_pairs={{0,4},{1,5},{2,6},{3,7},{4,0},{5,1},{6,2},{7,3}} | collective-permute-start | bytes 884744 | tf_op jit(solution)/shard_map/ppermute | solution.py:391
  108.1 46.5 %collective-permute-start.40 = (bf16[128,1024]{1,0:T(8,128)(2,1)S(1)}, bf16[128,1024]{1,0:T(8,128)(2,1)S(1)}, u32[]{:S(2)}, u32[]{:S(2)}) collective-permute-start(bf16[128,1024]{1,0:T(8,128)(2,1)S(1)} %get-tuple-element.114), channel_id=1, source_target_pairs={{16,0},{17,1},{18,2},{19,3},{20,4},{21,5},{22,6},{23,7}} | collective-permute-start | bytes 786440 | tf_op jit(solution)/shard_map/ppermute | solution.py:391
  155.3 22.6 %collective-permute-start.46 = (bf16[272,1024]{1,0:T(8,128)(2,1)S(1)}, bf16[272,1024]{1,0:T(8,128)(2,1)S(1)}, u32[]{:S(2)}, u32[]{:S(2)}) collective-permute-start(bf16[272,1024]{1,0:T(8,128)(2,1)S(1)} %get-tuple-element.122), channel_id=1, source_target_pairs={{0,8},{1,9},{2,10},{3,11},{4,12},{5,13},{6,14},{7,15}} | collective-permute-start | bytes 1671176 | tf_op jit(solution)/shard_map/ppermute | solution.py:391
  156.7 11.9 %collective-permute-start.41 = (bf16[144,1024]{1,0:T(8,128)(2,1)S(1)}, bf16[144,1024]{1,0:T(8,128)(2,1)S(1)}, u32[]{:S(2)}, u32[]{:S(2)}) collective-permute-start(bf16[144,1024]{1,0:T(8,128)(2,1)S(1)} %get-tuple-element.121), channel_id=1, source_target_pairs={{0,4},{1,5},{2,6},{3,7},{4,0},{5,1},{6,2},{7,3}} | collective-permute-start | bytes 884744 | tf_op jit(solution)/shard_map/ppermute | solution.py:391
  159.8 10.1 %collective-permute-start.47 = (bf16[144,1024]{1,0:T(8,128)(2,1)S(1)}, bf16[144,1024]{1,0:T(8,128)(2,1)S(1)}, u32[]{:S(2)}, u32[]{:S(2)}) collective-permute-start(bf16[144,1024]{1,0:T(8,128)(2,1)S(1)} %get-tuple-element.123), channel_id=1, source_target_pairs={{0,11},{1,10},{2,9},{3,8},{4,15},{5,14},{6,13},{7,12},{24,27},{25,... | collective-permute-start | bytes 884744 | tf_op jit(solution)/shard_map/ppermute | solution.py:391
  161.1 11.0 %collective-permute-start.48 = (bf16[144,1024]{1,0:T(8,128)(2,1)S(1)}, bf16[144,1024]{1,0:T(8,128)(2,1)S(1)}, u32[]{:S(2)}, u32[]{:S(2)}) collective-permute-start(bf16[144,1024]{1,0:T(8,128)(2,1)S(1)} %get-tuple-element.124), channel_id=1, source_target_pairs={{0,10},{1,11},{2,8},{3,9},{4,14},{5,15},{6,12},{7,13},{24,26},{25,... | collective-permute-start | bytes 884744 | tf_op jit(solution)/shard_map/ppermute | solution.py:391
  162.4 12.8 %collective-permute-start.49 = (bf16[144,1024]{1,0:T(8,128)(2,1)S(1)}, bf16[144,1024]{1,0:T(8,128)(2,1)S(1)}, u32[]{:S(2)}, u32[]{:S(2)}) collective-permute-start(bf16[144,1024]{1,0:T(8,128)(2,1)S(1)} %get-tuple-element.125), channel_id=1, source_target_pairs={{0,9},{1,8},{2,11},{3,10},{4,13},{5,12},{6,15},{7,14},{24,25},{25,... | collective-permute-start | bytes 884744 | tf_op jit(solution)/shard_map/ppermute | solution.py:391
  168.5 12.3 %collective-permute-start.45 = (bf16[144,1024]{1,0:T(8,128)(2,1)S(1)}, bf16[144,1024]{1,0:T(8,128)(2,1)S(1)}, u32[]{:S(2)}, u32[]{:S(2)}) collective-permute-start(bf16[144,1024]{1,0:T(8,128)(2,1)S(1)} %collective-permute-done.41), channel_id=1, source_target_pairs={{0,9},{1,8},{2,11},{3,10},{4,13},{5,12},{6,15},{7,14}} | collective-permute-start | bytes 884744 | tf_op jit(solution)/shard_map/ppermute | solution.py:391
  169.9 11.0 %collective-permute-start.44 = (bf16[144,1024]{1,0:T(8,128)(2,1)S(1)}, bf16[144,1024]{1,0:T(8,128)(2,1)S(1)}, u32[]{:S(2)}, u32[]{:S(2)}) collective-permute-start(bf16[144,1024]{1,0:T(8,128)(2,1)S(1)} %collective-permute-done.41), channel_id=1, source_target_pairs={{0,10},{1,11},{2,8},{3,9},{4,14},{5,15},{6,12},{7,13}} | collective-permute-start | bytes 884744 | tf_op jit(solution)/shard_map/ppermute | solution.py:391
  184.7 21.6 %collective-permute-start.55 = (bf16[272,1024]{1,0:T(8,128)(2,1)S(1)}, bf16[272,1024]{1,0:T(8,128)(2,1)S(1)}, u32[]{:S(2)}, u32[]{:S(2)}) collective-permute-start(bf16[272,1024]{1,0:T(8,128)(2,1)S(1)} %get-tuple-element.138), channel_id=1, source_target_pairs={{8,0},{9,1},{10,2},{11,3},{12,4},{13,5},{14,6},{15,7}} | collective-permute-start | bytes 1671176 | tf_op jit(solution)/shard_map/ppermute | solution.py:391
  186.6 10.4 %collective-permute-start.56 = (bf16[144,1024]{1,0:T(8,128)(2,1)S(1)}, bf16[144,1024]{1,0:T(8,128)(2,1)S(1)}, u32[]{:S(2)}, u32[]{:S(2)}) collective-permute-start(bf16[144,1024]{1,0:T(8,128)(2,1)S(1)} %get-tuple-element.139), channel_id=1, source_target_pairs={{8,3},{9,2},{10,1},{11,0},{12,7},{13,6},{14,5},{15,4},{24,27},{25,... | collective-permute-start | bytes 884744 | tf_op jit(solution)/shard_map/ppermute | solution.py:391
  187.9 14.0 %collective-permute-start.57 = (bf16[144,1024]{1,0:T(8,128)(2,1)S(1)}, bf16[144,1024]{1,0:T(8,128)(2,1)S(1)}, u32[]{:S(2)}, u32[]{:S(2)}) collective-permute-start(bf16[144,1024]{1,0:T(8,128)(2,1)S(1)} %get-tuple-element.140), channel_id=1, source_target_pairs={{8,2},{9,3},{10,0},{11,1},{12,6},{13,7},{14,4},{15,5},{24,26},{25,... | collective-permute-start | bytes 884744 | tf_op jit(solution)/shard_map/ppermute | solution.py:391
  189.2 14.0 %collective-permute-start.58 = (bf16[144,1024]{1,0:T(8,128)(2,1)S(1)}, bf16[144,1024]{1,0:T(8,128)(2,1)S(1)}, u32[]{:S(2)}, u32[]{:S(2)}) collective-permute-start(bf16[144,1024]{1,0:T(8,128)(2,1)S(1)} %get-tuple-element.141), channel_id=1, source_target_pairs={{8,1},{9,0},{10,3},{11,2},{12,5},{13,4},{14,7},{15,6},{24,25},{25,... | collective-permute-start | bytes 884744 | tf_op jit(solution)/shard_map/ppermute | solution.py:391
  190.5 18.6 %collective-permute-start.54 = (bf16[144,1024]{1,0:T(8,128)(2,1)S(1)}, bf16[144,1024]{1,0:T(8,128)(2,1)S(1)}, u32[]{:S(2)}, u32[]{:S(2)}) collective-permute-start(bf16[144,1024]{1,0:T(8,128)(2,1)S(1)} %collective-permute-done.50.refs_4_), channel_id=1, source_target_pairs={{8,1},{9,0},{10,3},{11,2},{12,5},{13,4},{14,7},{15,6}} | collective-permute-start | bytes 884744 | tf_op jit(solution)/shard_map/ppermute | solution.py:391
  197.0 12.1 %collective-permute-start.53 = (bf16[144,1024]{1,0:T(8,128)(2,1)S(1)}, bf16[144,1024]{1,0:T(8,128)(2,1)S(1)}, u32[]{:S(2)}, u32[]{:S(2)}) collective-permute-start(bf16[144,1024]{1,0:T(8,128)(2,1)S(1)} %collective-permute-done.50.refs_4_), channel_id=1, source_target_pairs={{8,2},{9,3},{10,0},{11,1},{12,6},{13,7},{14,4},{15,5}} | collective-permute-start | bytes 884744 | tf_op jit(solution)/shard_map/ppermute | solution.py:391
  (38 other events, 194.9 us)

commit v7 on v6

--- a/solution.py
+++ b/solution.py
@@ -64,37 +64,99 @@
     )
 
 
-def block_columns(tp, code, width, start=0, size=None):
-    size = size or width
-    return pl.ds(pl.multiple_of((tp ^ code) * width + start, size), size)
-
-
-def load(place, weights, cot):
-    rows, width = cot.shape
-
-    def kernel(tp, section, w_ref, cot_ref, out_ref, chunk_ref, done):
-        copy = pltpu.make_async_copy(w_ref, out_ref, done)
-        copy.start()
-        chunk_ref[:rows, :] = cot_ref[...]
-        chunk_ref[rows:, :] = jnp.zeros((TAIL, width), jnp.bfloat16)
-        copy.wait()
-
-    return local_kernel(
-        kernel,
-        place,
-        [pltpu.with_memory_space_constraint(weights, pltpu.HBM), cot],
-        [pltpu.VMEM(weights.shape, weights.dtype), bf16(rows + TAIL, width)],
-        limit=2 * MIB,
-        in_specs=[SMEM_SPEC, pl.BlockSpec(memory_space=pltpu.HBM), VMEM_SPEC],
-        scratch_shapes=[pltpu.SemaphoreType.DMA],
-        cost=pl.CostEstimate(flops=0, bytes_accessed=2 * weights.size, transcendentals=0),
-    )
-
-
-def forward_blocks(place, a, gain_row, w_rows, codes, pack=False, only=None, other=None, other_at=None):
+def in_hbm(array):
+    return pltpu.with_memory_space_constraint(array, pltpu.HBM)
+
+
+def in_vmem(array):
+    return pltpu.with_memory_space_constraint(array, pltpu.VMEM)
+
+
+def partial_chunks(tp, wide, gain_ref, take_block, out_refs):
+    rows, width = wide.shape
+    tile = min(width, 512)
+    scaled = (wide * gain_ref[...]).astype(jnp.bfloat16)
+    for number, out_ref in enumerate(out_refs):
+        w_ref = take_block(number)
+        for start in range(0, width, tile):
+            partial = jnp.dot(
+                scaled, w_ref[:, start : start + tile], preferred_element_type=jnp.float32
+            )
+            out_ref[:rows, start : start + tile] = partial.astype(jnp.bfloat16)
+    line = as_line(jnp.sum(wide * wide, axis=1, keepdims=True))
+    row_ids = lax.broadcasted_iota(jnp.int32, (TAIL, rows), 0)
+    own_row = jnp.where(row_ids == tp % TAIL, jnp.broadcast_to(line, (TAIL, rows)), 0.0)
+    for out_ref in out_refs:
+        out_ref[rows : rows + TAIL, :] = jnp.zeros((TAIL, width), jnp.bfloat16)
+        out_ref[rows : rows + TAIL, :rows] = own_row.astype(jnp.bfloat16)
+
+
+def chunk_shapes(rows, width, count, pack):
+    shapes = [bf16(rows + TAIL, width)] * count
+    if pack:
+        shapes[0] = bf16(2 * rows + TAIL, width)
+    return shapes
+
+
+def first_forward_blocks(place, a, gain_row, weights, codes, pack=False, other=None, other_at=None):
     rows, width = a.shape
-    chunk_rows = rows + TAIL
-    tile = min(width, 512)
+    count = len(codes)
+    others = [] if other is None else [other]
+
+    def kernel(tp, section, a_hbm, gain_ref, w_hbm, *refs):
+        w_ref, out_refs = refs[len(others)], refs[len(others) + 1 : len(others) + 1 + count]
+        a_ref, a_done, w_done = refs[-3:]
+        a_copy = pltpu.make_async_copy(a_hbm, a_ref, a_done)
+        a_copy.start()
+        copies = []
+        for number, code in enumerate(codes):
+            columns = pl.ds(pl.multiple_of((tp ^ code) * width, width), width)
+            copies.append(
+                pltpu.make_async_copy(w_hbm.at[:, columns], w_ref.at[number], w_done.at[number])
+            )
+            copies[-1].start()
+        if others:
+            chunk_ref = refs[len(others) + 1 + count]
+            chunk_ref[:rows, :] = refs[0][...]
+            chunk_ref[rows:, :] = jnp.zeros((TAIL, width), jnp.bfloat16)
+        a_copy.wait()
+
+        def take_block(number):
+            copies[number].wait()
+            return w_ref.at[number]
+
+        partial_chunks(tp, a_ref[...].astype(jnp.float32), gain_ref, take_block, out_refs)
+        if pack:
+            out_refs[0][rows + TAIL :, :] = a_ref[...]
+        if others:
+
+            @pl.when(section == other_at)
+            def _():
+                for out_ref in out_refs:
+                    out_ref[...] = chunk_ref[...]
+
+    return local_kernel(
+        kernel,
+        place,
+        [in_hbm(a), gain_row, in_hbm(weights)] + others,
+        [pltpu.VMEM((count, width, width), jnp.bfloat16)]
+        + chunk_shapes(rows, width, count, pack)
+        + [bf16(rows + TAIL, width)] * len(others),
+        in_specs=[SMEM_SPEC, pl.BlockSpec(memory_space=pltpu.HBM), VMEM_SPEC]
+        + [pl.BlockSpec(memory_space=pltpu.HBM)]
+        + [VMEM_SPEC] * len(others),
+        scratch_shapes=[
+            pltpu.VMEM((rows, width), jnp.bfloat16),
+            pltpu.SemaphoreType.DMA,
+            pltpu.SemaphoreType.DMA((count,)),
+        ],
+        cost=matmul_cost(rows, width, count),
+    )
+
+
+def forward_blocks(place, a, gain_row, w_half, pack=False, only=None, other=None, other_at=None):
+    rows, width = a.shape
+    count = w_half.shape[0]
     others = [] if other is None else [other]
 
     def kernel(tp, section, a_ref, gain_ref, w_ref, *refs):
@@ -102,23 +164,9 @@
 
         def work():
             wide = a_ref[...].astype(jnp.float32)
-            scaled = (wide * gain_ref[...]).astype(jnp.bfloat16)
-            for code, out_ref in zip(codes, out_refs):
-                for start in range(0, width, tile):
-                    partial = jnp.dot(
-                        scaled,
-                        w_ref[:, block_columns(tp, code, width, start, tile)],
-                        preferred_element_type=jnp.float32,
-                    )
-                    out_ref[:rows, start : start + tile] = partial.astype(jnp.bfloat16)
-            line = as_line(jnp.sum(wide * wide, axis=1, keepdims=True))
-            row_ids = lax.broadcasted_iota(jnp.int32, (TAIL, rows), 0)
-            own_row = jnp.where(row_ids == tp % TAIL, jnp.broadcast_to(line, (TAIL, rows)), 0.0)
-            for out_ref in out_refs:
-                out_ref[rows:chunk_rows, :] = jnp.zeros((TAIL, width), jnp.bfloat16)
-                out_ref[rows:chunk_rows, :rows] = own_row.astype(jnp.bfloat16)
+            partial_chunks(tp, wide, gain_ref, lambda number: w_ref.at[number], out_refs)
             if pack:
-                out_refs[0][chunk_rows:, :] = a_ref[...]
+                out_refs[0][rows + TAIL :, :] = a_ref[...]
 
         if only is not None:
             pl.when(section == only)(work)
@@ -131,15 +179,12 @@
                 for out_ref in out_refs:
                     out_ref[...] = refs[0][...]
 
-    shapes = [bf16(chunk_rows, width)] * len(codes)
-    if pack:
-        shapes[0] = bf16(chunk_rows + rows, width)
-    return local_kernel(
-        kernel,
-        place,
-        [a, gain_row, w_rows] + others,
-        shapes,
-        cost=matmul_cost(rows, width, len(codes)),
+    return local_kernel(
+        kernel,
+        place,
+        [a, gain_row, w_half] + others,
+        chunk_shapes(rows, width, count, pack),
+        cost=matmul_cost(rows, width, count),
     )
 
 
@@ -256,12 +301,11 @@
     )
 
 
-def block_products(tp, w_ref, codes, chunk_refs, rows, start, tile):
-    width = w_ref.shape[0]
+def block_products(blocks, rows, start, tile):
     total = None
-    for code, chunk in zip(codes, chunk_refs):
+    for w_ref, chunk in blocks:
         product = lax.dot_general(
-            w_ref[start : start + tile, block_columns(tp, code, width)],
+            w_ref[start : start + tile, :],
             chunk[:rows, :],
             (((1,), (1,)), ((), ())),
             preferred_element_type=jnp.float32,
@@ -270,53 +314,63 @@
     return total
 
 
-def scaled_back(place, chunks, w_rows, codes, gain_row, only):
-    width = w_rows.shape[0]
-    rows = chunks[0].shape[0] - TAIL
+def scaled_back(place, halves, gain_row, only):
+    w_far, w_near = halves[0][0], halves[1][0]
+    count, width, _ = w_far.shape
+    rows = halves[0][1][0].shape[0] - TAIL
     tile = min(width, 256)
 
-    def kernel(tp, section, w_ref, gain_ref, *refs):
+    def kernel(tp, section, far_ref, near_ref, gain_ref, *refs):
+        blocks = [(far_ref.at[k], refs[k]) for k in range(count)]
+        blocks += [(near_ref.at[k], refs[count + k]) for k in range(count)]
+
         @pl.when(section == only)
         def _():
             for start in range(0, width, tile):
-                products = block_products(tp, w_ref, codes, refs[:-1], rows, start, tile)
                 columns = slice(start, start + tile)
+                products = block_products(blocks, rows, start, tile)
                 refs[-1][:, columns] = gain_ref[:, columns] * products.T
 
     return local_kernel(
         kernel,
         place,
-        [w_rows, gain_row] + chunks,
+        [w_far, w_near, gain_row] + halves[0][1] + halves[1][1],
         [f32(rows, width)],
-        cost=matmul_cost(rows, width, len(codes)),
+        cost=matmul_cost(rows, width, 2 * count),
     )[0]
 
 
-def backward_half(place, chunks, w_rows, codes, rows):
-    width = w_rows.shape[0]
+def backward_part(place, chunks, w_half, numbers, rows, before=None):
+    width = w_half.shape[1]
     tile = min(width, 256)
+    given = [] if before is None else list(before)
 
     def kernel(tp, section, w_ref, *refs):
-        chunk_refs, (out_ref, sum_ref) = refs[:-2], refs[-2:]
+        chunk_refs, (out_ref, sum_ref) = refs[: len(chunks)], refs[-2:]
+        blocks = [(w_ref.at[k], chunk) for k, chunk in zip(numbers, chunk_refs)]
         for start in range(0, width, tile):
-            out_ref[start : start + tile, :] = block_products(
-                tp, w_ref, codes, chunk_refs, rows, start, tile
-            )
-        sum_ref[...] = tail_sum(chunk_refs, rows)
-
-    return local_kernel(
-        kernel,
-        place,
-        [w_rows] + chunks,
+            products = block_products(blocks, rows, start, tile)
+            if given:
+                products = products + refs[len(chunks)][start : start + tile, :]
+            out_ref[start : start + tile, :] = products
+        sums = tail_sum(chunk_refs, rows)
+        sum_ref[...] = sums + refs[len(chunks) + 1][...] if given else sums
+
+    return local_kernel(
+        kernel,
+        place,
+        [w_half] + chunks + given,
         [f32(width, rows), f32(TAIL, rows)],
-        cost=matmul_cost(rows, width, len(codes)),
-    )
-
-
-def finish_backward(place, chunks, w_rows, codes, half, pack, gain_row, a, full_width, results, at, last_output=None, last=None):
+        cost=matmul_cost(rows, width, len(chunks)),
+    )
+
+
+def finish_backward(
+    place, chunks, w_half, numbers, before, pack, gain_row, a, full_width, results, at, last_output=None, last=None
+):
     rows, width = a.shape
     chunk_rows = rows + TAIL
-    count = len(codes)
+    count = len(chunks)
     tile = min(width, 256)
     given = [] if last_output is None else [last_output]
 
@@ -328,8 +382,9 @@
         tail = pack_ref[rows:chunk_rows, :rows].astype(jnp.float32)
         rms = as_column(tail[1:2] + tail[2:3])
         scale = rms * rms * rms / full_width * row_dot
+        blocks = [(w_ref.at[k], chunk) for k, chunk in zip(numbers, chunk_refs)]
         for start in range(0, width, tile):
-            products = block_products(tp, w_ref, codes, chunk_refs, rows, start, tile)
+            products = block_products(blocks, rows, start, tile)
             back = (products + half_ref[start : start + tile, :]).T
             columns = slice(start, start + tile)
             out_ref[:, columns] = (
@@ -357,7 +412,7 @@
     return local_kernel(
         kernel,
         place,
-        [w_rows, *chunks, *half, pack, gain_row, a, *results] + given,
+        [w_half, *chunks, *before, pack, gain_row, a, *results] + given,
         [bf16(rows, width)] * 3,
         cost=matmul_cost(rows, width, count),
     )
@@ -391,30 +446,41 @@
         return lax.ppermute(value, ("section", "tp"), pairs)
 
     cot = cotangent.reshape(rows, width)
-    w_rows, cot_chunk = load(place, weights[0], cot)
-    w_rows = pltpu.with_memory_space_constraint(w_rows, pltpu.VMEM)
 
     block_in = inputs.reshape(rows, width)
     block_ins = []
     passed = []
-    other = cot_chunk
-    cot_found = {0: cot_chunk}
+    other = None
+    cot_found = {}
     for section in range(last):
         beside = section ^ 1
         route = [(section, beside)]
         shared = section < 2
         first_pass = section == 0
-        far = forward_blocks(
-            place, block_in, gains, w_rows, far_codes, other=other if shared else None, other_at=last
-        )
+        if first_pass:
+            w_far, *far, other = first_forward_blocks(
+                place, block_in, gains, weights[0], far_codes, other=cot, other_at=last
+            )
+            w_far = in_vmem(w_far)
+            cot_found[0] = other
+        else:
+            far = forward_blocks(
+                place, block_in, gains, w_far, other=other if shared else None, other_at=last
+            )
         far_route = route + inside if shared else route
         arrived = [send(chunk, far_route, e) for e, chunk in zip(near, far[1:])]
-        own = forward_blocks(place, block_in, gains, w_rows, near_codes, pack=True)
+        if first_pass:
+            w_near, *own = first_forward_blocks(
+                place, block_in, gains, weights[0], near_codes, pack=True
+            )
+            w_near = in_vmem(w_near)
+        else:
+            own = forward_blocks(place, block_in, gains, w_near, pack=True)
         if shared:
             for e, chunk in zip(near, arrived):
                 cot_found[e if first_pass else across ^ e] = chunk
         combined = add_chunks(
-            place, [send(far[0], route)] + arrived, other if first_pass else None, last
+            place, arrived + [send(far[0], route)], other if first_pass else None, last
         )
         crossed = send(combined, across_route(beside, first_pass), across)
         if first_pass:
@@ -427,10 +493,11 @@
         output = passed[-1][0]
         block_in = send(output, [(beside, section + 1)]) if section % 2 else output
         if section == 1:
-            codes = sorted(cot_found)
-            last_back = scaled_back(
-                place, [cot_found[e] for e in codes], w_rows, codes, gains, last
-            )
+            halves = [
+                (half, [cot_found[code] for code in codes])
+                for half, codes in ((w_far, far_codes), (w_near, near_codes))
+            ]
+            last_back = scaled_back(place, halves, gains, last)
 
     sums = row_statistics(place, block_in, last_back)
     step = 1
@@ -445,8 +512,8 @@
     results = (grad, grad)
 
     last_in, first_chunks = lax.optimization_barrier((last_in, first_chunks))
-    last_far = forward_blocks(place, last_in, gains, w_rows, far_codes, only=last)
-    last_own = forward_blocks(place, last_in, gains, w_rows, near_codes, only=last)
+    last_far = forward_blocks(place, last_in, gains, w_far, only=last)
+    last_own = forward_blocks(place, last_in, gains, w_near, only=last)
     last_output = None
     for section in range(last - 1, -1, -1):
         turn = last - 1 - section
@@ -470,8 +537,13 @@
         crossed = send(chunk, across_route(beside, turn == 2), across)
         pack = send(pack, route)
         direct = [send(chunk, route + riding, e) for e, chunk in zip(near, near_chunks)]
-        forwarded = [send(crossed, route)] + [send(crossed, route, e) for e in near]
-        half = backward_half(place, [pack] + direct, w_rows, near_codes, rows)
+        forwarded = [send(crossed, route, e) for e in near] + [send(crossed, route)]
+        numbers = list(range(1, across)) + [0]
+        part = backward_part(place, direct + [pack], w_near, numbers, rows)
+        middle = across // 2
+        part = backward_part(
+            place, forwarded[middle - 1 : -1], w_far, numbers[middle - 1 : -1], rows, part
+        )
         if turn == 1:
             last_combined = add_chunks(place, [last_far[0]] + direct)
         if turn == 2:
@@ -480,10 +552,10 @@
             )
         grad, *results = finish_backward(
             place,
-            forwarded,
-            w_rows,
-            far_codes,
-            half,
+            forwarded[: middle - 1] + forwarded[-1:],
+            w_far,
+            numbers[: middle - 1] + numbers[-1:],
+            part,
             pack,
             gains,
             block_ins[section],

time: 216 us -> 215 us (level)
  waiting for transfers between devices: 84.4 us -> 80 us
  Pallas kernels: 49.8 us -> 52.1 us
    ppermute x59, waiting for transfers between devices: 84.4 us -> 80 us  [send(): return lax.ppermute(value, ('section', 'tp'), pairs)]
    pallas_call x31 -> x33, Pallas kernels: 49.8 us -> 52.1 us  [local_kernel(): return list(call(place, *operands))]
  transfers between devices with their start and end apart: 59 -> 59, of which waited for: 15 -> 14; matrix products, arithmetic and copies ran while one was open for 0% -> 0% of each run, Pallas kernels for 10% -> 14%
where the time goes in v7:
time: 215 us; the launch traced here: 212 us
  waiting for transfers between devices  80 us (37%)
  starting transfers between devices  76.4 us (36%)
  Pallas kernels  52.1 us (24%)
    ppermute x59, waiting for transfers between devices, send(): return lax.ppermute(value, ('section', 'tp'), pairs)  80 us
    ppermute x59, starting transfers between devices, send(): return lax.ppermute(value, ('section', 'tp'), pairs)  76.4 us
    pallas_call x33, Pallas kernels, local_kernel(): return list(call(place, *operands))  52.1 us
  transfers between devices with their start and end apart: 59, of which 14 were waited for; matrix products, arithmetic and copies ran while one was open for 0% of the time, Pallas kernels for 14%

profile of v7, /device:TPU:0, one launch (start us, length us, event | category | flops | bytes accessed | tf_op | source)
XLA Modules:
  0.0 211.9 jit_solution(13994006075705874705)
XLA Ops:
  2.3 4.6 %shard_map.59 = (bf16[4,1024,1024]{2,1,0:T(8,128)(2,1)S(1)}, bf16[144,1024]{1,0:T(8,128)(2,1)S(1)}, bf16[144,1024]{1,0:T(8,128)(2,1)S(1)}, bf16[144,1024]{1,0:T(...) custom-call(s32[2]{0:T(128)S(1)} %pad_add_fusion.place_ref, bf16[128,1024]{1,0:T(8,128)(2,1)} %bitcast.7, ...), custom_call_target="tpu_custom_call" | custom-call | flops 1073741824 | bytes 8388608 | tf_op jit(solution)/shard_map/pallas_call | solution.py:29
  7.0 5.3 %collective-permute-start.4 = (bf16[144,1024]{1,0:T(8,128)(2,1)S(1)}, bf16[144,1024]{1,0:T(8,128)(2,1)S(1)}, u32[]{:S(2)}, u32[]{:S(2)}) collective-permute-start(bf16[144,1024]{1,0:T(8,128)(2,1)S(1)} %get-tuple-element.88), channel_id=1, source_target_pairs={{0,11},{1,10},{2,9},{3,8},{4,15},{5,14},{6,13},{7,12},{24,27},{25,... | collective-permute-start | bytes 884744 | tf_op jit(solution)/shard_map/ppermute | solution.py:446
  16.3 5.4 %shard_map.60 = (bf16[4,1024,1024]{2,1,0:T(8,128)(2,1)S(1)}, bf16[272,1024]{1,0:T(8,128)(2,1)S(1)}, bf16[144,1024]{1,0:T(8,128)(2,1)S(1)}, bf16[144,1024]{1,0:T(8,128)(2,1)S(1)}, bf16[144,1024]{1,0:T(8,128)(2,1)S(1)}) custom-call(s32[2]{0:T(128)S(1)} %pad_add_fusion.place_ref, bf16[128,1024]{1,0:T(8,128)(2,1)} %bitcast.8, f32[1,1024]{1,0:T(1,128)S(1)} %copy-done.3, ...), custom_call_target="tpu_custom_call" | custom-call | flops 1073741824 | bytes 8388608 | tf_op jit(solution)/shard_map/pallas_call | solution.py:29
  28.5 5.4 %collective-permute-done.2.refs_2_ = bf16[144,1024]{1,0:T(8,128)(2,1)S(1)} collective-permute-done((bf16[144,1024]{1,0:T(8,128)(2,1)S(1)}, bf16[144,1024]{1,0:T(8,128)(2,1)S(1)}, u32[]{:S(2)}, u32[]{:S(2)}) %collective-permute-start.2) | collective-permute-done | bytes 294944 | tf_op jit(solution)/shard_map/ppermute | solution.py:446
  34.8 1.9 shard_map.64
  41.9 1.9 shard_map.63
  52.5 4.4 %collective-permute-start.17 = (bf16[144,1024]{1,0:T(8,128)(2,1)S(1)}, bf16[144,1024]{1,0:T(8,128)(2,1)S(1)}, u32[]{:S(2)}, u32[]{:S(2)}) collective-permute-start(bf16[144,1024]{1,0:T(8,128)(2,1)S(1)} %shard_map.65), channel_id=1, source_target_pairs={{0,4},{1,5},{2,6},{3,7},{4,0},{5,1},{6,2},{7,3}} | collective-permute-start | bytes 884744 | tf_op jit(solution)/shard_map/ppermute | solution.py:446
  58.5 6.3 %collective-permute-done.17.refs_4_ = bf16[144,1024]{1,0:T(8,128)(2,1)S(1)} collective-permute-done((bf16[144,1024]{1,0:T(8,128)(2,1)S(1)}, bf16[144,1024]{1,0:T(8,128)(2,1)S(1)}, u32[]{:S(2)}, u32[]{:S(2)}) %collective-permute-start.17) | collective-permute-done | bytes 294944 | tf_op jit(solution)/shard_map/ppermute | solution.py:446
  67.0 3.9 %collective-permute-done.18.refs_0_.refs_7_ = bf16[128,1024]{1,0:T(8,128)(2,1)S(1)} collective-permute-done((bf16[128,1024]{1,0:T(8,128)(2,1)S(1)}, bf16[128,1024]{1,0:T(8,128)(2,1)S(1)}, u32[]{:S(2)}, u32[]{:S(2)}) %collective-permute-start.18) | collective-permute-done | bytes 262176 | tf_op jit(solution)/shard_map/ppermute | solution.py:446
  75.4 1.8 shard_map.67
  87.2 3.1 %collective-permute-start.29 = (f32[8,128]{1,0:T(8,128)S(1)}, f32[8,128]{1,0:T(8,128)S(1)}, u32[]{:S(2)}, u32[]{:S(2)}) collective-permute-start(f32[8,128]{1,0:T(8,128)S(1)} %shard_map.73.refs_0_), channel_id=1, source_target_pairs={{0,10},{1,11},{2,8},{3,9},{4,14},{5,15},{6,12},{7,13},{24,26},{25,... | collective-permute-start | bytes 12296 | tf_op jit(solution)/shard_map/ppermute | solution.py:446
  100.7 2.9 %shard_map.77 = (f32[1024,128]{1,0:T(8,128)S(1)}, f32[16,128]{1,0:T(8,128)S(1)}) custom-call(s32[2]{0:T(128)S(1)} %pad_add_fusion.place_ref, bf16[4,1024,1024]{2,1,0:T(8,128)(2,1)S(1)} %get-tuple-element.94.refs_2_.refs_1_.refs_0_, bf16[144,1024]{1,0:T(8,128)(2,1)S(1)} %collective-permute-done.36.refs_1_, ...), custom_call_target="tpu_custom_call" | custom-call | flops 1073741824 | bytes 8388608 | tf_op jit(solution)/shard_map/pallas_call | solution.py:29
  105.4 1.9 shard_map.79
  109.2 41.8 %collective-permute-done.40.refs_0_ = bf16[128,1024]{1,0:T(8,128)(2,1)S(1)} collective-permute-done((bf16[128,1024]{1,0:T(8,128)(2,1)S(1)}, bf16[128,1024]{1,0:T(8,128)(2,1)S(1)}, u32[]{:S(2)}, u32[]{:S(2)}) %collective-permute-start.40) | collective-permute-done | bytes 262176 | tf_op jit(solution)/shard_map/ppermute | solution.py:446
  153.1 2.3 %collective-permute-start.41 = (bf16[144,1024]{1,0:T(8,128)(2,1)S(1)}, bf16[144,1024]{1,0:T(8,128)(2,1)S(1)}, u32[]{:S(2)}, u32[]{:S(2)}) collective-permute-start(bf16[144,1024]{1,0:T(8,128)(2,1)S(1)} %get-tuple-element.131), channel_id=1, source_target_pairs={{0,4},{1,5},{2,6},{3,7},{4,0},{5,1},{6,2},{7,3}} | collective-permute-start | bytes 884744 | tf_op jit(solution)/shard_map/ppermute | solution.py:446
  159.4 6.5 %collective-permute-done.41 = bf16[144,1024]{1,0:T(8,128)(2,1)S(1)} collective-permute-done((bf16[144,1024]{1,0:T(8,128)(2,1)S(1)}, bf16[144,1024]{1,0:T(8,128)(2,1)S(1)}, u32[]{:S(2)}, u32[]{:S(2)}) %collective-permute-start.41) | collective-permute-done | bytes 294944 | tf_op jit(solution)/shard_map/ppermute | solution.py:446
  167.2 3.3 %collective-permute-start.45 = (bf16[144,1024]{1,0:T(8,128)(2,1)S(1)}, bf16[144,1024]{1,0:T(8,128)(2,1)S(1)}, u32[]{:S(2)}, u32[]{:S(2)}) collective-permute-start(bf16[144,1024]{1,0:T(8,128)(2,1)S(1)} %collective-permute-done.41), channel_id=1, source_target_pairs={{0,9},{1,8},{2,11},{3,10},{4,13},{5,12},{6,15},{7,14}} | collective-permute-start | bytes 884744 | tf_op jit(solution)/shard_map/ppermute | solution.py:446
  171.8 2.0 collective-permute-start.43
  175.3 2.9 %shard_map.82 = (f32[1024,128]{1,0:T(8,128)S(1)}, f32[16,128]{1,0:T(8,128)S(1)}) custom-call(s32[2]{0:T(128)S(1)} %pad_add_fusion.place_ref, bf16[4,1024,1024]{2,1,0:T(8,128)(2,1)S(1)} %get-tuple-element.94.refs_2_.refs_1_.refs_0_, bf16[144,1024]{1,0:T(8,128)(2,1)S(1)} %collective-permute-done.46.refs_1_, ...), custom_call_target="tpu_custom_call" | custom-call | flops 1073741824 | bytes 8388608 | tf_op jit(solution)/shard_map/pallas_call | solution.py:29
  180.0 1.9 shard_map.84
  189.9 6.0 %collective-permute-done.55.refs_1_ = bf16[144,1024]{1,0:T(8,128)(2,1)S(1)} collective-permute-done((bf16[144,1024]{1,0:T(8,128)(2,1)S(1)}, bf16[144,1024]{1,0:T(8,128)(2,1)S(1)}, u32[]{:S(2)}, u32[]{:S(2)}) %collective-permute-start.55) | collective-permute-done | bytes 294944 | tf_op jit(solution)/shard_map/ppermute | solution.py:446
  197.2 2.8 %collective-permute-done.56.refs_2_ = bf16[144,1024]{1,0:T(8,128)(2,1)S(1)} collective-permute-done((bf16[144,1024]{1,0:T(8,128)(2,1)S(1)}, bf16[144,1024]{1,0:T(8,128)(2,1)S(1)}, u32[]{:S(2)}, u32[]{:S(2)}) %collective-permute-start.56) | collective-permute-done | bytes 294944 | tf_op jit(solution)/shard_map/ppermute | solution.py:446
  204.3 2.9 %shard_map.88 = (f32[1024,128]{1,0:T(8,128)S(1)}, f32[16,128]{1,0:T(8,128)S(1)}) custom-call(s32[2]{0:T(128)S(1)} %pad_add_fusion.place_ref, bf16[4,1024,1024]{2,1,0:T(8,128)(2,1)S(1)} %get-tuple-element.94.refs_2_.refs_1_.refs_0_, bf16[144,1024]{1,0:T(8,128)(2,1)S(1)} %collective-permute-done.55.refs_1_, ...), custom_call_target="tpu_custom_call" | custom-call | flops 1073741824 | bytes 8388608 | tf_op jit(solution)/shard_map/pallas_call | solution.py:29
  209.0 2.8 %shard_map.91 = (bf16[128,1024]{1,0:T(8,128)(2,1)}, bf16[128,1024]{1,0:T(8,128)(2,1)}, bf16[128,1024]{1,0:T(8,128)(2,1)}) custom-call(s32[2]{0:T(128)S(1)} %pad_add_fusion.place_ref, bf16[4,1024,1024]{2,1,0:T(8,128)(2,1)S(1)} %get-tuple-element.83.refs_2_.refs_0_, bf16[144,1024]{1,0:T(8,128)(2,1)S(1)} %collective-permute-done.51.refs_1_, ...), custom_call_target="tpu_custom_call" | custom-call | flops 536870912 | bytes 4194304 | tf_op jit(solution)/shard_map/pallas_call | solution.py:29
  (138 shorter events, 86.3 us)
Async XLA Ops:
  7.0 16.0 %collective-permute-start.4 = (bf16[144,1024]{1,0:T(8,128)(2,1)S(1)}, bf16[144,1024]{1,0:T(8,128)(2,1)S(1)}, u32[]{:S(2)}, u32[]{:S(2)}) collective-permute-start(bf16[144,1024]{1,0:T(8,128)(2,1)S(1)} %get-tuple-element.88), channel_id=1, source_target_pairs={{0,11},{1,10},{2,9},{3,8},{4,15},{5,14},{6,13},{7,12},{24,27},{25,... | collective-permute-start | bytes 884744 | tf_op jit(solution)/shard_map/ppermute | solution.py:446
  12.3 12.0 %collective-permute-start.5 = (bf16[144,1024]{1,0:T(8,128)(2,1)S(1)}, bf16[144,1024]{1,0:T(8,128)(2,1)S(1)}, u32[]{:S(2)}, u32[]{:S(2)}) collective-permute-start(bf16[144,1024]{1,0:T(8,128)(2,1)S(1)} %get-tuple-element.89), channel_id=1, source_target_pairs={{0,10},{1,11},{2,8},{3,9},{4,14},{5,15},{6,12},{7,13},{24,26},{25,... | collective-permute-start | bytes 884744 | tf_op jit(solution)/shard_map/ppermute | solution.py:446
  13.6 12.0 %collective-permute-start.6 = (bf16[144,1024]{1,0:T(8,128)(2,1)S(1)}, bf16[144,1024]{1,0:T(8,128)(2,1)S(1)}, u32[]{:S(2)}, u32[]{:S(2)}) collective-permute-start(bf16[144,1024]{1,0:T(8,128)(2,1)S(1)} %get-tuple-element.90), channel_id=1, source_target_pairs={{0,9},{1,8},{2,11},{3,10},{4,13},{5,12},{6,15},{7,14},{24,25},{25,... | collective-permute-start | bytes 884744 | tf_op jit(solution)/shard_map/ppermute | solution.py:446
  14.9 12.0 %collective-permute-start.7 = (bf16[144,1024]{1,0:T(8,128)(2,1)S(1)}, bf16[144,1024]{1,0:T(8,128)(2,1)S(1)}, u32[]{:S(2)}, u32[]{:S(2)}) collective-permute-start(bf16[144,1024]{1,0:T(8,128)(2,1)S(1)} %get-tuple-element.91), channel_id=1, source_target_pairs={{0,8},{1,9},{2,10},{3,11},{4,12},{5,13},{6,14},{7,15}} | collective-permute-start | bytes 884744 | tf_op jit(solution)/shard_map/ppermute | solution.py:446
  21.7 12.3 %collective-permute-start = (bf16[272,1024]{1,0:T(8,128)(2,1)S(1)}, bf16[272,1024]{1,0:T(8,128)(2,1)S(1)}, u32[]{:S(2)}, u32[]{:S(2)}) collective-permute-start(bf16[272,1024]{1,0:T(8,128)(2,1)S(1)} %get-tuple-element.84), channel_id=1, source_target_pairs={{0,8},{1,9},{2,10},{3,11},{4,12},{5,13},{6,14},{7,15}} | collective-permute-start | bytes 1671176 | tf_op jit(solution)/shard_map/ppermute | solution.py:446
  38.0 11.2 %collective-permute-start.14 = (bf16[144,1024]{1,0:T(8,128)(2,1)S(1)}, bf16[144,1024]{1,0:T(8,128)(2,1)S(1)}, u32[]{:S(2)}, u32[]{:S(2)}) collective-permute-start(bf16[144,1024]{1,0:T(8,128)(2,1)S(1)} %get-tuple-element.100), channel_id=1, source_target_pairs={{8,2},{9,3},{10,0},{11,1},{12,6},{13,7},{14,4},{15,5},{24,26},{25,... | collective-permute-start | bytes 884744 | tf_op jit(solution)/shard_map/ppermute | solution.py:446
  39.3 11.2 %collective-permute-start.15 = (bf16[144,1024]{1,0:T(8,128)(2,1)S(1)}, bf16[144,1024]{1,0:T(8,128)(2,1)S(1)}, u32[]{:S(2)}, u32[]{:S(2)}) collective-permute-start(bf16[144,1024]{1,0:T(8,128)(2,1)S(1)} %get-tuple-element.101), channel_id=1, source_target_pairs={{8,1},{9,0},{10,3},{11,2},{12,5},{13,4},{14,7},{15,6},{24,25},{25,... | collective-permute-start | bytes 884744 | tf_op jit(solution)/shard_map/ppermute | solution.py:446
  40.6 11.2 %collective-permute-start.16 = (bf16[144,1024]{1,0:T(8,128)(2,1)S(1)}, bf16[144,1024]{1,0:T(8,128)(2,1)S(1)}, u32[]{:S(2)}, u32[]{:S(2)}) collective-permute-start(bf16[144,1024]{1,0:T(8,128)(2,1)S(1)} %get-tuple-element.102), channel_id=1, source_target_pairs={{8,0},{9,1},{10,2},{11,3},{12,4},{13,5},{14,6},{15,7}} | collective-permute-start | bytes 884744 | tf_op jit(solution)/shard_map/ppermute | solution.py:446
  43.7 14.8 %collective-permute-start.9 = (bf16[272,1024]{1,0:T(8,128)(2,1)S(1)}, bf16[272,1024]{1,0:T(8,128)(2,1)S(1)}, u32[]{:S(2)}, u32[]{:S(2)}) collective-permute-start(bf16[272,1024]{1,0:T(8,128)(2,1)S(1)} %get-tuple-element.95), channel_id=1, source_target_pairs={{8,0},{9,1},{10,2},{11,3},{12,4},{13,5},{14,6},{15,7}} | collective-permute-start | bytes 1671176 | tf_op jit(solution)/shard_map/ppermute | solution.py:446
  52.5 12.3 %collective-permute-start.17 = (bf16[144,1024]{1,0:T(8,128)(2,1)S(1)}, bf16[144,1024]{1,0:T(8,128)(2,1)S(1)}, u32[]{:S(2)}, u32[]{:S(2)}) collective-permute-start(bf16[144,1024]{1,0:T(8,128)(2,1)S(1)} %shard_map.65), channel_id=1, source_target_pairs={{0,4},{1,5},{2,6},{3,7},{4,0},{5,1},{6,2},{7,3}} | collective-permute-start | bytes 884744 | tf_op jit(solution)/shard_map/ppermute | solution.py:446
  107.4 43.6 %collective-permute-start.40 = (bf16[128,1024]{1,0:T(8,128)(2,1)S(1)}, bf16[128,1024]{1,0:T(8,128)(2,1)S(1)}, u32[]{:S(2)}, u32[]{:S(2)}) collective-permute-start(bf16[128,1024]{1,0:T(8,128)(2,1)S(1)} %get-tuple-element.124), channel_id=1, source_target_pairs={{16,0},{17,1},{18,2},{19,3},{20,4},{21,5},{22,6},{23,7}} | collective-permute-start | bytes 786440 | tf_op jit(solution)/shard_map/ppermute | solution.py:446
  151.8 23.5 %collective-permute-start.49 = (bf16[272,1024]{1,0:T(8,128)(2,1)S(1)}, bf16[272,1024]{1,0:T(8,128)(2,1)S(1)}, u32[]{:S(2)}, u32[]{:S(2)}) collective-permute-start(bf16[272,1024]{1,0:T(8,128)(2,1)S(1)} %get-tuple-element.135), channel_id=1, source_target_pairs={{0,8},{1,9},{2,10},{3,11},{4,12},{5,13},{6,14},{7,15}} | collective-permute-start | bytes 1671176 | tf_op jit(solution)/shard_map/ppermute | solution.py:446
  153.1 12.8 %collective-permute-start.41 = (bf16[144,1024]{1,0:T(8,128)(2,1)S(1)}, bf16[144,1024]{1,0:T(8,128)(2,1)S(1)}, u32[]{:S(2)}, u32[]{:S(2)}) collective-permute-start(bf16[144,1024]{1,0:T(8,128)(2,1)S(1)} %get-tuple-element.131), channel_id=1, source_target_pairs={{0,4},{1,5},{2,6},{3,7},{4,0},{5,1},{6,2},{7,3}} | collective-permute-start | bytes 884744 | tf_op jit(solution)/shard_map/ppermute | solution.py:446
  155.4 11.7 %collective-permute-start.46 = (bf16[144,1024]{1,0:T(8,128)(2,1)S(1)}, bf16[144,1024]{1,0:T(8,128)(2,1)S(1)}, u32[]{:S(2)}, u32[]{:S(2)}) collective-permute-start(bf16[144,1024]{1,0:T(8,128)(2,1)S(1)} %get-tuple-element.132), channel_id=1, source_target_pairs={{0,11},{1,10},{2,9},{3,8},{4,15},{5,14},{6,13},{7,12},{24,27},{25,... | collective-permute-start | bytes 884744 | tf_op jit(solution)/shard_map/ppermute | solution.py:446
  156.7 13.7 %collective-permute-start.47 = (bf16[144,1024]{1,0:T(8,128)(2,1)S(1)}, bf16[144,1024]{1,0:T(8,128)(2,1)S(1)}, u32[]{:S(2)}, u32[]{:S(2)}) collective-permute-start(bf16[144,1024]{1,0:T(8,128)(2,1)S(1)} %get-tuple-element.133), channel_id=1, source_target_pairs={{0,10},{1,11},{2,8},{3,9},{4,14},{5,15},{6,12},{7,13},{24,26},{25,... | collective-permute-start | bytes 884744 | tf_op jit(solution)/shard_map/ppermute | solution.py:446
  158.0 13.7 %collective-permute-start.48 = (bf16[144,1024]{1,0:T(8,128)(2,1)S(1)}, bf16[144,1024]{1,0:T(8,128)(2,1)S(1)}, u32[]{:S(2)}, u32[]{:S(2)}) collective-permute-start(bf16[144,1024]{1,0:T(8,128)(2,1)S(1)} %get-tuple-element.134), channel_id=1, source_target_pairs={{0,9},{1,8},{2,11},{3,10},{4,13},{5,12},{6,15},{7,14},{24,25},{25,... | collective-permute-start | bytes 884744 | tf_op jit(solution)/shard_map/ppermute | solution.py:446
  165.9 12.3 %collective-permute-start.44 = (bf16[144,1024]{1,0:T(8,128)(2,1)S(1)}, bf16[144,1024]{1,0:T(8,128)(2,1)S(1)}, u32[]{:S(2)}, u32[]{:S(2)}) collective-permute-start(bf16[144,1024]{1,0:T(8,128)(2,1)S(1)} %collective-permute-done.41), channel_id=1, source_target_pairs={{0,10},{1,11},{2,8},{3,9},{4,14},{5,15},{6,12},{7,13}} | collective-permute-start | bytes 884744 | tf_op jit(solution)/shard_map/ppermute | solution.py:446
  167.2 11.0 %collective-permute-start.45 = (bf16[144,1024]{1,0:T(8,128)(2,1)S(1)}, bf16[144,1024]{1,0:T(8,128)(2,1)S(1)}, u32[]{:S(2)}, u32[]{:S(2)}) collective-permute-start(bf16[144,1024]{1,0:T(8,128)(2,1)S(1)} %collective-permute-done.41), channel_id=1, source_target_pairs={{0,9},{1,8},{2,11},{3,10},{4,13},{5,12},{6,15},{7,14}} | collective-permute-start | bytes 884744 | tf_op jit(solution)/shard_map/ppermute | solution.py:446
  182.7 21.6 %collective-permute-start.58 = (bf16[272,1024]{1,0:T(8,128)(2,1)S(1)}, bf16[272,1024]{1,0:T(8,128)(2,1)S(1)}, u32[]{:S(2)}, u32[]{:S(2)}) collective-permute-start(bf16[272,1024]{1,0:T(8,128)(2,1)S(1)} %get-tuple-element.153), channel_id=1, source_target_pairs={{8,0},{9,1},{10,2},{11,3},{12,4},{13,5},{14,6},{15,7}} | collective-permute-start | bytes 1671176 | tf_op jit(solution)/shard_map/ppermute | solution.py:446
  184.7 11.2 %collective-permute-start.55 = (bf16[144,1024]{1,0:T(8,128)(2,1)S(1)}, bf16[144,1024]{1,0:T(8,128)(2,1)S(1)}, u32[]{:S(2)}, u32[]{:S(2)}) collective-permute-start(bf16[144,1024]{1,0:T(8,128)(2,1)S(1)} %get-tuple-element.150), channel_id=1, source_target_pairs={{8,3},{9,2},{10,1},{11,0},{12,7},{13,6},{14,5},{15,4},{24,27},{25,... | collective-permute-start | bytes 884744 | tf_op jit(solution)/shard_map/ppermute | solution.py:446
  186.0 14.0 %collective-permute-start.56 = (bf16[144,1024]{1,0:T(8,128)(2,1)S(1)}, bf16[144,1024]{1,0:T(8,128)(2,1)S(1)}, u32[]{:S(2)}, u32[]{:S(2)}) collective-permute-start(bf16[144,1024]{1,0:T(8,128)(2,1)S(1)} %get-tuple-element.151), channel_id=1, source_target_pairs={{8,2},{9,3},{10,0},{11,1},{12,6},{13,7},{14,4},{15,5},{24,26},{25,... | collective-permute-start | bytes 884744 | tf_op jit(solution)/shard_map/ppermute | solution.py:446
  187.3 14.0 %collective-permute-start.57 = (bf16[144,1024]{1,0:T(8,128)(2,1)S(1)}, bf16[144,1024]{1,0:T(8,128)(2,1)S(1)}, u32[]{:S(2)}, u32[]{:S(2)}) collective-permute-start(bf16[144,1024]{1,0:T(8,128)(2,1)S(1)} %get-tuple-element.152), channel_id=1, source_target_pairs={{8,1},{9,0},{10,3},{11,2},{12,5},{13,4},{14,7},{15,6},{24,25},{25,... | collective-permute-start | bytes 884744 | tf_op jit(solution)/shard_map/ppermute | solution.py:446
  188.6 18.6 %collective-permute-start.53 = (bf16[144,1024]{1,0:T(8,128)(2,1)S(1)}, bf16[144,1024]{1,0:T(8,128)(2,1)S(1)}, u32[]{:S(2)}, u32[]{:S(2)}) collective-permute-start(bf16[144,1024]{1,0:T(8,128)(2,1)S(1)} %collective-permute-done.50.refs_4_), channel_id=1, source_target_pairs={{8,2},{9,3},{10,0},{11,1},{12,6},{13,7},{14,4},{15,5}} | collective-permute-start | bytes 884744 | tf_op jit(solution)/shard_map/ppermute | solution.py:446
  195.9 11.3 %collective-permute-start.54 = (bf16[144,1024]{1,0:T(8,128)(2,1)S(1)}, bf16[144,1024]{1,0:T(8,128)(2,1)S(1)}, u32[]{:S(2)}, u32[]{:S(2)}) collective-permute-start(bf16[144,1024]{1,0:T(8,128)(2,1)S(1)} %collective-permute-done.50.refs_4_), channel_id=1, source_target_pairs={{8,1},{9,0},{10,3},{11,2},{12,5},{13,4},{14,7},{15,6}} | collective-permute-start | bytes 884744 | tf_op jit(solution)/shard_map/ppermute | solution.py:446
  (40 other events, 236.3 us)
